TPU v7x, 512 devices: a whole 4x8x8 slice. The times are simulated.
512 devices in a mesh: ctx: 16 (over x, y_lo), table: 32 (over y_hi, z, core).
Axes of the slice: x: 4, y: 8 (y_hi: 2, y_lo: 4; y = y_hi * 4 + y_lo), z: 8, core: 2. Of those that a mesh axis runs over, the one named last changes fastest.
Arguments:
- item_inputs: bfloat16 [32, 2048, 512], P('table', 'ctx'), may hold values from -6 to 6
- attn_saved: bfloat16 [32, 2048, 512], P('table', 'ctx'), may hold values from -0.125 to 0.125
- out_grad: bfloat16 [32, 2048, 512], P('table', 'ctx'), may hold values from -6 to 6
- seq_lengths: int32 [32], P('table'), may hold values from 512 to 2048, as said below
- token_slot: int32 [32, 2048], P('table', 'ctx'), may hold values from 0 to 127, as said below
- slot_rows: int32 [32, 2048], P('table', 'ctx'), may hold values from 0 to 32767, as said below
- in_proj: bfloat16 [512, 2048], replicated, may hold values from -0.25 to 0.25
- out_proj: bfloat16 [512, 512], replicated, may hold values from -0.25 to 0.25
- norm_gain: float32 [512], replicated, may hold values from 0.5 to 1.5
Outputs:
- proj_grad: bfloat16 [32, 2048, 2048], P('table', 'ctx')
- table_grad: float32 [32768, 512], P(('ctx', 'table'))
Inputs may be any that keep to these rules, and one draw needn't show every extreme that they name: `seq_lengths`: one history has length 2048. `token_slot`: position p names a slot of block p // 128. Slots o * 4 to o * 4 + 3 belong to table index o. In each block the named slots of one owner are a prefix of its 4 slots and every slot of that prefix is named. For every block index along the history there is an owner whose 4 slots are all named in that block of every history. `slot_rows`: entry c * 128 + s is the item row of slot s of block c. Its owner (row // 64) modulo the number of table indices is s // 4, and the 4 rows of one owner in one block differ.
All inputs are finite; a program needn't handle non-finite values.
Results may differ from a plain program's by a relative error of at most 0.0065.
Values may be sent and summed in bfloat16 or wider, within the bound.
No kernel may reach another device: no remote copies, remote signals or barrier semaphores. Data moves between devices by JAX's collectives and lax.ppermute only.
A program may use at most 64 MiB of HBM per device.

v0:
```python
import jax
import jax.numpy as jnp
from jax import lax
from jax.sharding import PartitionSpec as P

HEADS = 4
ROWS_DEV = 64


def silu_slope(value):
    squash = jax.nn.sigmoid(value)
    return squash * (1.0 + value * (1.0 - squash))


def tile_terms(queries, out_attn, key_rows, values, query_pos, key_pos, length, length_f, scale):
    scores = (
        jnp.einsum("ihd,jhd->hij", queries, key_rows, preferred_element_type=jnp.float32) * scale
    )
    live = (
        (key_pos[None, :] <= query_pos[:, None])
        & (query_pos[:, None] < length)
        & (key_pos[None, :] < length)
    )
    weight = jnp.where(live, 1.0 / length_f, 0.0)
    squash = jax.nn.sigmoid(scores)
    attend = (scores * squash * weight).astype(jnp.bfloat16)
    attn_grad = jnp.einsum("ihd,jhd->hij", out_attn, values, preferred_element_type=jnp.float32)
    score_grad = (attn_grad * squash * (1.0 + scores * (1.0 - squash)) * weight).astype(
        jnp.bfloat16
    )
    return (attend, score_grad)


def keep_same(accs):
    return accs


def per_device(
    item_inputs,
    attn_saved,
    out_grad,
    seq_lengths,
    token_slot,
    slot_rows,
    in_proj,
    out_proj,
    norm_gain,
):
    inputs_own = item_inputs[0]
    saved_own = attn_saved[0]
    grad_own = out_grad[0]
    length = seq_lengths[0]
    length_f = length.astype(jnp.float32)
    tok_rows, width = inputs_own.shape
    head_dim = width // HEADS
    scale = head_dim ** (-0.5)
    ctx_count = lax.axis_size("ctx")
    table_count = lax.axis_size("table")
    ctx_index = lax.axis_index("ctx")
    own_first = ctx_index * tok_rows
    own_pos = own_first + jnp.arange(tok_rows, dtype=jnp.int32)
    pre_act = jnp.dot(inputs_own, in_proj, preferred_element_type=jnp.float32)
    hidden = jax.nn.silu(pre_act).astype(jnp.bfloat16)
    slope = silu_slope(pre_act)
    gating = hidden[:, :width]
    values_own = hidden[:, width : 2 * width].reshape(tok_rows, HEADS, head_dim)
    queries_own = hidden[:, 2 * width : 3 * width].reshape(tok_rows, HEADS, head_dim)
    keys_own = hidden[:, 3 * width :].reshape(tok_rows, HEADS, head_dim)
    back = jnp.einsum("te,de->td", grad_own, out_proj, preferred_element_type=jnp.float32)
    saved = saved_own.astype(jnp.float32)
    row_mean = jnp.mean(saved, axis=1, keepdims=True)
    centred = saved - row_mean
    inv_std = lax.rsqrt(jnp.mean(centred * centred, axis=1, keepdims=True) + 1e-05)
    normed = centred * inv_std
    gating_grad = back * (normed * norm_gain)
    carried = back * gating.astype(jnp.float32) * norm_gain
    out_attn = inv_std * (
        carried
        - jnp.mean(carried, axis=1, keepdims=True)
        - normed * jnp.mean(carried * normed, axis=1, keepdims=True)
    )
    out_attn = out_attn.astype(jnp.bfloat16).reshape(tok_rows, HEADS, head_dim)
    slot_count = slot_rows.shape[1]
    slot_cap = slot_count // table_count
    row_ids = lax.all_to_all(
        slot_rows[0].reshape(table_count, slot_cap),
        "table",
        split_axis=0,
        concat_axis=0,
        tiled=True,
    )
    picks = (token_slot[0][:, None] == jnp.arange(slot_count, dtype=jnp.int32)[None, :]).astype(
        jnp.float32
    )
    zero = jnp.zeros((tok_rows, HEADS, head_dim), jnp.float32)
    running = zero
    anchor = jnp.int32(0)
    key_piece = lax.all_gather(keys_own, "ctx", axis=0, tiled=True)
    value_piece = lax.all_gather(values_own, "ctx", axis=0, tiled=True)
    extent = key_piece.shape[0]
    for offset in range(0, extent, 512):
        span = min(512, extent - offset)
        first_key = anchor + offset
        key_blk = key_piece[offset : offset + span]
        value_blk = value_piece[offset : offset + span]
        key_pos = first_key + jnp.arange(span, dtype=jnp.int32)
        needed = (
            (first_key <= own_first + tok_rows - 1) & (first_key < length) & (own_first < length)
        )

        def add_keys(accum, key_blk=key_blk, value_blk=value_blk, key_pos=key_pos):
            attend, score_grad = tile_terms(
                queries_own, out_attn, key_blk, value_blk, own_pos, key_pos, length, length_f, scale
            )
            return (
                accum
                + jnp.einsum(
                    "hij,jhd->ihd", score_grad, key_blk, preferred_element_type=jnp.float32
                )
                * scale
            )

        running = lax.cond(needed, add_keys, keep_same, running)
    query_acc = running
    running = (zero, zero)
    anchor = jnp.int32(0)
    query_piece = lax.all_gather(queries_own, "ctx", axis=0, tiled=True)
    out_piece = lax.all_gather(out_attn, "ctx", axis=0, tiled=True)
    extent = query_piece.shape[0]
    for offset in range(0, extent, 512):
        span = min(512, extent - offset)
        first_query = anchor + offset
        query_blk = query_piece[offset : offset + span]
        out_blk = out_piece[offset : offset + span]
        query_pos = first_query + jnp.arange(span, dtype=jnp.int32)
        needed = (
            (own_first <= first_query + span - 1) & (own_first < length) & (first_query < length)
        )

        def add_queries(accums, query_blk=query_blk, out_blk=out_blk, query_pos=query_pos):
            key_part, value_part = accums
            attend, score_grad = tile_terms(
                query_blk,
                out_blk,
                keys_own,
                values_own,
                query_pos,
                own_pos,
                length,
                length_f,
                scale,
            )
            key_part = (
                key_part
                + jnp.einsum(
                    "hij,ihd->jhd", score_grad, query_blk, preferred_element_type=jnp.float32
                )
                * scale
            )
            value_part = value_part + jnp.einsum(
                "hij,ihd->jhd", attend, out_blk, preferred_element_type=jnp.float32
            )
            return (key_part, value_part)

        running = lax.cond(needed, add_queries, keep_same, running)
    key_acc, value_acc = running
    joined = jnp.concatenate(
        [
            gating_grad,
            value_acc.reshape(tok_rows, width),
            query_acc.reshape(tok_rows, width),
            key_acc.reshape(tok_rows, width),
        ],
        axis=1,
    )
    proj_grad = (joined * slope).astype(jnp.bfloat16)
    input_grad = grad_own.astype(jnp.float32) + jnp.einsum(
        "tf,df->td", proj_grad, in_proj, preferred_element_type=jnp.float32
    )
    summed = jnp.einsum(
        "ts,td->sd",
        picks,
        input_grad,
        precision=lax.Precision.HIGHEST,
        preferred_element_type=jnp.float32,
    )
    received = lax.all_to_all(
        summed.reshape(table_count, slot_cap, width),
        "table",
        split_axis=0,
        concat_axis=0,
        tiled=True,
    )
    local_rows = row_ids // (ROWS_DEV * table_count) * ROWS_DEV + row_ids % ROWS_DEV
    flat_rows = received.reshape(table_count * slot_cap, width)
    flat_index = local_rows.reshape(table_count * slot_cap)
    dense = jax.ops.segment_sum(flat_rows, flat_index, num_segments=ctx_count * ROWS_DEV)
    table_grad = lax.psum_scatter(dense, "ctx", scatter_dimension=0, tiled=True)
    return (proj_grad[None], table_grad)


def solution(mesh):
    return jax.shard_map(
        per_device,
        mesh=mesh,
        in_specs=(
            P("table", "ctx", None),
            P("table", "ctx", None),
            P("table", "ctx", None),
            P("table"),
            P("table", "ctx"),
            P("table", "ctx"),
            P(),
            P(),
            P(),
        ),
        out_specs=(P("table", "ctx", None), P(("ctx", "table"), None)),
        check_vma=False,
    )
```

profile of v0, /device:TPU:64, one launch (start us, length us, event | category | flops | bytes accessed | tf_op | source)
XLA Modules:
  0.0 569.9 jit_solution(15659992695295212546)
XLA Ops:
  7.2 1.5 copy-done
  8.8 2.4 multiply_convert_fusion.8
  13.8 1.4 fusion.207
  16.2 1.6 copy.205
  19.7 15.4 %all-to-all-start = ((s32[32,1,4]{2,1,0:T(1,128)}), s32[32,1,4]{2,1,0:T(1,128)S(1)}, u32[]{:S(2)}, u32[]{:S(2)}) async-start(s32[32,1,4]{2,1,0:T(1,128)} %bitcast.23), calls=%async_computation | async-start | bytes 32768 | tf_op jit(solution)/shard_map/all_to_all | solution.py:85
  35.8 0.9 reshape.650
  36.7 0.9 reshape.651
  38.4 68.5 %all-gather.9.cloned.1.call-done = bf16[2048,4,128]{2,1,0:T(4,128)(2,1)} async-done(((bf16[128,4,128]{2,1,0:T(4,128)(2,1)}), bf16[2048,4,128]{2,1,0:T(4,128)(2,1)}) %all-gather.9.cloned.1.call-update) | async-done | bytes 2097168 | tf_op jit(solution)/shard_map/all_gather | solution.py:99
  106.9 91.5 %all-gather.11.cloned.1.call-done = bf16[2048,4,128]{2,0,1:T(8,128)(2,1)} async-done(((bf16[128,4,128]{2,0,1:T(8,128)(2,1)}), bf16[2048,4,128]{2,0,1:T(8,128)(2,1)}) %all-gather.11.cloned.1.call-update) | async-done | bytes 2097168 | tf_op jit(solution)/shard_map/all_gather | solution.py:98
  198.3 9.3 %conditional.12 = (f32[128,4,128]{2,0,1:T(8,128)S(1)}) conditional(s32[]{:T(128)} %convert_element_type.98, () %tuple.87, (bf16[128,4,128]{2,1,0:T(4,128)(2,1)}, bf16[2048,4,128]{2,1,0:T(4,128)(2,1)}, bf16[128,4,128]{2,1,0:T(4,128)(2,1)S(1)}, bf16[2048,4,128]{2,0,1:T(8,128)(2,1)}, s32[512]{0:T(512)S(1)}, /*index=5*/s32[128]{0:T(128)S(1)}, ...), branch_computations={%region_12.13_spmd, %region_13.14_spmd} | conditional | flops 204538496 | bytes 9443644 | solution.py:123
  199.8 2.4 convolution_multiply_fusion.6
  202.2 3.3 copy.101
  205.5 2.2 fusion.72
  207.7 82.4 %all-gather.5.cloned.1.call-done = bf16[2048,4,128]{2,1,0:T(4,128)(2,1)} async-done(((bf16[128,4,128]{2,1,0:T(4,128)(2,1)}), bf16[2048,4,128]{2,1,0:T(4,128)(2,1)}) %all-gather.5.cloned.1.call-update) | async-done | bytes 2097168 | tf_op jit(solution)/shard_map/all_gather | solution.py:128
  290.1 2.6 fusion.212
  292.7 88.7 %all-gather.7.cloned.1.call-done = bf16[2048,4,128]{2,0,1:T(8,128)(2,1)} async-done(((bf16[128,4,128]{2,0,1:T(8,128)(2,1)}), bf16[2048,4,128]{2,0,1:T(8,128)(2,1)}) %all-gather.7.cloned.1.call-update) | async-done | bytes 2097168 | tf_op jit(solution)/shard_map/all_gather | solution.py:127
  381.3 2.2 fusion.211
  383.6 9.0 %conditional.8 = (f32[128,4,128]{2,0,1:T(8,128)S(1)}, f32[128,4,128]{2,0,1:T(8,128)S(1)}) conditional(s32[]{:T(128)} %convert_element_type.90, () %tuple.82, (bf16[512,4,128]{2,1,0:T(4,128)(2,1)}, bf16[128,4,128]{2,1,0:T(4,128)(2,1)}, bf16[512,4,128]{2,0,1:T(8,128)(2,1)}, bf16[128,4,128]{2,1,0:T(4,128)(2,1)S(1)}, s32[128]{0:T(128)S(1)}, ...), branch_computations={%region_4.5_spmd, %region_5.6_spmd} | conditional | flops 273220224 | bytes 7879008 | solution.py:165
  384.9 0.9 and_select_fusion
  385.8 2.4 convolution_multiply_fusion
  388.2 2.4 fusion.5
  390.6 2.0 convolution_bitcast_fusion
  392.6 12.2 %conditional.9 = ((f32[128,4,128]{2,0,1:T(8,128)S(1)}, f32[128,4,128]{2,0,1:T(8,128)S(1)})) conditional(s32[]{:T(128)} %convert_element_type.89, (f32[128,4,128]{2,0,1:T(8,128)S(1)}, f32[128,4,128]{2,0,1:T(8,128)S(1)}) %conditional.8, (bf16[512,4,128]{2,1,0:T(4,128)(2,1)}, bf16[128,4,128]{2,1,0:T(4,128)(2,1)}, bf16[512,4,128]{2,0,1:T(8,128)(2,1)}, ...), branch_computations={%region_6.7_spmd, %region_7.8_spmd} | conditional | flops 273351296 | bytes 7346480 | solution.py:165
  392.6 1.8 broadcast_compare_fusion.3
  394.4 1.9 broadcast_compare_fusion.2
  396.3 1.6 and_select_fusion.1
  397.9 2.3 convolution_multiply_fusion.2
  400.3 2.5 fusion.25
  402.8 2.0 fusion.26
  404.7 16.1 %conditional.10 = (f32[128,4,128]{2,0,1:T(8,128)S(1)}, f32[128,4,128]{2,0,1:T(8,128)S(1)}, (f32[128,4,128]{0,2,1:T(8,128)}, f32[128,4,128]{0,2,1:T(8,128)})) conditional(s32[]{:T(128)} %convert_element_type.88, (f32[128,4,128]{2,0,1:T(8,128)S(1)}, f32[128,4,128]{2,0,1:T(8,128)S(1)}) %get-tuple-element.633, ...), branch_computations={%region_8.9_spmd.clone, %region_9.10_spmd.clone} | conditional | flops 273351296 | bytes 9443648 | solution.py:165
  404.9 1.9 broadcast_compare_fusion.15
  406.8 1.8 broadcast_compare_fusion.14
  408.7 1.6 and_select_fusion.7
  410.3 2.3 convolution_multiply_fusion.14
  412.6 2.0 slice.88
  414.6 2.5 fusion.168
  418.0 2.0 fusion.169
  420.8 2.0 conditional.15
  420.8 0.9 copy.137
  421.7 1.1 copy.135
  423.5 2.2 conditional.11
  423.5 1.1 copy.131
  424.6 1.1 copy.133
  426.4 1.8 fusion.187
  430.2 29.8 %all-to-all-start.1 = ((f32[32,4,512]{2,1,0:T(4,128)}), f32[32,4,512]{2,1,0:T(4,128)S(1)}, u32[]{:S(2)}, u32[]{:S(2)}) async-start(f32[32,4,512]{2,1,0:T(4,128)} %reshape.655), calls=%async_computation.1 | async-start | bytes 524288 | tf_op jit(solution)/shard_map/all_to_all | solution.py:187
  460.8 12.4 %all-to-all-done.1 = f32[32,4,512]{2,1,0:T(4,128)S(1)} async-done(((f32[32,4,512]{2,1,0:T(4,128)}), f32[32,4,512]{2,1,0:T(4,128)S(1)}, u32[]{:S(2)}, u32[]{:S(2)}) %all-to-all-start.1) | async-done | bytes 262176 | tf_op jit(solution)/shard_map/all_to_all | solution.py:187
  473.3 2.8 scatter_custom_fusion
  476.1 87.3 %reduce-scatter.2.cloned.1.call-done = f32[64,512]{1,0:T(8,128)} async-done(((f32[1024,512]{1,0:T(8,128)}), f32[64,512]{1,0:T(8,128)}) %reduce-scatter.2.cloned.1.call-update) | async-done | bytes 131088 | tf_op jit(solution)/shard_map/reduce_scatter | solution.py:198
  (75 shorter events, 14.8 us)
Async XLA Ops:
  7.2 1.6 copy-start
  7.2 6.2 %copy-start.1 = (bf16[1,128,512]{2,1,0:T(8,128)(2,1)S(1)}, bf16[1,128,512]{2,1,0:T(8,128)(2,1)}, u32[]{:S(2)}) copy-start(bf16[1,128,512]{2,1,0:T(8,128)(2,1)} %param.26) | copy-start | bytes 393220
  7.2 99.7 %all-gather.9.cloned.1.call-start = ((), (), s32[]{:S(2)}) async-start(), calls=%async_computation.5 | async-start | bytes 2228224 | tf_op jit(solution)/shard_map/all_gather | solution.py:99
  11.1 2.6 copy-start.6
  11.1 2.6 copy-start.18
  11.9 6.4 %copy-start.20 = (s32[1,128]{1,0:T(1,128)S(1)}, s32[1,128]{1,0:T(1,128)}, u32[]{:S(2)}) copy-start(s32[1,128]{1,0:T(1,128)} %param.30) | copy-start | bytes 1540
  12.6 185.7 %all-gather.11.cloned.1.call-start = ((), (), s32[]{:S(2)}) async-start(), calls=%async_computation.6 | async-start | bytes 2228224 | tf_op jit(solution)/shard_map/all_gather | solution.py:98
  13.4 276.7 %all-gather.5.cloned.1.call-start = ((), (), s32[]{:S(2)}) async-start(), calls=%async_computation.3 | async-start | bytes 2228224 | tf_op jit(solution)/shard_map/all_gather | solution.py:128
  16.1 365.2 %all-gather.7.cloned.1.call-start = ((), (), s32[]{:S(2)}) async-start(), calls=%async_computation.4 | async-start | bytes 2228224 | tf_op jit(solution)/shard_map/all_gather | solution.py:127
  19.7 410.5 %all-to-all-start = ((s32[32,1,4]{2,1,0:T(1,128)}), s32[32,1,4]{2,1,0:T(1,128)S(1)}, u32[]{:S(2)}, u32[]{:S(2)}) async-start(s32[32,1,4]{2,1,0:T(1,128)} %bitcast.23), calls=%async_computation | async-start | bytes 32768 | tf_op jit(solution)/shard_map/all_to_all | solution.py:85
  37.7 345.8 %copy-start.16 = (s32[128]{0:T(128)}, s32[128]{0:T(128)S(1)}, u32[]{:S(2)}) copy-start(s32[128]{0:T(128)S(1)} %iota_add_fusion.3) | copy-start | bytes 1540
  37.8 169.9 %copy-start.15 = (s32[512]{0:T(512)}, s32[512]{0:T(512)S(1)}, u32[]{:S(2)}) copy-start(s32[512]{0:T(512)S(1)} %iota_add_fusion.2) | copy-start | bytes 6148
  37.8 169.9 %copy-start.14 = (s32[512]{0:T(512)}, s32[512]{0:T(512)S(1)}, u32[]{:S(2)}) copy-start(s32[512]{0:T(512)S(1)} %iota_add_fusion.1) | copy-start | bytes 6148
  202.2 3.3 copy-start.8
  383.6 0.7 copy-start.17
  385.8 2.4 copy-start.13
  422.8 0.7 copy-start.3
  425.6 0.7 copy-start.4
  428.1 2.1 copy-start.2
  428.1 0.9 copy-start.19
  430.2 43.0 %all-to-all-start.1 = ((f32[32,4,512]{2,1,0:T(4,128)}), f32[32,4,512]{2,1,0:T(4,128)S(1)}, u32[]{:S(2)}, u32[]{:S(2)}) async-start(f32[32,4,512]{2,1,0:T(4,128)} %reshape.655), calls=%async_computation.1 | async-start | bytes 524288 | tf_op jit(solution)/shard_map/all_to_all | solution.py:187
  460.0 103.4 %reduce-scatter.2.cloned.1.call-start = ((), (), s32[]{:S(2)}) async-start(), calls=%async_computation.7 | async-start | bytes 2228224 | tf_op jit(solution)/shard_map/reduce_scatter | solution.py:198
Sparse Core Ops, SparseCore 0:
  12.7 94.0 all-gather.8
  108.9 89.3 all-gather.10
  201.0 89.0 all-gather.4
  292.0 89.2 all-gather.6
  476.2 87.1 reduce-scatter.1
where the time goes:
time: 571 us; the launch traced here: 570 us
  waiting for transfers between devices  431 us (75%)
  starting transfers between devices  45.4 us (8%)
  matrix products  29.9 us (5%)
  local copies, waits for them, and re-layouts  27.4 us (5%)
  other arithmetic  21.1 us (4%)
  between operations  14.8 us (3%)
    all_gather x1, waiting for transfers between devices, per_device(): key_piece = lax.all_gather(keys_own, 'ctx', axis=0, tiled=True)  91.5 us
    all_gather x1, waiting for transfers between devices, per_device(): query_piece = lax.all_gather(queries_own, 'ctx', axis=0, tiled=True)  88.7 us
    reduce_scatter x1, waiting for transfers between devices, per_device(): table_grad = lax.psum_scatter(dense, 'ctx', scatter_dimension=0, tiled=True)  87.3 us
    all_gather x1, waiting for transfers between devices, per_device(): out_piece = lax.all_gather(out_attn, 'ctx', axis=0, tiled=True)  82.4 us
    all_gather x1, waiting for transfers between devices, per_device(): value_piece = lax.all_gather(values_own, 'ctx', axis=0, tiled=True)  68.5 us
    all_to_all x1, starting transfers between devices, per_device(): lax.all_to_all(summed.reshape(table_count, slot_cap, width), 'table', spl...  29.8 us
    all_to_all x1, starting transfers between devices, per_device(): lax.all_to_all(slot_rows[0].reshape(table_count, slot_cap), 'table', spli...  15.4 us
    all_to_all x1, waiting for transfers between devices, per_device(): lax.all_to_all(summed.reshape(table_count, slot_cap, width), 'table', spl...  12.4 us
  transfers between devices with their start and end apart: 7, of which 6 were waited for; matrix products, arithmetic and copies ran while one was open for 12% of the time, Pallas kernels for 0%

commit v1 on v0

v1 whole, which is shorter than its diff:
```python
import functools

import jax
import jax.numpy as jnp
from jax import lax
from jax.experimental import pallas as pl
from jax.experimental.pallas import tpu as pltpu
from jax.sharding import PartitionSpec as P

HEADS = 4
HEAD_DIM = 128
WIDTH = 512
TOKENS = 128
ROWS_DEV = 64
TABLES = 32
CAP = 4
SUM_ROWS = CAP * WIDTH // 128
SEND_ROWS = SUM_ROWS + 8
X_COUNT = 4
Y_COUNT = 4
VMEM_LIMIT = 48 * 1024 * 1024
ALL_VMEM = 63 * 1024 * 1024
BF16 = jnp.bfloat16
F32 = jnp.float32

X_GROUPS = [[x * Y_COUNT + y for x in range(X_COUNT)] for y in range(Y_COUNT)]
Y_GROUPS = [[x * Y_COUNT + y for y in range(Y_COUNT)] for x in range(X_COUNT)]
SWAP_QUERY = [(c, c ^ 2) for c in range(X_COUNT * Y_COUNT)]
SWAP_KEY = [(c, c ^ 1) for c in range(X_COUNT * Y_COUNT)]

MATMUL = (((1,), (0,)), ((), ()))
MATMUL_NT = (((1,), (1,)), ((), ()))
MATMUL_TN = (((0,), (0,)), ((), ()))


def dot(lhs, rhs, dims):
    return lax.dot_general(lhs, rhs, dims, preferred_element_type=F32)


def in_vmem(count):
    return [pl.BlockSpec(memory_space=pltpu.VMEM)] * count


def in_smem():
    return pl.BlockSpec(memory_space=pltpu.SMEM)


def in_hbm(count):
    return [pl.BlockSpec(memory_space=pltpu.HBM)] * count


def params(limit=VMEM_LIMIT):
    return pltpu.CompilerParams(vmem_limit_bytes=limit)


def project_kernel(
    length_ref,
    inputs_hbm,
    saved_hbm,
    grad_hbm,
    in_proj_hbm,
    out_proj_hbm,
    gain_hbm,
    parts_ref,
    slope_ref,
    gate_ref,
    base_ref,
    inputs_ref,
    saved_ref,
    grad_ref,
    in_proj_ref,
    out_proj_ref,
    gain_ref,
    sems,
):
    def copy_of(place, source, target):
        copy = pltpu.make_async_copy(source, target, sems.at[place])
        copy.start()
        return copy

    saved_copy = copy_of(0, saved_hbm, saved_ref)
    grad_copy = copy_of(1, grad_hbm, grad_ref)
    gain_copy = copy_of(2, gain_hbm, gain_ref)
    out_copy = copy_of(3, out_proj_hbm, out_proj_ref)
    inputs_copy = copy_of(4, inputs_hbm, inputs_ref)
    in_copies = [
        copy_of(
            5 + block,
            in_proj_hbm.at[:, block * WIDTH : (block + 1) * WIDTH],
            in_proj_ref.at[block],
        )
        for block in range(4)
    ]
    first = lax.axis_index("ctx") * TOKENS
    length = length_ref[0]
    saved_copy.wait()
    saved = saved_ref[...].astype(F32)
    row_mean = jnp.mean(saved, axis=1, keepdims=True)
    centred = saved - row_mean
    inv_std = lax.rsqrt(jnp.mean(centred * centred, axis=1, keepdims=True) + 1e-05)
    normed = centred * inv_std
    grad_copy.wait()
    gain_copy.wait()
    out_copy.wait()
    gain = gain_ref[...]
    grad = grad_ref[...]
    back = dot(grad, out_proj_ref[...], MATMUL_NT)

    inputs_copy.wait()
    in_copies[0].wait()
    inputs = inputs_ref[...]
    pre = dot(inputs, in_proj_ref[0], MATMUL)
    squash = jax.nn.sigmoid(pre)
    gating = (pre * squash).astype(BF16).astype(F32)
    gate = (back * (normed * gain) * (squash * (1.0 + pre * (1.0 - squash)))).astype(BF16)
    gate_ref[...] = gate
    base_ref[...] = grad.astype(F32) + dot(gate, in_proj_ref[0], MATMUL_NT)

    carried = back * gating * gain
    out_attn = inv_std * (
        carried
        - jnp.mean(carried, axis=1, keepdims=True)
        - normed * jnp.mean(carried * normed, axis=1, keepdims=True)
    )
    position = first + lax.broadcasted_iota(jnp.int32, (TOKENS, 1), 0)
    out_attn = jnp.where(position < length, out_attn, 0.0).astype(BF16)
    for head in range(HEADS):
        cols = slice(head * HEAD_DIM, (head + 1) * HEAD_DIM)
        parts_ref[head, :, HEAD_DIM : 2 * HEAD_DIM] = out_attn[:, cols]
    for block, place in ((1, 3), (2, 0), (3, 2)):
        in_copies[block].wait()
        pre = dot(inputs, in_proj_ref[block], MATMUL)
        squash = jax.nn.sigmoid(pre)
        slope_ref[:, (block - 1) * WIDTH : block * WIDTH] = squash * (1.0 + pre * (1.0 - squash))
        hidden = (pre * squash).astype(BF16)
        for head in range(HEADS):
            cols = slice(head * HEAD_DIM, (head + 1) * HEAD_DIM)
            parts_ref[head, :, place * HEAD_DIM : (place + 1) * HEAD_DIM] = hidden[:, cols]


def project(length, inputs, saved, grad, in_proj, out_proj, gain):
    return pl.pallas_call(
        project_kernel,
        out_shape=(
            jax.ShapeDtypeStruct((HEADS, TOKENS, 4 * HEAD_DIM), BF16),
            jax.ShapeDtypeStruct((TOKENS, 3 * WIDTH), F32),
            jax.ShapeDtypeStruct((TOKENS, WIDTH), BF16),
            jax.ShapeDtypeStruct((TOKENS, WIDTH), F32),
        ),
        in_specs=[in_smem()] + in_hbm(6),
        out_specs=tuple(in_vmem(4)),
        scratch_shapes=[
            pltpu.VMEM((TOKENS, WIDTH), BF16),
            pltpu.VMEM((TOKENS, WIDTH), BF16),
            pltpu.VMEM((TOKENS, WIDTH), BF16),
            pltpu.VMEM((4, WIDTH, WIDTH), BF16),
            pltpu.VMEM((WIDTH, WIDTH), BF16),
            pltpu.VMEM((1, WIDTH), F32),
            pltpu.SemaphoreType.DMA((9,)),
        ],
        compiler_params=params(ALL_VMEM),
        name="project",
    )(length, inputs, saved, grad, in_proj, out_proj, gain)


def tile_grads(queries, outs, keys, values, weight, live):
    scale = HEAD_DIM ** (-0.5)
    scores = dot(queries, keys, MATMUL_NT) * scale
    attn_grad = dot(outs, values, MATMUL_NT)
    squash = jax.nn.sigmoid(scores)
    weighted = squash * weight
    if live is not None:
        weighted = jnp.where(live, weighted, 0.0)
    attend = (scores * weighted).astype(BF16)
    score_grad = (attn_grad * weighted * (1.0 + scores * (1.0 - squash))).astype(BF16)
    return (
        dot(score_grad, keys, MATMUL) * scale,
        dot(score_grad, queries, MATMUL_TN) * scale,
        dot(attend, outs, MATMUL_TN),
    )


def attend_rows(length_ref, query_of, out_of, own_ref, key_far_ref, query_class, take_query, take_key):
    lane = lax.rem(lax.axis_index("ctx"), Y_COUNT)
    weight = jnp.full((1, 1), 1.0, F32) / jnp.full((1, 1), length_ref[0].astype(F32), F32)
    rows = lax.broadcasted_iota(jnp.int32, (TOKENS, 1), 0)
    columns = lax.broadcasted_iota(jnp.int32, (1, 2 * TOKENS), 1)
    row_pos = (lane ^ query_class) * TOKENS + rows
    column_pos = jnp.where(
        columns < TOKENS, lane * TOKENS + columns, (lane ^ 1) * TOKENS + columns - TOKENS
    )
    live = column_pos <= row_pos
    keys, values = [], []
    for x in range(X_COUNT):
        keys.append(
            jnp.concatenate(
                [own_ref[x, :, 2 * HEAD_DIM : 3 * HEAD_DIM], key_far_ref[x, :, :HEAD_DIM]], axis=0
            )
        )
        values.append(
            jnp.concatenate([own_ref[x, :, 3 * HEAD_DIM :], key_far_ref[x, :, HEAD_DIM:]], axis=0)
        )
    for query_x in range(X_COUNT):
        queries, outs = query_of(query_x), out_of(query_x)
        query_acc = None
        for key_x in range(query_x + 1):
            query_part, key_part, value_part = tile_grads(
                queries, outs, keys[key_x], values[key_x], weight, live if query_x == key_x else None
            )
            query_acc = query_part if query_acc is None else query_acc + query_part
            take_key(query_x, key_x, key_part, value_part)
        take_query(query_x, query_acc)


def attend_own_kernel(length_ref, own_ref, key_far_ref, query_ref, key_ref):
    def take_query(x, part):
        query_ref[x] = part

    def take_key(query_x, x, key_part, value_part):
        if query_x == x:
            key_ref[x, :, :HEAD_DIM] = key_part
            key_ref[x, :, HEAD_DIM:] = value_part
        else:
            key_ref[x, :, :HEAD_DIM] += key_part
            key_ref[x, :, HEAD_DIM:] += value_part

    attend_rows(
        length_ref,
        lambda x: own_ref[x, :, :HEAD_DIM],
        lambda x: own_ref[x, :, HEAD_DIM : 2 * HEAD_DIM],
        own_ref,
        key_far_ref,
        0,
        take_query,
        take_key,
    )


def attend_far_kernel(
    length_ref, own_ref, query_far_ref, key_far_ref, sums_ref, query_ref, key_own_ref, key_send_ref, acc_ref
):
    def take_query(x, part):
        query_ref[x] = part.astype(BF16)

    def take_key(query_x, x, key_part, value_part):
        source = sums_ref if query_x == x else acc_ref
        acc_ref[x, :, :HEAD_DIM] = source[x, :, :HEAD_DIM] + key_part
        acc_ref[x, :, HEAD_DIM:] = source[x, :, HEAD_DIM:] + value_part

    attend_rows(
        length_ref,
        lambda x: query_far_ref[x, :, :HEAD_DIM],
        lambda x: query_far_ref[x, :, HEAD_DIM:],
        own_ref,
        key_far_ref,
        2,
        take_query,
        take_key,
    )
    key_own_ref[...] = acc_ref[:, :TOKENS, :]
    key_send_ref[...] = acc_ref[:, TOKENS:, :].astype(BF16)


ATTEND_COST = pl.CostEstimate(
    flops=10 * 5 * 2 * 128 * 256 * 128, bytes_accessed=2 << 20, transcendentals=10 * 128 * 256
)


def attend_own(length, own, key_far):
    return pl.pallas_call(
        attend_own_kernel,
        out_shape=(
            jax.ShapeDtypeStruct((X_COUNT, TOKENS, HEAD_DIM), F32),
            jax.ShapeDtypeStruct((X_COUNT, 2 * TOKENS, 2 * HEAD_DIM), F32),
        ),
        in_specs=[in_smem()] + in_vmem(2),
        out_specs=tuple(in_vmem(2)),
        compiler_params=params(),
        cost_estimate=ATTEND_COST,
        name="attend_own",
    )(length, own, key_far)


def attend_far(length, own, query_far, key_far, sums):
    return pl.pallas_call(
        attend_far_kernel,
        out_shape=(
            jax.ShapeDtypeStruct((X_COUNT, TOKENS, HEAD_DIM), BF16),
            jax.ShapeDtypeStruct((X_COUNT, TOKENS, 2 * HEAD_DIM), F32),
            jax.ShapeDtypeStruct((X_COUNT, TOKENS, 2 * HEAD_DIM), BF16),
        ),
        in_specs=[in_smem()] + in_vmem(4),
        out_specs=tuple(in_vmem(3)),
        scratch_shapes=[pltpu.VMEM((X_COUNT, 2 * TOKENS, 2 * HEAD_DIM), F32)],
        compiler_params=params(),
        cost_estimate=ATTEND_COST,
        name="attend_far",
    )(length, own, query_far, key_far, sums)


def join_kernel(query_own_ref, query_got_ref, key_own_ref, key_got_ref, out_ref):
    out_ref[:, :, :HEAD_DIM] = (
        key_own_ref[:, :, HEAD_DIM:] + key_got_ref[:, :, HEAD_DIM:].astype(F32)
    ).astype(BF16)
    out_ref[:, :, HEAD_DIM : 2 * HEAD_DIM] = (
        query_own_ref[...] + query_got_ref[...].astype(F32)
    ).astype(BF16)
    out_ref[:, :, 2 * HEAD_DIM :] = (
        key_own_ref[:, :, :HEAD_DIM] + key_got_ref[:, :, :HEAD_DIM].astype(F32)
    ).astype(BF16)


def join_parts(query_own, query_got, key_own, key_got):
    return pl.pallas_call(
        join_kernel,
        out_shape=jax.ShapeDtypeStruct((X_COUNT, TOKENS, 3 * HEAD_DIM), BF16),
        in_specs=in_vmem(4),
        out_specs=in_vmem(1)[0],
        compiler_params=params(),
        name="join_parts",
    )(query_own, query_got, key_own, key_got)


def finish_kernel(
    grads_ref,
    slope_ref,
    gate_ref,
    base_ref,
    in_proj_ref,
    slot_ref,
    item_ref,
    proj_ref,
    rows_ref,
    wide_ref,
):
    proj_ref[:, :WIDTH] = gate_ref[...]
    for block in range(3):
        joined = jnp.concatenate(
            [
                grads_ref[head, :, block * HEAD_DIM : (block + 1) * HEAD_DIM].astype(F32)
                for head in range(HEADS)
            ],
            axis=1,
        )
        cols = slice((block + 1) * WIDTH, (block + 2) * WIDTH)
        proj_ref[:, cols] = (joined * slope_ref[:, block * WIDTH : (block + 1) * WIDTH]).astype(
            BF16
        )
    input_grad = base_ref[...] + dot(proj_ref[:, WIDTH:], in_proj_ref[:, WIDTH:], MATMUL_NT)
    high = input_grad.astype(BF16)
    low = (input_grad - high.astype(F32)).astype(BF16)
    order = lax.broadcasted_iota(jnp.int32, (TABLES * CAP, 1), 0)
    slot_of = (order % TABLES) * CAP + order // TABLES
    picks = (slot_ref[...] == slot_of).astype(F32).astype(BF16)
    summed = dot(picks, high, MATMUL) + dot(picks, low, MATMUL)
    for level in range(CAP):
        for chunk in range(WIDTH // 128):
            wide_ref[pl.ds(level * 4 + chunk, TABLES, stride=SEND_ROWS), :] = summed[
                level * TABLES : (level + 1) * TABLES, chunk * 128 : (chunk + 1) * 128
            ]
    items = item_ref[...]
    owner_of = (items // (ROWS_DEV * TABLES)).astype(F32)
    place_of = (items % ROWS_DEV).astype(F32)
    slot = lax.broadcasted_iota(jnp.int32, (TABLES, TABLES * CAP), 1)
    owner = lax.broadcasted_iota(jnp.int32, (TABLES, TABLES * CAP), 0)
    coded = jnp.zeros((TABLES, 128), F32)
    for level in range(CAP):
        match = slot == owner * CAP + level
        for value, lane in ((owner_of, level), (place_of, CAP + level)):
            column = jnp.sum(jnp.where(match, value, 0.0), axis=1, keepdims=True)
            coded = jnp.where(slot == lane, column, coded)
    wide_ref[pl.ds(SUM_ROWS, TABLES, stride=SEND_ROWS), :] = coded
    for row in range(SUM_ROWS + 1, SEND_ROWS):
        wide_ref[pl.ds(row, TABLES, stride=SEND_ROWS), :] = jnp.zeros((TABLES, 128), F32)
    rows_ref[...] = wide_ref[...].astype(BF16)


def finish(grads, slope, gate, base, in_proj, slots, items):
    return pl.pallas_call(
        finish_kernel,
        out_shape=(
            jax.ShapeDtypeStruct((TOKENS, 4 * WIDTH), BF16),
            jax.ShapeDtypeStruct((TABLES * SEND_ROWS, 128), BF16),
        ),
        in_specs=in_vmem(7),
        out_specs=tuple(in_vmem(2)),
        scratch_shapes=[pltpu.VMEM((TABLES * SEND_ROWS, 128), F32)],
        compiler_params=params(),
        name="finish",
    )(grads, slope, gate, base, in_proj, slots, items)


def scatter_kernel(rows_ref, out_ref, wide_ref):
    targets = Y_COUNT * ROWS_DEV
    count = X_COUNT * TABLES
    first = lax.div(lax.axis_index("ctx"), Y_COUNT) * targets
    wide_ref[...] = rows_ref[...].astype(F32)
    coded = wide_ref[pl.ds(SUM_ROWS, count, stride=SEND_ROWS), :].T
    ids = (coded[:CAP] * ROWS_DEV + coded[CAP : 2 * CAP]).astype(jnp.int32)
    target = first + lax.broadcasted_iota(jnp.int32, (targets, 1), 0)
    hots = [(ids[level : level + 1, :] == target).astype(F32).astype(BF16) for level in range(CAP)]
    for chunk in range(WIDTH // 128):
        total = None
        for level in range(CAP):
            rows = wide_ref[pl.ds(level * 4 + chunk, count, stride=SEND_ROWS), :].astype(BF16)
            part = dot(hots[level], rows, MATMUL)
            total = part if total is None else total + part
        out_ref[:, chunk * 128 : (chunk + 1) * 128] = total.astype(BF16)


def scatter_rows(rows):
    return pl.pallas_call(
        scatter_kernel,
        out_shape=jax.ShapeDtypeStruct((Y_COUNT * ROWS_DEV, WIDTH), BF16),
        in_specs=in_vmem(1),
        out_specs=in_vmem(1)[0],
        scratch_shapes=[pltpu.VMEM((X_COUNT * TABLES * SEND_ROWS, 128), F32)],
        compiler_params=params(),
        name="scatter_rows",
    )(rows)


def per_device(
    item_inputs,
    attn_saved,
    out_grad,
    seq_lengths,
    token_slot,
    slot_rows,
    in_proj,
    out_proj,
    norm_gain,
):
    parts, slope, gate, base = project(
        seq_lengths, item_inputs[0], attn_saved[0], out_grad[0], in_proj, out_proj, norm_gain[None]
    )
    own = lax.all_to_all(parts, "ctx", 0, 0, axis_index_groups=X_GROUPS)
    key_far = lax.ppermute(own[:, :, 2 * HEAD_DIM :], "ctx", SWAP_KEY)
    query_far = lax.ppermute(own[:, :, : 2 * HEAD_DIM], "ctx", SWAP_QUERY)
    query_own, sums = attend_own(seq_lengths, own, key_far)
    query_send, key_own, key_send = attend_far(seq_lengths, own, query_far, key_far, sums)
    key_got = lax.ppermute(key_send, "ctx", SWAP_KEY)
    query_got = lax.ppermute(query_send, "ctx", SWAP_QUERY)
    joined = join_parts(query_own, query_got, key_own, key_got)
    grads = lax.all_to_all(joined, "ctx", 0, 0, axis_index_groups=X_GROUPS)
    proj_grad, rows = finish(grads, slope, gate, base, in_proj, token_slot, slot_rows)
    rows = lax.all_to_all(rows.reshape(TABLES, SEND_ROWS, 128), "table", 0, 0)
    rows = lax.all_gather(rows, "ctx", axis_index_groups=X_GROUPS)
    dense = scatter_rows(rows.reshape(X_COUNT * TABLES * SEND_ROWS, 128))
    pieces = lax.all_to_all(
        dense.reshape(Y_COUNT, ROWS_DEV, WIDTH), "ctx", 0, 0, axis_index_groups=Y_GROUPS
    )
    table_grad = jnp.sum(pieces.astype(F32), axis=0)
    return (proj_grad[None], table_grad)


def solution(mesh):
    return jax.shard_map(
        per_device,
        mesh=mesh,
        in_specs=(
            P("table", "ctx", None),
            P("table", "ctx", None),
            P("table", "ctx", None),
            P("table"),
            P("table", "ctx"),
            P("table", "ctx"),
            P(),
            P(),
            P(),
        ),
        out_specs=(P("table", "ctx", None), P(("ctx", "table"), None)),
        check_vma=False,
    )
```

time: 571 us -> 118 us (0.21)
  the two profiles are of different devices: /device:TPU:64 before, /device:TPU:8 now
where the time goes in v1:
time: 118 us; the launch traced here: 117 us
  blocking collectives  77.3 us (66%)
  starting transfers between devices  14.6 us (12%)
  waiting for transfers between devices  12 us (10%)
  Pallas kernels  11.4 us (10%)
  between operations  1.4 us (1%)
    all_to_all x1, blocking collectives, per_device(): rows = lax.all_to_all(rows.reshape(TABLES, SEND_ROWS, 128), 'table', 0, 0)  30.1 us
    all_gather x1, blocking collectives, per_device(): rows = lax.all_gather(rows, 'ctx', axis_index_groups=X_GROUPS)  14.3 us
    all_to_all x1, blocking collectives, per_device(): own = lax.all_to_all(parts, 'ctx', 0, 0, axis_index_groups=X_GROUPS)  13.8 us
    all_to_all x1, blocking collectives, per_device(): grads = lax.all_to_all(joined, 'ctx', 0, 0, axis_index_groups=X_GROUPS)  9.77 us
    all_to_all x1, blocking collectives, per_device(): lax.all_to_all(dense.reshape(Y_COUNT, ROWS_DEV, WIDTH), 'ctx', 0, 0, axis...  9.31 us
    ppermute x1, starting transfers between devices, per_device(): key_far = lax.ppermute(own[:, :, 2 * HEAD_DIM:], 'ctx', SWAP_KEY)  5.48 us
    ppermute x1, waiting for transfers between devices, per_device(): query_got = lax.ppermute(query_send, 'ctx', SWAP_QUERY)  5.35 us
    ppermute x1, waiting for transfers between devices, per_device(): key_far = lax.ppermute(own[:, :, 2 * HEAD_DIM:], 'ctx', SWAP_KEY)  4.88 us
  transfers between devices with their start and end apart: 4, of which 3 were waited for; matrix products, arithmetic and copies ran while one was open for 0% of the time, Pallas kernels for 2%

profile of v1, /device:TPU:8, one launch (start us, length us, event | category | flops | bytes accessed | tf_op | source)
XLA Modules:
  0.0 117.4 jit_solution(16539620110880311669)
XLA Ops:
  1.3 4.0 %project.1 = (bf16[4,128,512]{2,1,0:T(8,128)(2,1)}, f32[128,1536]{1,0:T(8,128)}, bf16[128,512]{1,0:T(8,128)(2,1)}, f32[128,512]{1,0:T(8,128)}) custom-call(s32[1]{0:T(128)S(6)} %copy.11.length_ref, bf16[128,512]{1,0:T(8,128)(2,1)} %bitcast.11, bf16[128,512]{1,0:T(8,128)(2,1)} %bitcast.12, bf16[128,512]{1,0:T(8,128)(2,1)} %bitcast.13, ...), custom_call_target="tpu_custom_call" | custom-call | tf_op jit(solution)/shard_map/project/pallas_call | solution.py:142
  5.3 13.8 %all_to_all.20.own_ref = bf16[4,128,512]{2,1,0:T(8,128)(2,1)S(1)} all-to-all(bf16[4,128,512]{2,1,0:T(8,128)(2,1)} %get-tuple-element.13), channel_id=1, replica_groups={{0,128,256,384},{32,160,288,416},{64,192,320,448},{96,224,352,480},{1,1..., dimensions={0} | all-to-all | bytes 1048576 | tf_op jit(solution)/shard_map/all_to_all | solution.py:437
  19.1 5.5 %collective-permute-start = (bf16[4,128,256]{2,1,0:T(8,128)(2,1)S(1)}, bf16[4,128,256]{2,1,0:T(8,128)(2,1)S(1)}, u32[]{:S(2)}, u32[]{:S(2)}) collective-permute-start(bf16[4,128,256]{2,1,0:T(8,128)(2,1)S(1)} %get-tuple-element.25), channel_id=1, source_target_pairs={{0,32},{32,0},{64,96},{96,64},{128,160},{160,128},{192,224},{224,1... | collective-permute-start | bytes 786440 | tf_op jit(solution)/shard_map/ppermute | solution.py:438
  24.6 1.9 %collective-permute-start.1 = (bf16[4,128,256]{2,1,0:T(8,128)(2,1)S(1)}, bf16[4,128,256]{2,1,0:T(8,128)(2,1)S(1)}, u32[]{:S(2)}, u32[]{:S(2)}) collective-permute-start(bf16[4,128,256]{2,1,0:T(8,128)(2,1)S(1)} %get-tuple-element.24), channel_id=1, source_target_pairs={{0,64},{32,96},{64,0},{96,32},{128,192},{160,224},{192,128},{224,1... | collective-permute-start | bytes 786440 | tf_op jit(solution)/shard_map/ppermute | solution.py:439
  26.6 4.9 %collective-permute-done.key_far_ref = bf16[4,128,256]{2,1,0:T(8,128)(2,1)S(1)} collective-permute-done((bf16[4,128,256]{2,1,0:T(8,128)(2,1)S(1)}, bf16[4,128,256]{2,1,0:T(8,128)(2,1)S(1)}, u32[]{:S(2)}, u32[]{:S(2)}) %collective-permute-start) | collective-permute-done | bytes 262176 | tf_op jit(solution)/shard_map/ppermute | solution.py:438
  31.4 2.5 %attend_own.1 = (f32[4,128,128]{2,1,0:T(8,128)S(1)}, f32[4,256,256]{2,1,0:T(8,128)S(1)}) custom-call(s32[1]{0:T(128)S(6)} %copy.11.length_ref, bf16[4,128,512]{2,1,0:T(8,128)(2,1)S(1)} %all_to_all.20.own_ref, bf16[4,128,256]{2,1,0:T(8,128)(2,1)S(1)} %collective-permute-done.key_far_ref), custom_call_target="tpu_custom_call" | custom-call | flops 419430400 | bytes 2097152 | tf_op jit(solution)/shard_map/attend_own/pallas_call | solution.py:270
  34.0 1.8 %collective-permute-done.1.query_far_ref = bf16[4,128,256]{2,1,0:T(8,128)(2,1)S(1)} collective-permute-done((bf16[4,128,256]{2,1,0:T(8,128)(2,1)S(1)}, bf16[4,128,256]{2,1,0:T(8,128)(2,1)S(1)}, u32[]{:S(2)}, u32[]{:S(2)}) %collective-permute-start.1) | collective-permute-done | bytes 262176 | tf_op jit(solution)/shard_map/ppermute | solution.py:439
  35.8 0.0 copy-start
  35.8 0.0 copy-start.1
  35.8 0.0 copy-start.2
  35.8 0.0 copy-start.3
  35.8 0.0 copy-start.4
  35.8 0.0 copy-start.5
  35.8 2.6 %attend_far.1 = (bf16[4,128,128]{2,1,0:T(8,128)(2,1)S(1)}, f32[4,128,256]{2,1,0:T(8,128)S(1)}, bf16[4,128,256]{2,1,0:T(8,128)(2,1)S(1)}) custom-call(s32[1]{0:T(128)S(6)} %copy.11.length_ref, bf16[4,128,512]{2,1,0:T(8,128)(2,1)S(1)} %all_to_all.20.own_ref, bf16[4,128,256]{2,1,0:T(8,128)(2,1)S(1)} %collective-permute-done.1.query_far_ref, ...), custom_call_target="tpu_custom_call" | custom-call | flops 419430400 | bytes 2097152 | tf_op jit(solution)/shard_map/attend_far/pallas_call | solution.py:285
  38.3 4.2 %collective-permute-start.3 = (bf16[4,128,256]{2,1,0:T(8,128)(2,1)S(1)}, bf16[4,128,256]{2,1,0:T(8,128)(2,1)S(1)}, u32[]{:S(2)}, u32[]{:S(2)}) collective-permute-start(bf16[4,128,256]{2,1,0:T(8,128)(2,1)S(1)} %get-tuple-element.18), channel_id=1, source_target_pairs={{0,32},{32,0},{64,96},{96,64},{128,160},{160,128},{192,224},{224,1... | collective-permute-start | bytes 786440 | tf_op jit(solution)/shard_map/ppermute | solution.py:442
  42.6 3.0 %collective-permute-start.2 = (bf16[4,128,128]{2,1,0:T(8,128)(2,1)S(1)}, bf16[4,128,128]{2,1,0:T(8,128)(2,1)S(1)}, u32[]{:S(2)}, u32[]{:S(2)}) collective-permute-start(bf16[4,128,128]{2,1,0:T(8,128)(2,1)S(1)} %get-tuple-element.16), channel_id=1, source_target_pairs={{0,64},{32,96},{64,0},{96,32},{128,192},{160,224},{192,128},{224,1... | collective-permute-start | bytes 393224 | tf_op jit(solution)/shard_map/ppermute | solution.py:443
  45.6 5.4 %collective-permute-done.2.query_got_ref = bf16[4,128,128]{2,1,0:T(8,128)(2,1)S(1)} collective-permute-done((bf16[4,128,128]{2,1,0:T(8,128)(2,1)S(1)}, bf16[4,128,128]{2,1,0:T(8,128)(2,1)S(1)}, u32[]{:S(2)}, u32[]{:S(2)}) %collective-permute-start.2) | collective-permute-done | bytes 131104 | tf_op jit(solution)/shard_map/ppermute | solution.py:443
  50.9 0.0 collective-permute-done.3.key_got_ref
  50.9 0.1 join_parts.1
  51.0 9.8 %all_to_all.21.grads_ref = bf16[4,128,384]{2,1,0:T(8,128)(2,1)S(1)} all-to-all(bf16[4,128,384]{2,1,0:T(8,128)(2,1)S(1)} %join_parts.1), channel_id=1, replica_groups={{0,128,256,384},{32,160,288,416},{64,192,320,448},{96,224,352,480},{1,1..., dimensions={0} | all-to-all | bytes 786432 | tf_op jit(solution)/shard_map/all_to_all | solution.py:445
  60.8 0.0 copy-done
  60.8 0.0 copy-done.1
  60.8 0.0 copy-done.2
  60.8 0.0 copy-done.3
  60.8 0.0 copy-done.4
  60.8 0.0 copy-done.5
  60.8 1.6 %finish.1 = (bf16[128,2048]{1,0:T(8,128)(2,1)}, bf16[768,128]{1,0:T(8,128)(2,1)S(1)}) custom-call(bf16[4,128,384]{2,1,0:T(8,128)(2,1)S(1)} %all_to_all.21.grads_ref, f32[128,1536]{1,0:T(8,128)S(1)} %copy-done.1, bf16[128,512]{1,0:T(8,128)(2,1)S(1)} %copy-done.3, f32[128,512]{1,0:T(8,128)S(1)} %copy-done.2, bf16[512,2048]{1,0:T(8,128)(2,1)S(1)} %copy-done, ...), custom_call_target="tpu_custom_call" | custom-call | tf_op jit(solution)/shard_map/finish/pallas_call | solution.py:379
  62.4 30.1 %all_to_all.22 = bf16[32,24,128]{2,1,0:T(8,128)(2,1)S(1)} all-to-all(bf16[32,24,128]{2,1,0:T(8,128)(2,1)S(1)} %bitcast.10), channel_id=1, replica_groups=mesh['ctx'=16,'table'=32] {'table'}, dimensions={0} | all-to-all | bytes 393216 | tf_op jit(solution)/shard_map/all_to_all | solution.py:447
  92.5 14.3 %all-gather = bf16[128,24,128]{2,1,0:T(8,128)(2,1)S(1)} all-gather(bf16[32,24,128]{2,1,0:T(8,128)(2,1)S(1)} %all_to_all.22), channel_id=2, replica_groups={{0,128,256,384},{32,160,288,416},{64,192,320,448},{96,224,352,480},{1,1..., dimensions={0}, use_global_device_ids=true | all-gather | bytes 983040 | tf_op jit(solution)/shard_map/all_gather | solution.py:448
  106.8 0.6 scatter_rows.1
  107.4 9.3 %all_to_all.23 = bf16[4,64,512]{2,1,0:T(8,128)(2,1)S(1)} all-to-all(bf16[4,64,512]{2,1,0:T(8,128)(2,1)S(1)} %bitcast.9), channel_id=1, replica_groups={{0,32,64,96},{128,160,192,224},{256,288,320,352},{384,416,448,480},{1,3..., dimensions={0} | all-to-all | bytes 524288 | tf_op jit(solution)/shard_map/all_to_all | solution.py:450
  116.7 0.7 convert_reduce_fusion
  (1 shorter events, 0.0 us)
Async XLA Ops:
  19.1 12.3 %collective-permute-start = (bf16[4,128,256]{2,1,0:T(8,128)(2,1)S(1)}, bf16[4,128,256]{2,1,0:T(8,128)(2,1)S(1)}, u32[]{:S(2)}, u32[]{:S(2)}) collective-permute-start(bf16[4,128,256]{2,1,0:T(8,128)(2,1)S(1)} %get-tuple-element.25), channel_id=1, source_target_pairs={{0,32},{32,0},{64,96},{96,64},{128,160},{160,128},{192,224},{224,1... | collective-permute-start | bytes 786440 | tf_op jit(solution)/shard_map/ppermute | solution.py:438
  24.6 11.1 %collective-permute-start.1 = (bf16[4,128,256]{2,1,0:T(8,128)(2,1)S(1)}, bf16[4,128,256]{2,1,0:T(8,128)(2,1)S(1)}, u32[]{:S(2)}, u32[]{:S(2)}) collective-permute-start(bf16[4,128,256]{2,1,0:T(8,128)(2,1)S(1)} %get-tuple-element.24), channel_id=1, source_target_pairs={{0,64},{32,96},{64,0},{96,32},{128,192},{160,224},{192,128},{224,1... | collective-permute-start | bytes 786440 | tf_op jit(solution)/shard_map/ppermute | solution.py:439
  35.8 25.0 %copy-start = (bf16[512,2048]{1,0:T(8,128)(2,1)S(1)}, bf16[512,2048]{1,0:T(8,128)(2,1)}, u32[]{:S(2)}) copy-start(bf16[512,2048]{1,0:T(8,128)(2,1)} %in_proj_ref.1) | copy-start | bytes 6291460
  35.8 25.0 %copy-start.1 = (f32[128,1536]{1,0:T(8,128)S(1)}, f32[128,1536]{1,0:T(8,128)}, u32[]{:S(2)}) copy-start(f32[128,1536]{1,0:T(8,128)} %get-tuple-element.19.slope_ref) | copy-start | bytes 2359300
  35.8 25.0 %copy-start.2 = (f32[128,512]{1,0:T(8,128)S(1)}, f32[128,512]{1,0:T(8,128)}, u32[]{:S(2)}) copy-start(f32[128,512]{1,0:T(8,128)} %get-tuple-element.21.base_ref) | copy-start | bytes 786436
  35.8 25.0 %copy-start.3 = (bf16[128,512]{1,0:T(8,128)(2,1)S(1)}, bf16[128,512]{1,0:T(8,128)(2,1)}, u32[]{:S(2)}) copy-start(bf16[128,512]{1,0:T(8,128)(2,1)} %get-tuple-element.20.gate_ref) | copy-start | bytes 393220
  35.8 25.1 %copy-start.4 = (s32[1,128]{1,0:T(1,128)S(1)}, s32[1,128]{1,0:T(1,128)}, u32[]{:S(2)}) copy-start(s32[1,128]{1,0:T(1,128)} %slot_ref.1) | copy-start | bytes 1540
  35.8 25.1 %copy-start.5 = (s32[1,128]{1,0:T(1,128)S(1)}, s32[1,128]{1,0:T(1,128)}, u32[]{:S(2)}) copy-start(s32[1,128]{1,0:T(1,128)} %item_ref.1) | copy-start | bytes 1540
  38.3 12.6 %collective-permute-start.3 = (bf16[4,128,256]{2,1,0:T(8,128)(2,1)S(1)}, bf16[4,128,256]{2,1,0:T(8,128)(2,1)S(1)}, u32[]{:S(2)}, u32[]{:S(2)}) collective-permute-start(bf16[4,128,256]{2,1,0:T(8,128)(2,1)S(1)} %get-tuple-element.18), channel_id=1, source_target_pairs={{0,32},{32,0},{64,96},{96,64},{128,160},{160,128},{192,224},{224,1... | collective-permute-start | bytes 786440 | tf_op jit(solution)/shard_map/ppermute | solution.py:442
  42.6 8.3 %collective-permute-start.2 = (bf16[4,128,128]{2,1,0:T(8,128)(2,1)S(1)}, bf16[4,128,128]{2,1,0:T(8,128)(2,1)S(1)}, u32[]{:S(2)}, u32[]{:S(2)}) collective-permute-start(bf16[4,128,128]{2,1,0:T(8,128)(2,1)S(1)} %get-tuple-element.16), channel_id=1, source_target_pairs={{0,64},{32,96},{64,0},{96,32},{128,192},{160,224},{192,128},{224,1... | collective-permute-start | bytes 393224 | tf_op jit(solution)/shard_map/ppermute | solution.py:443

commit v2 on v1

--- a/solution.py
+++ b/solution.py
@@ -16,17 +16,25 @@
 CAP = 4
 SUM_ROWS = CAP * WIDTH // 128
 SEND_ROWS = SUM_ROWS + 8
+GIVE_SUMS = TABLES * SUM_ROWS
+GIVE_ROWS = GIVE_SUMS + 16
 X_COUNT = 4
 Y_COUNT = 4
+TILE = 2 * TOKENS
 VMEM_LIMIT = 48 * 1024 * 1024
-ALL_VMEM = 63 * 1024 * 1024
 BF16 = jnp.bfloat16
 F32 = jnp.float32
 
+X_PAIRS = ((0, 3), (1, 2))
+HEAD_GROUPS = [
+    [X_PAIRS[pair][place] * Y_COUNT + upper * 2 + parity for place in range(2) for parity in range(2)]
+    for pair in range(2)
+    for upper in range(2)
+]
 X_GROUPS = [[x * Y_COUNT + y for x in range(X_COUNT)] for y in range(Y_COUNT)]
 Y_GROUPS = [[x * Y_COUNT + y for y in range(Y_COUNT)] for x in range(X_COUNT)]
 SWAP_QUERY = [(c, c ^ 2) for c in range(X_COUNT * Y_COUNT)]
-SWAP_KEY = [(c, c ^ 1) for c in range(X_COUNT * Y_COUNT)]
+SWAP_KEY = [(c, c ^ Y_COUNT) for c in range(X_COUNT * Y_COUNT)]
 
 MATMUL = (((1,), (0,)), ((), ()))
 MATMUL_NT = (((1,), (1,)), ((), ()))
@@ -138,7 +146,7 @@
             parts_ref[head, :, place * HEAD_DIM : (place + 1) * HEAD_DIM] = hidden[:, cols]
 
 
-def project(length, inputs, saved, grad, in_proj, out_proj, gain):
+def project(length, *arrays):
     return pl.pallas_call(
         project_kernel,
         out_shape=(
@@ -158,144 +166,170 @@
             pltpu.VMEM((1, WIDTH), F32),
             pltpu.SemaphoreType.DMA((9,)),
         ],
-        compiler_params=params(ALL_VMEM),
+        compiler_params=params(),
         name="project",
-    )(length, inputs, saved, grad, in_proj, out_proj, gain)
-
-
-def tile_grads(queries, outs, keys, values, weight, live):
+    )(length, *(pltpu.with_memory_space_constraint(array, pltpu.HBM) for array in arrays))
+
+
+def tile_grads(query_ref, query_place, key_ref, key_place, key_column, weight, live):
     scale = HEAD_DIM ** (-0.5)
-    scores = dot(queries, keys, MATMUL_NT) * scale
-    attn_grad = dot(outs, values, MATMUL_NT)
-    squash = jax.nn.sigmoid(scores)
+    queries = query_ref[query_place, :, :HEAD_DIM]
+    outs = query_ref[query_place, :, HEAD_DIM : 2 * HEAD_DIM]
+    keys = key_ref[key_place, :, key_column : key_column + HEAD_DIM]
+    values = key_ref[key_place, :, key_column + HEAD_DIM : key_column + 2 * HEAD_DIM]
+    scores = dot(keys, queries, MATMUL_NT) * scale
+    attn_grad = dot(values, outs, MATMUL_NT)
+    squash = 0.5 + 0.5 * jnp.tanh(scores * 0.5)
     weighted = squash * weight
     if live is not None:
         weighted = jnp.where(live, weighted, 0.0)
-    attend = (scores * weighted).astype(BF16)
-    score_grad = (attn_grad * weighted * (1.0 + scores * (1.0 - squash))).astype(BF16)
+    gated = scores * weighted
+    attend = gated.astype(BF16)
+    score_grad = (attn_grad * (weighted + gated * (1.0 - squash))).astype(BF16)
     return (
-        dot(score_grad, keys, MATMUL) * scale,
-        dot(score_grad, queries, MATMUL_TN) * scale,
-        dot(attend, outs, MATMUL_TN),
-    )
-
-
-def attend_rows(length_ref, query_of, out_of, own_ref, key_far_ref, query_class, take_query, take_key):
-    lane = lax.rem(lax.axis_index("ctx"), Y_COUNT)
-    weight = jnp.full((1, 1), 1.0, F32) / jnp.full((1, 1), length_ref[0].astype(F32), F32)
-    rows = lax.broadcasted_iota(jnp.int32, (TOKENS, 1), 0)
-    columns = lax.broadcasted_iota(jnp.int32, (1, 2 * TOKENS), 1)
-    row_pos = (lane ^ query_class) * TOKENS + rows
-    column_pos = jnp.where(
-        columns < TOKENS, lane * TOKENS + columns, (lane ^ 1) * TOKENS + columns - TOKENS
-    )
-    live = column_pos <= row_pos
-    keys, values = [], []
-    for x in range(X_COUNT):
-        keys.append(
-            jnp.concatenate(
-                [own_ref[x, :, 2 * HEAD_DIM : 3 * HEAD_DIM], key_far_ref[x, :, :HEAD_DIM]], axis=0
-            )
-        )
-        values.append(
-            jnp.concatenate([own_ref[x, :, 3 * HEAD_DIM :], key_far_ref[x, :, HEAD_DIM:]], axis=0)
-        )
-    for query_x in range(X_COUNT):
-        queries, outs = query_of(query_x), out_of(query_x)
-        query_acc = None
-        for key_x in range(query_x + 1):
-            query_part, key_part, value_part = tile_grads(
-                queries, outs, keys[key_x], values[key_x], weight, live if query_x == key_x else None
-            )
-            query_acc = query_part if query_acc is None else query_acc + query_part
-            take_key(query_x, key_x, key_part, value_part)
-        take_query(query_x, query_acc)
-
-
-def attend_own_kernel(length_ref, own_ref, key_far_ref, query_ref, key_ref):
-    def take_query(x, part):
-        query_ref[x] = part
-
-    def take_key(query_x, x, key_part, value_part):
-        if query_x == x:
-            key_ref[x, :, :HEAD_DIM] = key_part
-            key_ref[x, :, HEAD_DIM:] = value_part
+        dot(score_grad, keys, MATMUL_TN) * scale,
+        dot(score_grad, queries, MATMUL) * scale,
+        dot(attend, outs, MATMUL),
+    )
+
+
+def place_of_device():
+    ctx = lax.axis_index("ctx")
+    x = lax.div(ctx, Y_COUNT)
+    return (x ^ lax.div(x, 2)) & 1, lax.div(lax.rem(ctx, Y_COUNT), 2)
+
+
+def weight_of(length_ref):
+    return jnp.full((1, 1), 1.0, F32) / jnp.full((1, 1), length_ref[0].astype(F32), F32)
+
+
+def attend_near(length_ref, query_ref, own_ref, flip):
+    _, upper = place_of_device()
+    weight = weight_of(length_ref)
+    rows = lax.broadcasted_iota(jnp.int32, (TILE, 1), 0) + upper * TILE
+    columns = lax.broadcasted_iota(jnp.int32, (1, TILE), 1) + (upper ^ flip) * TILE
+    live = rows <= columns
+    column = 2 * HEAD_DIM
+    low = tile_grads(query_ref, 0, own_ref, 0, column, weight, live)
+    whole = tile_grads(query_ref, 1, own_ref, 0, column, weight, None)
+    high = tile_grads(query_ref, 1, own_ref, 1, column, weight, live)
+    return low, whole, high
+
+
+def attend_own_kernel(length_ref, own_ref, query_ref, key_ref):
+    low, whole, high = attend_near(length_ref, own_ref, own_ref, 0)
+    query_ref[0] = low[0]
+    query_ref[1] = whole[0] + high[0]
+    key_ref[0, :, :HEAD_DIM] = low[1] + whole[1]
+    key_ref[0, :, HEAD_DIM:] = low[2] + whole[2]
+    key_ref[1, :, :HEAD_DIM] = high[1]
+    key_ref[1, :, HEAD_DIM:] = high[2]
+
+
+def attend_queries_kernel(length_ref, own_ref, query_far_ref, sums_ref, query_ref, key_ref):
+    low, whole, high = attend_near(length_ref, query_far_ref, own_ref, 1)
+    query_ref[0] = low[0]
+    query_ref[1] = whole[0] + high[0]
+    key_ref[0, :, :HEAD_DIM] = sums_ref[0, :, :HEAD_DIM] + (low[1] + whole[1])
+    key_ref[0, :, HEAD_DIM:] = sums_ref[0, :, HEAD_DIM:] + (low[2] + whole[2])
+    key_ref[1, :, :HEAD_DIM] = sums_ref[1, :, :HEAD_DIM] + high[1]
+    key_ref[1, :, HEAD_DIM:] = sums_ref[1, :, HEAD_DIM:] + high[2]
+
+
+def attend_keys_kernel(
+    length_ref,
+    own_ref,
+    query_far_ref,
+    key_far_ref,
+    near_own_ref,
+    near_far_ref,
+    query_own_ref,
+    query_send_ref,
+    key_send_ref,
+    query_acc,
+    key_acc,
+):
+    pair, _ = place_of_device()
+    weight = weight_of(length_ref)
+    last = 1 - pair
+    for place, (query_ref, near_ref) in enumerate(
+        ((own_ref, near_own_ref), (query_far_ref, near_far_ref))
+    ):
+        query_acc[...] = near_ref[...]
+        first = tile_grads(query_ref, 1, key_far_ref, 0, 0, weight, None)
+        query_acc[1] += first[0]
+        if place == 0:
+            key_acc[0, :, :HEAD_DIM] = first[1]
+            key_acc[0, :, HEAD_DIM:] = first[2]
+            key_acc[1] = jnp.zeros_like(key_acc[1])
         else:
-            key_ref[x, :, :HEAD_DIM] += key_part
-            key_ref[x, :, HEAD_DIM:] += value_part
-
-    attend_rows(
-        length_ref,
-        lambda x: own_ref[x, :, :HEAD_DIM],
-        lambda x: own_ref[x, :, HEAD_DIM : 2 * HEAD_DIM],
-        own_ref,
-        key_far_ref,
-        0,
-        take_query,
-        take_key,
-    )
-
-
-def attend_far_kernel(
-    length_ref, own_ref, query_far_ref, key_far_ref, sums_ref, query_ref, key_own_ref, key_send_ref, acc_ref
-):
-    def take_query(x, part):
-        query_ref[x] = part.astype(BF16)
-
-    def take_key(query_x, x, key_part, value_part):
-        source = sums_ref if query_x == x else acc_ref
-        acc_ref[x, :, :HEAD_DIM] = source[x, :, :HEAD_DIM] + key_part
-        acc_ref[x, :, HEAD_DIM:] = source[x, :, HEAD_DIM:] + value_part
-
-    attend_rows(
-        length_ref,
-        lambda x: query_far_ref[x, :, :HEAD_DIM],
-        lambda x: query_far_ref[x, :, HEAD_DIM:],
-        own_ref,
-        key_far_ref,
-        2,
-        take_query,
-        take_key,
-    )
-    key_own_ref[...] = acc_ref[:, :TOKENS, :]
-    key_send_ref[...] = acc_ref[:, TOKENS:, :].astype(BF16)
-
-
-ATTEND_COST = pl.CostEstimate(
-    flops=10 * 5 * 2 * 128 * 256 * 128, bytes_accessed=2 << 20, transcendentals=10 * 128 * 256
-)
-
-
-def attend_own(length, own, key_far):
+            key_acc[0, :, :HEAD_DIM] += first[1]
+            key_acc[0, :, HEAD_DIM:] += first[2]
+        second = tile_grads(query_ref, last, key_far_ref, last, 0, weight, None)
+        query_acc[last] += second[0]
+        key_acc[last, :, :HEAD_DIM] += second[1]
+        key_acc[last, :, HEAD_DIM:] += second[2]
+        if place == 0:
+            query_own_ref[...] = query_acc[...]
+        else:
+            query_send_ref[...] = query_acc[...].astype(BF16)
+    key_send_ref[...] = key_acc[...].astype(BF16)
+
+
+def attend_cost(tiles):
+    return pl.CostEstimate(
+        flops=tiles * 5 * 2 * TILE * TILE * HEAD_DIM,
+        bytes_accessed=2 << 20,
+        transcendentals=tiles * TILE * TILE,
+    )
+
+
+QUERY_SUMS = jax.ShapeDtypeStruct((2, TILE, HEAD_DIM), F32)
+KEY_SUMS = jax.ShapeDtypeStruct((2, TILE, 2 * HEAD_DIM), F32)
+
+
+def attend_own(length, own):
     return pl.pallas_call(
         attend_own_kernel,
+        out_shape=(QUERY_SUMS, KEY_SUMS),
+        in_specs=[in_smem()] + in_vmem(1),
+        out_specs=tuple(in_vmem(2)),
+        compiler_params=params(),
+        cost_estimate=attend_cost(3),
+        name="attend_own",
+    )(length, own)
+
+
+def attend_queries(length, own, query_far, sums):
+    return pl.pallas_call(
+        attend_queries_kernel,
+        out_shape=(QUERY_SUMS, KEY_SUMS),
+        in_specs=[in_smem()] + in_vmem(3),
+        out_specs=tuple(in_vmem(2)),
+        compiler_params=params(),
+        cost_estimate=attend_cost(3),
+        name="attend_queries",
+    )(length, own, query_far, sums)
+
+
+def attend_keys(length, own, query_far, key_far, near_own, near_far):
+    return pl.pallas_call(
+        attend_keys_kernel,
         out_shape=(
-            jax.ShapeDtypeStruct((X_COUNT, TOKENS, HEAD_DIM), F32),
-            jax.ShapeDtypeStruct((X_COUNT, 2 * TOKENS, 2 * HEAD_DIM), F32),
+            QUERY_SUMS,
+            jax.ShapeDtypeStruct((2, TILE, HEAD_DIM), BF16),
+            jax.ShapeDtypeStruct((2, TILE, 2 * HEAD_DIM), BF16),
         ),
-        in_specs=[in_smem()] + in_vmem(2),
-        out_specs=tuple(in_vmem(2)),
-        compiler_params=params(),
-        cost_estimate=ATTEND_COST,
-        name="attend_own",
-    )(length, own, key_far)
-
-
-def attend_far(length, own, query_far, key_far, sums):
-    return pl.pallas_call(
-        attend_far_kernel,
-        out_shape=(
-            jax.ShapeDtypeStruct((X_COUNT, TOKENS, HEAD_DIM), BF16),
-            jax.ShapeDtypeStruct((X_COUNT, TOKENS, 2 * HEAD_DIM), F32),
-            jax.ShapeDtypeStruct((X_COUNT, TOKENS, 2 * HEAD_DIM), BF16),
-        ),
-        in_specs=[in_smem()] + in_vmem(4),
+        in_specs=[in_smem()] + in_vmem(5),
         out_specs=tuple(in_vmem(3)),
-        scratch_shapes=[pltpu.VMEM((X_COUNT, 2 * TOKENS, 2 * HEAD_DIM), F32)],
-        compiler_params=params(),
-        cost_estimate=ATTEND_COST,
-        name="attend_far",
-    )(length, own, query_far, key_far, sums)
+        scratch_shapes=[
+            pltpu.VMEM((2, TILE, HEAD_DIM), F32),
+            pltpu.VMEM((2, TILE, 2 * HEAD_DIM), F32),
+        ],
+        compiler_params=params(),
+        cost_estimate=attend_cost(4),
+        name="attend_keys",
+    )(length, own, query_far, key_far, near_own, near_far)
 
 
 def join_kernel(query_own_ref, query_got_ref, key_own_ref, key_got_ref, out_ref):
@@ -313,7 +347,7 @@
 def join_parts(query_own, query_got, key_own, key_got):
     return pl.pallas_call(
         join_kernel,
-        out_shape=jax.ShapeDtypeStruct((X_COUNT, TOKENS, 3 * HEAD_DIM), BF16),
+        out_shape=jax.ShapeDtypeStruct((2, TILE, 3 * HEAD_DIM), BF16),
         in_specs=in_vmem(4),
         out_specs=in_vmem(1)[0],
         compiler_params=params(),
@@ -390,19 +424,54 @@
     )(grads, slope, gate, base, in_proj, slots, items)
 
 
+def compact_kernel(rows_ref, out_ref, wide_ref, packed_ref):
+    x = lax.div(lax.axis_index("ctx"), Y_COUNT)
+    wide_ref[...] = rows_ref[...].astype(F32)
+    for owner in range(TABLES):
+        packed_ref[owner * SUM_ROWS : (owner + 1) * SUM_ROWS, :] = wide_ref[
+            owner * SEND_ROWS : owner * SEND_ROWS + SUM_ROWS, :
+        ]
+    coded = wide_ref[pl.ds(SUM_ROWS, TABLES, stride=SEND_ROWS), :].T[: 2 * CAP]
+    lane = lax.broadcasted_iota(jnp.int32, (2 * CAP, 128), 1)
+    spaced = jnp.where(lane // TABLES == x, jnp.concatenate([coded] * X_COUNT, axis=1), 0.0)
+    packed_ref[GIVE_SUMS : GIVE_SUMS + 2 * CAP, :] = spaced
+    packed_ref[GIVE_SUMS + 2 * CAP :, :] = jnp.zeros((GIVE_ROWS - GIVE_SUMS - 2 * CAP, 128), F32)
+    out_ref[...] = packed_ref[...].astype(BF16)
+
+
+def compact_rows(rows):
+    return pl.pallas_call(
+        compact_kernel,
+        out_shape=jax.ShapeDtypeStruct((GIVE_ROWS, 128), BF16),
+        in_specs=in_vmem(1),
+        out_specs=in_vmem(1)[0],
+        scratch_shapes=[
+            pltpu.VMEM((TABLES * SEND_ROWS, 128), F32),
+            pltpu.VMEM((GIVE_ROWS, 128), F32),
+        ],
+        compiler_params=params(),
+        name="compact_rows",
+    )(rows)
+
+
 def scatter_kernel(rows_ref, out_ref, wide_ref):
     targets = Y_COUNT * ROWS_DEV
-    count = X_COUNT * TABLES
     first = lax.div(lax.axis_index("ctx"), Y_COUNT) * targets
     wide_ref[...] = rows_ref[...].astype(F32)
-    coded = wide_ref[pl.ds(SUM_ROWS, count, stride=SEND_ROWS), :].T
-    ids = (coded[:CAP] * ROWS_DEV + coded[CAP : 2 * CAP]).astype(jnp.int32)
+    coded = sum(wide_ref[x, GIVE_SUMS : GIVE_SUMS + 2 * CAP, :] for x in range(X_COUNT))
+    ids = (coded[:CAP] * ROWS_DEV + coded[CAP:]).astype(jnp.int32)
     target = first + lax.broadcasted_iota(jnp.int32, (targets, 1), 0)
     hots = [(ids[level : level + 1, :] == target).astype(F32).astype(BF16) for level in range(CAP)]
     for chunk in range(WIDTH // 128):
         total = None
         for level in range(CAP):
-            rows = wide_ref[pl.ds(level * 4 + chunk, count, stride=SEND_ROWS), :].astype(BF16)
+            rows = jnp.concatenate(
+                [
+                    wide_ref[x, pl.ds(level * 4 + chunk, TABLES, stride=SUM_ROWS), :]
+                    for x in range(X_COUNT)
+                ],
+                axis=0,
+            ).astype(BF16)
             part = dot(hots[level], rows, MATMUL)
             total = part if total is None else total + part
         out_ref[:, chunk * 128 : (chunk + 1) * 128] = total.astype(BF16)
@@ -414,7 +483,7 @@
         out_shape=jax.ShapeDtypeStruct((Y_COUNT * ROWS_DEV, WIDTH), BF16),
         in_specs=in_vmem(1),
         out_specs=in_vmem(1)[0],
-        scratch_shapes=[pltpu.VMEM((X_COUNT * TABLES * SEND_ROWS, 128), F32)],
+        scratch_shapes=[pltpu.VMEM((X_COUNT, GIVE_ROWS, 128), F32)],
         compiler_params=params(),
         name="scatter_rows",
     )(rows)
@@ -434,19 +503,26 @@
     parts, slope, gate, base = project(
         seq_lengths, item_inputs[0], attn_saved[0], out_grad[0], in_proj, out_proj, norm_gain[None]
     )
-    own = lax.all_to_all(parts, "ctx", 0, 0, axis_index_groups=X_GROUPS)
+    own = lax.all_to_all(parts, "ctx", 0, 0, axis_index_groups=HEAD_GROUPS)
+    own = own.reshape(2, TILE, 4 * HEAD_DIM)
+    query_far = lax.ppermute(own[:, :, : 2 * HEAD_DIM], "ctx", SWAP_QUERY)
     key_far = lax.ppermute(own[:, :, 2 * HEAD_DIM :], "ctx", SWAP_KEY)
-    query_far = lax.ppermute(own[:, :, : 2 * HEAD_DIM], "ctx", SWAP_QUERY)
-    query_own, sums = attend_own(seq_lengths, own, key_far)
-    query_send, key_own, key_send = attend_far(seq_lengths, own, query_far, key_far, sums)
+    near_own, sums = attend_own(seq_lengths, own)
+    near_far, key_own = attend_queries(seq_lengths, own, query_far, sums)
+    query_own, query_send, key_send = attend_keys(
+        seq_lengths, own, query_far, key_far, near_own, near_far
+    )
+    query_got = lax.ppermute(query_send, "ctx", SWAP_QUERY)
     key_got = lax.ppermute(key_send, "ctx", SWAP_KEY)
-    query_got = lax.ppermute(query_send, "ctx", SWAP_QUERY)
     joined = join_parts(query_own, query_got, key_own, key_got)
-    grads = lax.all_to_all(joined, "ctx", 0, 0, axis_index_groups=X_GROUPS)
+    grads = lax.all_to_all(
+        joined.reshape(HEADS, TOKENS, 3 * HEAD_DIM), "ctx", 0, 0, axis_index_groups=HEAD_GROUPS
+    )
     proj_grad, rows = finish(grads, slope, gate, base, in_proj, token_slot, slot_rows)
     rows = lax.all_to_all(rows.reshape(TABLES, SEND_ROWS, 128), "table", 0, 0)
+    rows = compact_rows(rows.reshape(TABLES * SEND_ROWS, 128))
     rows = lax.all_gather(rows, "ctx", axis_index_groups=X_GROUPS)
-    dense = scatter_rows(rows.reshape(X_COUNT * TABLES * SEND_ROWS, 128))
+    dense = scatter_rows(rows)
     pieces = lax.all_to_all(
         dense.reshape(Y_COUNT, ROWS_DEV, WIDTH), "ctx", 0, 0, axis_index_groups=Y_GROUPS
     )

time: 118 us -> 116 us (0.983)
  blocking collectives: 77.3 us -> 81.2 us
  starting transfers between devices: 14.6 us -> 12.1 us
  Pallas kernels: 11.4 us -> 9.69 us
  waiting for transfers between devices: 12 us -> 10.3 us
    ppermute x1, waiting for transfers between devices: 1.77 us -> 6.75 us  [per_device(): query_far = lax.ppermute(own[:, :, :2 * HEAD_DIM], 'ctx', SWAP_QUERY)]
    ppermute x1, waiting for transfers between devices: 4.88 us -> 0.01 us  [per_device(): key_far = lax.ppermute(own[:, :, 2 * HEAD_DIM:], 'ctx', SWAP_KEY)]
    all_to_all x2, blocking collectives: 23.6 us -> 27.6 us  [the longest x1 15.5 us: per_device(): own = lax.all_to_all(parts, 'ctx', 0, 0, axis_index_groups=HEAD_GROUPS)]
    ppermute x1, starting transfers between devices: 5.48 us -> 1.92 us  [per_device(): key_far = lax.ppermute(own[:, :, 2 * HEAD_DIM:], 'ctx', SWAP_KEY)]
    ppermute x1, starting transfers between devices: 4.24 us -> 1.92 us  [per_device(): key_got = lax.ppermute(key_send, 'ctx', SWAP_KEY)]
    ppermute x1, starting transfers between devices: 2.97 us -> 5.29 us  [per_device(): query_got = lax.ppermute(query_send, 'ctx', SWAP_QUERY)]
    ppermute x1, waiting for transfers between devices: 5.35 us -> 3.56 us  [per_device(): query_got = lax.ppermute(query_send, 'ctx', SWAP_QUERY)]
    pallas_call x3 -> x5, Pallas kernels: 5.16 us -> 4.59 us  [the longest x1 1.78 us: attend_keys(): pl.pallas_call(attend_keys_kernel, out_shape=(QUERY_SUMS, jax.ShapeDtypeS...]
  transfers between devices with their start and end apart: 4 -> 4, of which waited for: 3 -> 2; matrix products, arithmetic and copies ran while one was open for 0% -> 0% of each run, Pallas kernels for 2% -> 2%
where the time goes in v2:
time: 116 us; the launch traced here: 115 us
  blocking collectives  81.2 us (70%)
  starting transfers between devices  12.1 us (10%)
  waiting for transfers between devices  10.3 us (9%)
  Pallas kernels  9.69 us (8%)
  between operations  1.39 us (1%)
    all_to_all x1, blocking collectives, per_device(): rows = lax.all_to_all(rows.reshape(TABLES, SEND_ROWS, 128), 'table', 0, 0)  31 us
    all_to_all x1, blocking collectives, per_device(): own = lax.all_to_all(parts, 'ctx', 0, 0, axis_index_groups=HEAD_GROUPS)  15.5 us
    all_gather x1, blocking collectives, per_device(): rows = lax.all_gather(rows, 'ctx', axis_index_groups=X_GROUPS)  13.4 us
    all_to_all x1, blocking collectives, per_device(): lax.all_to_all(joined.reshape(HEADS, TOKENS, 3 * HEAD_DIM), 'ctx', 0, 0,...  12.2 us
    all_to_all x1, blocking collectives, per_device(): lax.all_to_all(dense.reshape(Y_COUNT, ROWS_DEV, WIDTH), 'ctx', 0, 0, axis...  9.31 us
    ppermute x1, waiting for transfers between devices, per_device(): query_far = lax.ppermute(own[:, :, :2 * HEAD_DIM], 'ctx', SWAP_QUERY)  6.75 us
    ppermute x1, starting transfers between devices, per_device(): query_got = lax.ppermute(query_send, 'ctx', SWAP_QUERY)  5.29 us
    ppermute x1, waiting for transfers between devices, per_device(): query_got = lax.ppermute(query_send, 'ctx', SWAP_QUERY)  3.56 us
  transfers between devices with their start and end apart: 4, of which 2 were waited for; matrix products, arithmetic and copies ran while one was open for 0% of the time, Pallas kernels for 2%

profile of v2, /device:TPU:8, one launch (start us, length us, event | category | flops | bytes accessed | tf_op | source)
XLA Modules:
  0.0 115.5 jit_solution(11679935811313043544)
XLA Ops:
  1.3 3.0 %project.1 = (bf16[4,128,512]{2,1,0:T(8,128)(2,1)S(1)}, f32[128,1536]{1,0:T(8,128)S(1)}, bf16[128,512]{1,0:T(8,128)(2,1)S(1)}, f32[128,512]{1,0:T(8,128)S(1)}) custom-call(s32[1]{0:T(128)S(6)} %copy.11.length_ref, bf16[128,512]{1,0:T(8,128)(2,1)} %bitcast.20, bf16[128,512]{1,0:T(8,128)(2,1)} %bitcast.21, bf16[128,512]{1,0:T(8,128)(2,1)} %bitcast.22, ...), custom_call_target="tpu_custom_call" | custom-call | tf_op jit(solution)/shard_map/project/pallas_call | solution.py:150
  4.2 15.5 %all_to_all.20 = bf16[4,128,512]{2,1,0:T(8,128)(2,1)S(1)} all-to-all(bf16[4,128,512]{2,1,0:T(8,128)(2,1)S(1)} %get-tuple-element.15), channel_id=1, replica_groups={{0,32,384,416},{64,96,448,480},{128,160,256,288},{192,224,320,352},{1,3..., dimensions={0} | all-to-all | bytes 1048576 | tf_op jit(solution)/shard_map/all_to_all | solution.py:506
  19.7 3.0 %collective-permute-start = (bf16[2,256,256]{2,1,0:T(8,128)(2,1)S(1)}, bf16[2,256,256]{2,1,0:T(8,128)(2,1)S(1)}, u32[]{:S(2)}, u32[]{:S(2)}) collective-permute-start(bf16[2,256,256]{2,1,0:T(8,128)(2,1)S(1)} %get-tuple-element.29), channel_id=1, source_target_pairs={{0,64},{32,96},{64,0},{96,32},{128,192},{160,224},{192,128},{224,1... | collective-permute-start | bytes 786440 | tf_op jit(solution)/shard_map/ppermute | solution.py:508
  22.7 1.9 %collective-permute-start.1 = (bf16[2,256,256]{2,1,0:T(8,128)(2,1)S(1)}, bf16[2,256,256]{2,1,0:T(8,128)(2,1)S(1)}, u32[]{:S(2)}, u32[]{:S(2)}) collective-permute-start(bf16[2,256,256]{2,1,0:T(8,128)(2,1)S(1)} %get-tuple-element.28), channel_id=1, source_target_pairs={{0,128},{32,160},{64,192},{96,224},{128,0},{160,32},{192,64},{224,... | collective-permute-start | bytes 786440 | tf_op jit(solution)/shard_map/ppermute | solution.py:509
  24.6 1.3 %attend_own.1 = (f32[2,256,128]{2,1,0:T(8,128)S(1)}, f32[2,256,256]{2,1,0:T(8,128)S(1)}) custom-call(s32[1]{0:T(128)S(6)} %copy.11.length_ref, bf16[2,256,512]{2,1,0:T(8,128)(2,1)S(1)} %bitcast.12), custom_call_target="tpu_custom_call" | custom-call | flops 251658240 | bytes 2097152 | tf_op jit(solution)/shard_map/attend_own/pallas_call | solution.py:292
  25.9 6.8 %collective-permute-done.query_far_ref = bf16[2,256,256]{2,1,0:T(8,128)(2,1)S(1)} collective-permute-done((bf16[2,256,256]{2,1,0:T(8,128)(2,1)S(1)}, bf16[2,256,256]{2,1,0:T(8,128)(2,1)S(1)}, u32[]{:S(2)}, u32[]{:S(2)}) %collective-permute-start) | collective-permute-done | bytes 262176 | tf_op jit(solution)/shard_map/ppermute | solution.py:508
  32.7 1.3 %attend_queries.1 = (f32[2,256,128]{2,1,0:T(8,128)S(1)}, f32[2,256,256]{2,1,0:T(8,128)S(1)}) custom-call(s32[1]{0:T(128)S(6)} %copy.11.length_ref, bf16[2,256,512]{2,1,0:T(8,128)(2,1)S(1)} %bitcast.13, bf16[2,256,256]{2,1,0:T(8,128)(2,1)S(1)} %collective-permute-done.query_far_ref, f32[2,256,256]{2,1,0:T(8,128)S(1)} %get-tuple-element.17.sums_ref), custom_call_target="tpu_custom_call" | custom-call | flops 251658240 | bytes 2097152 | tf_op jit(solution)/shard_map/attend_queries/pallas_call | solution.py:304
  34.0 0.0 copy-start
  34.0 0.0 copy-start.1
  34.0 0.0 copy-start.2
  34.0 0.0 collective-permute-done.1.key_far_ref
  34.0 1.8 %attend_keys.1 = (f32[2,256,128]{2,1,0:T(8,128)S(1)}, bf16[2,256,128]{2,1,0:T(8,128)(2,1)S(1)}, bf16[2,256,256]{2,1,0:T(8,128)(2,1)S(1)}) custom-call(s32[1]{0:T(128)S(6)} %copy.11.length_ref, bf16[2,256,512]{2,1,0:T(8,128)(2,1)S(1)} %bitcast.14, bf16[2,256,256]{2,1,0:T(8,128)(2,1)S(1)} %collective-permute-done.query_far_ref, ...), custom_call_target="tpu_custom_call" | custom-call | flops 335544320 | bytes 2097152 | tf_op jit(solution)/shard_map/attend_keys/pallas_call | solution.py:316
  35.8 1.9 %collective-permute-start.3 = (bf16[2,256,256]{2,1,0:T(8,128)(2,1)S(1)}, bf16[2,256,256]{2,1,0:T(8,128)(2,1)S(1)}, u32[]{:S(2)}, u32[]{:S(2)}) collective-permute-start(bf16[2,256,256]{2,1,0:T(8,128)(2,1)S(1)} %get-tuple-element.22), channel_id=1, source_target_pairs={{0,128},{32,160},{64,192},{96,224},{128,0},{160,32},{192,64},{224,... | collective-permute-start | bytes 786440 | tf_op jit(solution)/shard_map/ppermute | solution.py:516
  37.7 5.3 %collective-permute-start.2 = (bf16[2,256,128]{2,1,0:T(8,128)(2,1)S(1)}, bf16[2,256,128]{2,1,0:T(8,128)(2,1)S(1)}, u32[]{:S(2)}, u32[]{:S(2)}) collective-permute-start(bf16[2,256,128]{2,1,0:T(8,128)(2,1)S(1)} %get-tuple-element.20), channel_id=1, source_target_pairs={{0,64},{32,96},{64,0},{96,32},{128,192},{160,224},{192,128},{224,1... | collective-permute-start | bytes 393224 | tf_op jit(solution)/shard_map/ppermute | solution.py:515
  43.0 3.6 %collective-permute-done.2.query_got_ref = bf16[2,256,128]{2,1,0:T(8,128)(2,1)S(1)} collective-permute-done((bf16[2,256,128]{2,1,0:T(8,128)(2,1)S(1)}, bf16[2,256,128]{2,1,0:T(8,128)(2,1)S(1)}, u32[]{:S(2)}, u32[]{:S(2)}) %collective-permute-start.2) | collective-permute-done | bytes 131104 | tf_op jit(solution)/shard_map/ppermute | solution.py:515
  46.6 0.0 collective-permute-done.3.key_got_ref
  46.6 0.1 join_parts.1
  46.7 12.2 %all_to_all.21.grads_ref = bf16[4,128,384]{2,1,0:T(8,128)(2,1)S(1)} all-to-all(bf16[4,128,384]{2,1,0:T(8,128)(2,1)S(1)} %bitcast.16), channel_id=1, replica_groups={{0,32,384,416},{64,96,448,480},{128,160,256,288},{192,224,320,352},{1,3..., dimensions={0} | all-to-all | bytes 786432 | tf_op jit(solution)/shard_map/all_to_all | solution.py:518
  58.8 0.0 copy-done
  58.8 0.0 copy-done.1
  58.8 0.0 copy-done.2
  58.8 1.6 %finish.1 = (bf16[128,2048]{1,0:T(8,128)(2,1)}, bf16[768,128]{1,0:T(8,128)(2,1)S(1)}) custom-call(bf16[4,128,384]{2,1,0:T(8,128)(2,1)S(1)} %all_to_all.21.grads_ref, f32[128,1536]{1,0:T(8,128)S(1)} %get-tuple-element.23.slope_ref, bf16[128,512]{1,0:T(8,128)(2,1)S(1)} %get-tuple-element.24.gate_ref, f32[128,512]{1,0:T(8,128)S(1)} %get-tuple-element.25.base_ref, ...), custom_call_target="tpu_custom_call" | custom-call | tf_op jit(solution)/shard_map/finish/pallas_call | solution.py:413
  60.4 31.0 %all_to_all.22 = bf16[32,24,128]{2,1,0:T(8,128)(2,1)S(1)} all-to-all(bf16[32,24,128]{2,1,0:T(8,128)(2,1)S(1)} %bitcast.19), channel_id=1, replica_groups=mesh['ctx'=16,'table'=32] {'table'}, dimensions={0} | all-to-all | bytes 393216 | tf_op jit(solution)/shard_map/all_to_all | solution.py:522
  91.4 0.2 compact_rows.1
  91.5 13.4 %all-gather = bf16[2112,128]{1,0:T(8,128)(2,1)S(1)} all-gather(bf16[528,128]{1,0:T(8,128)(2,1)S(1)} %compact_rows.1), channel_id=2, replica_groups={{0,128,256,384},{32,160,288,416},{64,192,320,448},{96,224,352,480},{1,1..., dimensions={0}, use_global_device_ids=true | all-gather | bytes 675840 | tf_op jit(solution)/shard_map/all_gather | solution.py:524
  104.9 0.6 scatter_rows.1
  105.5 9.3 %all_to_all.23 = bf16[4,64,512]{2,1,0:T(8,128)(2,1)S(1)} all-to-all(bf16[4,64,512]{2,1,0:T(8,128)(2,1)S(1)} %bitcast.17), channel_id=1, replica_groups={{0,32,64,96},{128,160,192,224},{256,288,320,352},{384,416,448,480},{1,3..., dimensions={0} | all-to-all | bytes 524288 | tf_op jit(solution)/shard_map/all_to_all | solution.py:526
  114.8 0.7 convert_reduce_fusion
  (1 shorter events, 0.0 us)
Async XLA Ops:
  19.7 12.9 %collective-permute-start = (bf16[2,256,256]{2,1,0:T(8,128)(2,1)S(1)}, bf16[2,256,256]{2,1,0:T(8,128)(2,1)S(1)}, u32[]{:S(2)}, u32[]{:S(2)}) collective-permute-start(bf16[2,256,256]{2,1,0:T(8,128)(2,1)S(1)} %get-tuple-element.29), channel_id=1, source_target_pairs={{0,64},{32,96},{64,0},{96,32},{128,192},{160,224},{192,128},{224,1... | collective-permute-start | bytes 786440 | tf_op jit(solution)/shard_map/ppermute | solution.py:508
  22.7 11.3 %collective-permute-start.1 = (bf16[2,256,256]{2,1,0:T(8,128)(2,1)S(1)}, bf16[2,256,256]{2,1,0:T(8,128)(2,1)S(1)}, u32[]{:S(2)}, u32[]{:S(2)}) collective-permute-start(bf16[2,256,256]{2,1,0:T(8,128)(2,1)S(1)} %get-tuple-element.28), channel_id=1, source_target_pairs={{0,128},{32,160},{64,192},{96,224},{128,0},{160,32},{192,64},{224,... | collective-permute-start | bytes 786440 | tf_op jit(solution)/shard_map/ppermute | solution.py:509
  34.0 24.9 %copy-start = (bf16[512,2048]{1,0:T(8,128)(2,1)S(1)}, bf16[512,2048]{1,0:T(8,128)(2,1)}, u32[]{:S(2)}) copy-start(bf16[512,2048]{1,0:T(8,128)(2,1)} %in_proj_ref.1) | copy-start | bytes 6291460
  34.0 24.9 %copy-start.1 = (s32[1,128]{1,0:T(1,128)S(1)}, s32[1,128]{1,0:T(1,128)}, u32[]{:S(2)}) copy-start(s32[1,128]{1,0:T(1,128)} %slot_ref.1) | copy-start | bytes 1540
  34.0 24.8 %copy-start.2 = (s32[1,128]{1,0:T(1,128)S(1)}, s32[1,128]{1,0:T(1,128)}, u32[]{:S(2)}) copy-start(s32[1,128]{1,0:T(1,128)} %item_ref.1) | copy-start | bytes 1540
  35.8 10.8 %collective-permute-start.3 = (bf16[2,256,256]{2,1,0:T(8,128)(2,1)S(1)}, bf16[2,256,256]{2,1,0:T(8,128)(2,1)S(1)}, u32[]{:S(2)}, u32[]{:S(2)}) collective-permute-start(bf16[2,256,256]{2,1,0:T(8,128)(2,1)S(1)} %get-tuple-element.22), channel_id=1, source_target_pairs={{0,128},{32,160},{64,192},{96,224},{128,0},{160,32},{192,64},{224,... | collective-permute-start | bytes 786440 | tf_op jit(solution)/shard_map/ppermute | solution.py:516
  37.7 8.9 %collective-permute-start.2 = (bf16[2,256,128]{2,1,0:T(8,128)(2,1)S(1)}, bf16[2,256,128]{2,1,0:T(8,128)(2,1)S(1)}, u32[]{:S(2)}, u32[]{:S(2)}) collective-permute-start(bf16[2,256,128]{2,1,0:T(8,128)(2,1)S(1)} %get-tuple-element.20), channel_id=1, source_target_pairs={{0,64},{32,96},{64,0},{96,32},{128,192},{160,224},{192,128},{224,1... | collective-permute-start | bytes 393224 | tf_op jit(solution)/shard_map/ppermute | solution.py:515

commit v3 on v2

--- a/solution.py
+++ b/solution.py
@@ -70,9 +70,8 @@
     out_proj_hbm,
     gain_hbm,
     parts_ref,
-    slope_ref,
-    gate_ref,
-    base_ref,
+    pre_ref,
+    gain_grad_ref,
     inputs_ref,
     saved_ref,
     grad_ref,
@@ -118,12 +117,9 @@
     in_copies[0].wait()
     inputs = inputs_ref[...]
     pre = dot(inputs, in_proj_ref[0], MATMUL)
-    squash = jax.nn.sigmoid(pre)
-    gating = (pre * squash).astype(BF16).astype(F32)
-    gate = (back * (normed * gain) * (squash * (1.0 + pre * (1.0 - squash)))).astype(BF16)
-    gate_ref[...] = gate
-    base_ref[...] = grad.astype(F32) + dot(gate, in_proj_ref[0], MATMUL_NT)
-
+    pre_ref[:, :WIDTH] = pre
+    gating = (pre * jax.nn.sigmoid(pre)).astype(BF16).astype(F32)
+    gain_grad_ref[...] = back * (normed * gain)
     carried = back * gating * gain
     out_attn = inv_std * (
         carried
@@ -138,9 +134,8 @@
     for block, place in ((1, 3), (2, 0), (3, 2)):
         in_copies[block].wait()
         pre = dot(inputs, in_proj_ref[block], MATMUL)
-        squash = jax.nn.sigmoid(pre)
-        slope_ref[:, (block - 1) * WIDTH : block * WIDTH] = squash * (1.0 + pre * (1.0 - squash))
-        hidden = (pre * squash).astype(BF16)
+        pre_ref[:, block * WIDTH : (block + 1) * WIDTH] = pre
+        hidden = (pre * jax.nn.sigmoid(pre)).astype(BF16)
         for head in range(HEADS):
             cols = slice(head * HEAD_DIM, (head + 1) * HEAD_DIM)
             parts_ref[head, :, place * HEAD_DIM : (place + 1) * HEAD_DIM] = hidden[:, cols]
@@ -151,12 +146,11 @@
         project_kernel,
         out_shape=(
             jax.ShapeDtypeStruct((HEADS, TOKENS, 4 * HEAD_DIM), BF16),
-            jax.ShapeDtypeStruct((TOKENS, 3 * WIDTH), F32),
-            jax.ShapeDtypeStruct((TOKENS, WIDTH), BF16),
+            jax.ShapeDtypeStruct((TOKENS, 4 * WIDTH), F32),
             jax.ShapeDtypeStruct((TOKENS, WIDTH), F32),
         ),
         in_specs=[in_smem()] + in_hbm(6),
-        out_specs=tuple(in_vmem(4)),
+        out_specs=tuple(in_vmem(3)),
         scratch_shapes=[
             pltpu.VMEM((TOKENS, WIDTH), BF16),
             pltpu.VMEM((TOKENS, WIDTH), BF16),
@@ -171,12 +165,63 @@
     )(length, *(pltpu.with_memory_space_constraint(array, pltpu.HBM) for array in arrays))
 
 
+def local_kernel(
+    pre_ref, gain_grad_ref, grad_ref, in_proj_ref, item_ref, slope_ref, gate_ref, base_ref, code_ref
+):
+    pre = pre_ref[...]
+    squash = jax.nn.sigmoid(pre)
+    slope = squash * (1.0 + pre * (1.0 - squash))
+    slope_ref[...] = slope[:, WIDTH:]
+    gate = (gain_grad_ref[...] * slope[:, :WIDTH]).astype(BF16)
+    gate_ref[...] = gate
+    base_ref[...] = grad_ref[...].astype(F32) + dot(gate, in_proj_ref[:, :WIDTH], MATMUL_NT)
+    items = item_ref[...]
+    owner_of = (items // (ROWS_DEV * TABLES)).astype(F32)
+    place_of = (items % ROWS_DEV).astype(F32)
+    slot = lax.broadcasted_iota(jnp.int32, (TABLES, TABLES * CAP), 1)
+    owner = lax.broadcasted_iota(jnp.int32, (TABLES, TABLES * CAP), 0)
+    coded = jnp.zeros((TABLES, 128), F32)
+    for level in range(CAP):
+        match = slot == owner * CAP + level
+        for value, lane in ((owner_of, level), (place_of, CAP + level)):
+            column = jnp.sum(jnp.where(match, value, 0.0), axis=1, keepdims=True)
+            coded = jnp.where(slot == lane, column, coded)
+    code_ref[...] = coded
+
+
+def local_terms(pre, gain_grad, grad, in_proj, items):
+    return pl.pallas_call(
+        local_kernel,
+        out_shape=(
+            jax.ShapeDtypeStruct((TOKENS, 3 * WIDTH), F32),
+            jax.ShapeDtypeStruct((TOKENS, WIDTH), BF16),
+            jax.ShapeDtypeStruct((TOKENS, WIDTH), F32),
+            jax.ShapeDtypeStruct((TABLES, 128), F32),
+        ),
+        in_specs=in_vmem(5),
+        out_specs=tuple(in_vmem(4)),
+        compiler_params=params(),
+        cost_estimate=pl.CostEstimate(
+            flops=2 * TOKENS * WIDTH * WIDTH,
+            bytes_accessed=3 << 20,
+            transcendentals=TOKENS * 4 * WIDTH,
+        ),
+        name="local_terms",
+    )(pre, gain_grad, grad, in_proj, items)
+
+
 def tile_grads(query_ref, query_place, key_ref, key_place, key_column, weight, live):
     scale = HEAD_DIM ** (-0.5)
     queries = query_ref[query_place, :, :HEAD_DIM]
     outs = query_ref[query_place, :, HEAD_DIM : 2 * HEAD_DIM]
-    keys = key_ref[key_place, :, key_column : key_column + HEAD_DIM]
-    values = key_ref[key_place, :, key_column + HEAD_DIM : key_column + 2 * HEAD_DIM]
+    if key_place is None:
+        keys, values = (
+            key_ref[:, :, column : column + HEAD_DIM].reshape(2 * TILE, HEAD_DIM)
+            for column in (key_column, key_column + HEAD_DIM)
+        )
+    else:
+        keys = key_ref[key_place, :, key_column : key_column + HEAD_DIM]
+        values = key_ref[key_place, :, key_column + HEAD_DIM : key_column + 2 * HEAD_DIM]
     scores = dot(keys, queries, MATMUL_NT) * scale
     attn_grad = dot(values, outs, MATMUL_NT)
     squash = 0.5 + 0.5 * jnp.tanh(scores * 0.5)
@@ -206,34 +251,36 @@
 def attend_near(length_ref, query_ref, own_ref, flip):
     _, upper = place_of_device()
     weight = weight_of(length_ref)
-    rows = lax.broadcasted_iota(jnp.int32, (TILE, 1), 0) + upper * TILE
+    rows = lax.broadcasted_iota(jnp.int32, (2 * TILE, 1), 0)
+    rows = jnp.where(rows < TILE, -1, rows - TILE + upper * TILE)
     columns = lax.broadcasted_iota(jnp.int32, (1, TILE), 1) + (upper ^ flip) * TILE
     live = rows <= columns
     column = 2 * HEAD_DIM
-    low = tile_grads(query_ref, 0, own_ref, 0, column, weight, live)
-    whole = tile_grads(query_ref, 1, own_ref, 0, column, weight, None)
-    high = tile_grads(query_ref, 1, own_ref, 1, column, weight, live)
-    return low, whole, high
+    low = tile_grads(query_ref, 0, own_ref, 0, column, weight, live[TILE:])
+    high = tile_grads(query_ref, 1, own_ref, None, column, weight, live)
+    return low, high
 
 
 def attend_own_kernel(length_ref, own_ref, query_ref, key_ref):
-    low, whole, high = attend_near(length_ref, own_ref, own_ref, 0)
+    low, high = attend_near(length_ref, own_ref, own_ref, 0)
     query_ref[0] = low[0]
-    query_ref[1] = whole[0] + high[0]
-    key_ref[0, :, :HEAD_DIM] = low[1] + whole[1]
-    key_ref[0, :, HEAD_DIM:] = low[2] + whole[2]
-    key_ref[1, :, :HEAD_DIM] = high[1]
-    key_ref[1, :, HEAD_DIM:] = high[2]
-
-
-def attend_queries_kernel(length_ref, own_ref, query_far_ref, sums_ref, query_ref, key_ref):
-    low, whole, high = attend_near(length_ref, query_far_ref, own_ref, 1)
+    query_ref[1] = high[0]
+    key_ref[0, :, :HEAD_DIM] = low[1] + high[1][:TILE]
+    key_ref[0, :, HEAD_DIM:] = low[2] + high[2][:TILE]
+    key_ref[1, :, :HEAD_DIM] = high[1][TILE:]
+    key_ref[1, :, HEAD_DIM:] = high[2][TILE:]
+
+
+def attend_queries_kernel(
+    length_ref, own_ref, query_far_ref, sums_ref, _, query_ref, key_ref
+):
+    low, high = attend_near(length_ref, query_far_ref, own_ref, 1)
     query_ref[0] = low[0]
-    query_ref[1] = whole[0] + high[0]
-    key_ref[0, :, :HEAD_DIM] = sums_ref[0, :, :HEAD_DIM] + (low[1] + whole[1])
-    key_ref[0, :, HEAD_DIM:] = sums_ref[0, :, HEAD_DIM:] + (low[2] + whole[2])
-    key_ref[1, :, :HEAD_DIM] = sums_ref[1, :, :HEAD_DIM] + high[1]
-    key_ref[1, :, HEAD_DIM:] = sums_ref[1, :, HEAD_DIM:] + high[2]
+    query_ref[1] = high[0]
+    key_ref[0, :, :HEAD_DIM] = sums_ref[0, :, :HEAD_DIM] + (low[1] + high[1][:TILE])
+    key_ref[0, :, HEAD_DIM:] = sums_ref[0, :, HEAD_DIM:] + (low[2] + high[2][:TILE])
+    key_ref[1, :, :HEAD_DIM] = sums_ref[1, :, :HEAD_DIM] + high[1][TILE:]
+    key_ref[1, :, HEAD_DIM:] = sums_ref[1, :, HEAD_DIM:] + high[2][TILE:]
 
 
 def attend_keys_kernel(
@@ -300,16 +347,16 @@
     )(length, own)
 
 
-def attend_queries(length, own, query_far, sums):
+def attend_queries(length, own, query_far, sums, codes):
     return pl.pallas_call(
         attend_queries_kernel,
         out_shape=(QUERY_SUMS, KEY_SUMS),
-        in_specs=[in_smem()] + in_vmem(3),
+        in_specs=[in_smem()] + in_vmem(3) + [pl.BlockSpec(memory_space=pl.ANY)],
         out_specs=tuple(in_vmem(2)),
         compiler_params=params(),
         cost_estimate=attend_cost(3),
         name="attend_queries",
-    )(length, own, query_far, sums)
+    )(length, own, query_far, sums, codes)
 
 
 def attend_keys(length, own, query_far, key_far, near_own, near_far):
@@ -362,7 +409,7 @@
     base_ref,
     in_proj_ref,
     slot_ref,
-    item_ref,
+    code_ref,
     proj_ref,
     rows_ref,
     wide_ref,
@@ -392,28 +439,17 @@
             wide_ref[pl.ds(level * 4 + chunk, TABLES, stride=SEND_ROWS), :] = summed[
                 level * TABLES : (level + 1) * TABLES, chunk * 128 : (chunk + 1) * 128
             ]
-    items = item_ref[...]
-    owner_of = (items // (ROWS_DEV * TABLES)).astype(F32)
-    place_of = (items % ROWS_DEV).astype(F32)
-    slot = lax.broadcasted_iota(jnp.int32, (TABLES, TABLES * CAP), 1)
-    owner = lax.broadcasted_iota(jnp.int32, (TABLES, TABLES * CAP), 0)
-    coded = jnp.zeros((TABLES, 128), F32)
-    for level in range(CAP):
-        match = slot == owner * CAP + level
-        for value, lane in ((owner_of, level), (place_of, CAP + level)):
-            column = jnp.sum(jnp.where(match, value, 0.0), axis=1, keepdims=True)
-            coded = jnp.where(slot == lane, column, coded)
-    wide_ref[pl.ds(SUM_ROWS, TABLES, stride=SEND_ROWS), :] = coded
+    wide_ref[pl.ds(SUM_ROWS, TABLES, stride=SEND_ROWS), :] = code_ref[...]
     for row in range(SUM_ROWS + 1, SEND_ROWS):
         wide_ref[pl.ds(row, TABLES, stride=SEND_ROWS), :] = jnp.zeros((TABLES, 128), F32)
     rows_ref[...] = wide_ref[...].astype(BF16)
 
 
-def finish(grads, slope, gate, base, in_proj, slots, items):
+def finish(grads, slope, gate, base, in_proj, slots, codes):
     return pl.pallas_call(
         finish_kernel,
         out_shape=(
-            jax.ShapeDtypeStruct((TOKENS, 4 * WIDTH), BF16),
+            pltpu.VMEM((TOKENS, 4 * WIDTH), BF16),
             jax.ShapeDtypeStruct((TABLES * SEND_ROWS, 128), BF16),
         ),
         in_specs=in_vmem(7),
@@ -421,7 +457,7 @@
         scratch_shapes=[pltpu.VMEM((TABLES * SEND_ROWS, 128), F32)],
         compiler_params=params(),
         name="finish",
-    )(grads, slope, gate, base, in_proj, slots, items)
+    )(grads, slope, gate, base, in_proj, slots, codes)
 
 
 def compact_kernel(rows_ref, out_ref, wide_ref, packed_ref):
@@ -436,13 +472,15 @@
     spaced = jnp.where(lane // TABLES == x, jnp.concatenate([coded] * X_COUNT, axis=1), 0.0)
     packed_ref[GIVE_SUMS : GIVE_SUMS + 2 * CAP, :] = spaced
     packed_ref[GIVE_SUMS + 2 * CAP :, :] = jnp.zeros((GIVE_ROWS - GIVE_SUMS - 2 * CAP, 128), F32)
-    out_ref[...] = packed_ref[...].astype(BF16)
+    packed = packed_ref[...].astype(BF16)
+    for x_to in range(X_COUNT):
+        out_ref[x_to] = packed
 
 
 def compact_rows(rows):
     return pl.pallas_call(
         compact_kernel,
-        out_shape=jax.ShapeDtypeStruct((GIVE_ROWS, 128), BF16),
+        out_shape=jax.ShapeDtypeStruct((X_COUNT, GIVE_ROWS, 128), BF16),
         in_specs=in_vmem(1),
         out_specs=in_vmem(1)[0],
         scratch_shapes=[
@@ -454,7 +492,9 @@
     )(rows)
 
 
-def scatter_kernel(rows_ref, out_ref, wide_ref):
+def scatter_kernel(rows_ref, proj_ref, out_ref, proj_out, wide_ref, sem):
+    copy = pltpu.make_async_copy(proj_ref, proj_out, sem)
+    copy.start()
     targets = Y_COUNT * ROWS_DEV
     first = lax.div(lax.axis_index("ctx"), Y_COUNT) * targets
     wide_ref[...] = rows_ref[...].astype(F32)
@@ -475,18 +515,25 @@
             part = dot(hots[level], rows, MATMUL)
             total = part if total is None else total + part
         out_ref[:, chunk * 128 : (chunk + 1) * 128] = total.astype(BF16)
-
-
-def scatter_rows(rows):
+    copy.wait()
+
+
+def scatter_rows(rows, proj):
     return pl.pallas_call(
         scatter_kernel,
-        out_shape=jax.ShapeDtypeStruct((Y_COUNT * ROWS_DEV, WIDTH), BF16),
-        in_specs=in_vmem(1),
-        out_specs=in_vmem(1)[0],
-        scratch_shapes=[pltpu.VMEM((X_COUNT, GIVE_ROWS, 128), F32)],
+        out_shape=(
+            jax.ShapeDtypeStruct((Y_COUNT * ROWS_DEV, WIDTH), BF16),
+            jax.ShapeDtypeStruct((TOKENS, 4 * WIDTH), BF16),
+        ),
+        in_specs=in_vmem(2),
+        out_specs=tuple(in_vmem(1) + in_hbm(1)),
+        scratch_shapes=[
+            pltpu.VMEM((X_COUNT, GIVE_ROWS, 128), F32),
+            pltpu.SemaphoreType.DMA(()),
+        ],
         compiler_params=params(),
         name="scatter_rows",
-    )(rows)
+    )(rows, proj)
 
 
 def per_device(
@@ -500,7 +547,7 @@
     out_proj,
     norm_gain,
 ):
-    parts, slope, gate, base = project(
+    parts, pre, gain_grad = project(
         seq_lengths, item_inputs[0], attn_saved[0], out_grad[0], in_proj, out_proj, norm_gain[None]
     )
     own = lax.all_to_all(parts, "ctx", 0, 0, axis_index_groups=HEAD_GROUPS)
@@ -508,7 +555,8 @@
     query_far = lax.ppermute(own[:, :, : 2 * HEAD_DIM], "ctx", SWAP_QUERY)
     key_far = lax.ppermute(own[:, :, 2 * HEAD_DIM :], "ctx", SWAP_KEY)
     near_own, sums = attend_own(seq_lengths, own)
-    near_far, key_own = attend_queries(seq_lengths, own, query_far, sums)
+    slope, gate, base, codes = local_terms(pre, gain_grad, out_grad[0], in_proj, slot_rows)
+    near_far, key_own = attend_queries(seq_lengths, own, query_far, sums, codes)
     query_own, query_send, key_send = attend_keys(
         seq_lengths, own, query_far, key_far, near_own, near_far
     )
@@ -518,11 +566,11 @@
     grads = lax.all_to_all(
         joined.reshape(HEADS, TOKENS, 3 * HEAD_DIM), "ctx", 0, 0, axis_index_groups=HEAD_GROUPS
     )
-    proj_grad, rows = finish(grads, slope, gate, base, in_proj, token_slot, slot_rows)
+    proj_grad, rows = finish(grads, slope, gate, base, in_proj, token_slot, codes)
     rows = lax.all_to_all(rows.reshape(TABLES, SEND_ROWS, 128), "table", 0, 0)
     rows = compact_rows(rows.reshape(TABLES * SEND_ROWS, 128))
-    rows = lax.all_gather(rows, "ctx", axis_index_groups=X_GROUPS)
-    dense = scatter_rows(rows)
+    rows = lax.all_to_all(rows, "ctx", 0, 0, axis_index_groups=X_GROUPS)
+    dense, proj_grad = scatter_rows(rows, proj_grad)
     pieces = lax.all_to_all(
         dense.reshape(Y_COUNT, ROWS_DEV, WIDTH), "ctx", 0, 0, axis_index_groups=Y_GROUPS
     )

time: 116 us -> 114 us (0.983)
  blocking collectives: 81.2 us -> 79.7 us
    all_gather x1 -> x0, blocking collectives: 13.4 us -> none  [per_device(): rows = lax.all_gather(rows, 'ctx', axis_index_groups=X_GROUPS)]
    all_to_all x0 -> x1, blocking collectives: none -> 11.8 us  [per_device(): rows = lax.all_to_all(rows, 'ctx', 0, 0, axis_index_groups=X_GROUPS)]
    pallas_call x3 -> x4, Pallas kernels: 2.31 us -> 2.46 us  [the longest x1 0.9 us: finish(): pl.pallas_call(finish_kernel, out_shape=(pltpu.VMEM((TOKENS, 4 * WIDTH),...]
  transfers between devices with their start and end apart: 4 -> 4, of which waited for: 2 -> 2; matrix products, arithmetic and copies ran while one was open for 0% -> 0% of each run, Pallas kernels for 2% -> 3%
where the time goes in v3:
time: 114 us; the launch traced here: 113 us
  blocking collectives  79.7 us (70%)
  starting transfers between devices  12.1 us (11%)
  waiting for transfers between devices  9.86 us (9%)
  Pallas kernels  9.43 us (8%)
  between operations  1.43 us (1%)
    all_to_all x1, blocking collectives, per_device(): rows = lax.all_to_all(rows.reshape(TABLES, SEND_ROWS, 128), 'table', 0, 0)  31 us
    all_to_all x1, blocking collectives, per_device(): own = lax.all_to_all(parts, 'ctx', 0, 0, axis_index_groups=HEAD_GROUPS)  15.5 us
    all_to_all x1, blocking collectives, per_device(): lax.all_to_all(joined.reshape(HEADS, TOKENS, 3 * HEAD_DIM), 'ctx', 0, 0,...  12.2 us
    all_to_all x1, blocking collectives, per_device(): rows = lax.all_to_all(rows, 'ctx', 0, 0, axis_index_groups=X_GROUPS)  11.8 us
    all_to_all x1, blocking collectives, per_device(): lax.all_to_all(dense.reshape(Y_COUNT, ROWS_DEV, WIDTH), 'ctx', 0, 0, axis...  9.31 us
    ppermute x1, waiting for transfers between devices, per_device(): query_far = lax.ppermute(own[:, :, :2 * HEAD_DIM], 'ctx', SWAP_QUERY)  6.3 us
    ppermute x1, starting transfers between devices, per_device(): query_got = lax.ppermute(query_send, 'ctx', SWAP_QUERY)  5.29 us
    ppermute x1, waiting for transfers between devices, per_device(): query_got = lax.ppermute(query_send, 'ctx', SWAP_QUERY)  3.56 us
  transfers between devices with their start and end apart: 4, of which 2 were waited for; matrix products, arithmetic and copies ran while one was open for 0% of the time, Pallas kernels for 3%

profile of v3, /device:TPU:8, one launch (start us, length us, event | category | flops | bytes accessed | tf_op | source)
XLA Modules:
  0.0 113.2 jit_solution(16159027690436570210)
XLA Ops:
  1.3 0.0 copy-start
  1.3 0.0 copy-start.1
  1.3 0.0 copy-start.2
  1.3 2.8 %project.1 = (bf16[4,128,512]{2,1,0:T(8,128)(2,1)S(1)}, f32[128,2048]{1,0:T(8,128)S(1)}, f32[128,512]{1,0:T(8,128)S(1)}) custom-call(s32[1]{0:T(128)S(6)} %copy.11.length_ref, bf16[128,512]{1,0:T(8,128)(2,1)} %bitcast.20, bf16[128,512]{1,0:T(8,128)(2,1)} %bitcast.21, bf16[128,512]{1,0:T(8,128)(2,1)} %bitcast.16, bf16[512,2048]{1,0:T(8,128)(2,1)} %in_proj_ref.3, ...), custom_call_target="tpu_custom_call" | custom-call | tf_op jit(solution)/shard_map/project/pallas_call | solution.py:145
  4.2 15.5 %all_to_all.25 = bf16[4,128,512]{2,1,0:T(8,128)(2,1)S(1)} all-to-all(bf16[4,128,512]{2,1,0:T(8,128)(2,1)S(1)} %get-tuple-element.20), channel_id=1, replica_groups={{0,32,384,416},{64,96,448,480},{128,160,256,288},{192,224,320,352},{1,3..., dimensions={0} | all-to-all | bytes 1048576 | tf_op jit(solution)/shard_map/all_to_all | solution.py:553
  19.7 3.0 %collective-permute-start = (bf16[2,256,256]{2,1,0:T(8,128)(2,1)S(1)}, bf16[2,256,256]{2,1,0:T(8,128)(2,1)S(1)}, u32[]{:S(2)}, u32[]{:S(2)}) collective-permute-start(bf16[2,256,256]{2,1,0:T(8,128)(2,1)S(1)} %get-tuple-element.39), channel_id=1, source_target_pairs={{0,64},{32,96},{64,0},{96,32},{128,192},{160,224},{192,128},{224,1... | collective-permute-start | bytes 786440 | tf_op jit(solution)/shard_map/ppermute | solution.py:555
  22.6 1.9 %collective-permute-start.1 = (bf16[2,256,256]{2,1,0:T(8,128)(2,1)S(1)}, bf16[2,256,256]{2,1,0:T(8,128)(2,1)S(1)}, u32[]{:S(2)}, u32[]{:S(2)}) collective-permute-start(bf16[2,256,256]{2,1,0:T(8,128)(2,1)S(1)} %get-tuple-element.38), channel_id=1, source_target_pairs={{0,128},{32,160},{64,192},{96,224},{128,0},{160,32},{192,64},{224,... | collective-permute-start | bytes 786440 | tf_op jit(solution)/shard_map/ppermute | solution.py:556
  24.5 0.0 copy-done
  24.6 0.0 copy-done.1
  24.6 0.0 copy-done.2
  24.6 0.6 local_terms.1
  25.2 1.1 %attend_own.1 = (f32[2,256,128]{2,1,0:T(8,128)S(1)}, f32[2,256,256]{2,1,0:T(8,128)S(1)}) custom-call(s32[1]{0:T(128)S(6)} %copy.11.length_ref, bf16[2,256,512]{2,1,0:T(8,128)(2,1)S(1)} %bitcast.11), custom_call_target="tpu_custom_call" | custom-call | flops 251658240 | bytes 2097152 | tf_op jit(solution)/shard_map/attend_own/pallas_call | solution.py:339
  26.3 6.3 %collective-permute-done.query_far_ref = bf16[2,256,256]{2,1,0:T(8,128)(2,1)S(1)} collective-permute-done((bf16[2,256,256]{2,1,0:T(8,128)(2,1)S(1)}, bf16[2,256,256]{2,1,0:T(8,128)(2,1)S(1)}, u32[]{:S(2)}, u32[]{:S(2)}) %collective-permute-start) | collective-permute-done | bytes 262176 | tf_op jit(solution)/shard_map/ppermute | solution.py:555
  32.6 1.1 attend_queries.1
  33.7 0.0 copy-start.3
  33.7 0.0 collective-permute-done.1.key_far_ref
  33.7 1.8 %attend_keys.1 = (f32[2,256,128]{2,1,0:T(8,128)S(1)}, bf16[2,256,128]{2,1,0:T(8,128)(2,1)S(1)}, bf16[2,256,256]{2,1,0:T(8,128)(2,1)S(1)}) custom-call(s32[1]{0:T(128)S(6)} %copy.11.length_ref, bf16[2,256,512]{2,1,0:T(8,128)(2,1)S(1)} %bitcast.13, bf16[2,256,256]{2,1,0:T(8,128)(2,1)S(1)} %collective-permute-done.query_far_ref, ...), custom_call_target="tpu_custom_call" | custom-call | flops 335544320 | bytes 2097152 | tf_op jit(solution)/shard_map/attend_keys/pallas_call | solution.py:363
  35.5 1.9 %collective-permute-start.3 = (bf16[2,256,256]{2,1,0:T(8,128)(2,1)S(1)}, bf16[2,256,256]{2,1,0:T(8,128)(2,1)S(1)}, u32[]{:S(2)}, u32[]{:S(2)}) collective-permute-start(bf16[2,256,256]{2,1,0:T(8,128)(2,1)S(1)} %get-tuple-element.30), channel_id=1, source_target_pairs={{0,128},{32,160},{64,192},{96,224},{128,0},{160,32},{192,64},{224,... | collective-permute-start | bytes 786440 | tf_op jit(solution)/shard_map/ppermute | solution.py:564
  37.5 5.3 %collective-permute-start.2 = (bf16[2,256,128]{2,1,0:T(8,128)(2,1)S(1)}, bf16[2,256,128]{2,1,0:T(8,128)(2,1)S(1)}, u32[]{:S(2)}, u32[]{:S(2)}) collective-permute-start(bf16[2,256,128]{2,1,0:T(8,128)(2,1)S(1)} %get-tuple-element.28), channel_id=1, source_target_pairs={{0,64},{32,96},{64,0},{96,32},{128,192},{160,224},{192,128},{224,1... | collective-permute-start | bytes 393224 | tf_op jit(solution)/shard_map/ppermute | solution.py:563
  42.8 3.6 %collective-permute-done.2.query_got_ref = bf16[2,256,128]{2,1,0:T(8,128)(2,1)S(1)} collective-permute-done((bf16[2,256,128]{2,1,0:T(8,128)(2,1)S(1)}, bf16[2,256,128]{2,1,0:T(8,128)(2,1)S(1)}, u32[]{:S(2)}, u32[]{:S(2)}) %collective-permute-start.2) | collective-permute-done | bytes 131104 | tf_op jit(solution)/shard_map/ppermute | solution.py:563
  46.3 0.0 collective-permute-done.3.key_got_ref
  46.3 0.1 join_parts.1
  46.4 12.2 %all_to_all.26.grads_ref = bf16[4,128,384]{2,1,0:T(8,128)(2,1)S(1)} all-to-all(bf16[4,128,384]{2,1,0:T(8,128)(2,1)S(1)} %bitcast.14), channel_id=1, replica_groups={{0,32,384,416},{64,96,448,480},{128,160,256,288},{192,224,320,352},{1,3..., dimensions={0} | all-to-all | bytes 786432 | tf_op jit(solution)/shard_map/all_to_all | solution.py:566
  58.6 0.0 copy-done.3
  58.6 0.9 finish.1
  59.5 31.0 %all_to_all.27 = bf16[32,24,128]{2,1,0:T(8,128)(2,1)S(1)} all-to-all(bf16[32,24,128]{2,1,0:T(8,128)(2,1)S(1)} %bitcast.19), channel_id=1, replica_groups=mesh['ctx'=16,'table'=32] {'table'}, dimensions={0} | all-to-all | bytes 393216 | tf_op jit(solution)/shard_map/all_to_all | solution.py:570
  90.4 0.2 compact_rows.1
  90.6 11.8 %all_to_all.28.rows_ref = bf16[4,528,128]{2,1,0:T(8,128)(2,1)S(1)} all-to-all(bf16[4,528,128]{2,1,0:T(8,128)(2,1)S(1)} %compact_rows.1), channel_id=1, replica_groups={{0,128,256,384},{32,160,288,416},{64,192,320,448},{96,224,352,480},{1,1..., dimensions={0} | all-to-all | bytes 1081344 | tf_op jit(solution)/shard_map/all_to_all | solution.py:572
  102.4 0.8 scatter_rows.1
  103.2 9.3 %all_to_all.29 = bf16[4,64,512]{2,1,0:T(8,128)(2,1)S(1)} all-to-all(bf16[4,64,512]{2,1,0:T(8,128)(2,1)S(1)} %bitcast.18), channel_id=1, replica_groups={{0,32,64,96},{128,160,192,224},{256,288,320,352},{384,416,448,480},{1,3..., dimensions={0} | all-to-all | bytes 524288 | tf_op jit(solution)/shard_map/all_to_all | solution.py:574
  112.5 0.7 convert_reduce_fusion
  (1 shorter events, 0.0 us)
Async XLA Ops:
  1.3 23.3 %copy-start = (bf16[512,2048]{1,0:T(8,128)(2,1)S(1)}, bf16[512,2048]{1,0:T(8,128)(2,1)}, u32[]{:S(2)}) copy-start(bf16[512,2048]{1,0:T(8,128)(2,1)} %in_proj_ref.3) | copy-start | bytes 6291460
  1.3 23.3 %copy-start.1 = (bf16[1,128,512]{2,1,0:T(8,128)(2,1)S(1)}, bf16[1,128,512]{2,1,0:T(8,128)(2,1)}, u32[]{:S(2)}) copy-start(bf16[1,128,512]{2,1,0:T(8,128)(2,1)} %param.11) | copy-start | bytes 393220
  1.3 23.3 %copy-start.2 = (s32[1,128]{1,0:T(1,128)S(1)}, s32[1,128]{1,0:T(1,128)}, u32[]{:S(2)}) copy-start(s32[1,128]{1,0:T(1,128)} %item_ref.1) | copy-start | bytes 1540
  19.7 12.9 %collective-permute-start = (bf16[2,256,256]{2,1,0:T(8,128)(2,1)S(1)}, bf16[2,256,256]{2,1,0:T(8,128)(2,1)S(1)}, u32[]{:S(2)}, u32[]{:S(2)}) collective-permute-start(bf16[2,256,256]{2,1,0:T(8,128)(2,1)S(1)} %get-tuple-element.39), channel_id=1, source_target_pairs={{0,64},{32,96},{64,0},{96,32},{128,192},{160,224},{192,128},{224,1... | collective-permute-start | bytes 786440 | tf_op jit(solution)/shard_map/ppermute | solution.py:555
  22.6 11.1 %collective-permute-start.1 = (bf16[2,256,256]{2,1,0:T(8,128)(2,1)S(1)}, bf16[2,256,256]{2,1,0:T(8,128)(2,1)S(1)}, u32[]{:S(2)}, u32[]{:S(2)}) collective-permute-start(bf16[2,256,256]{2,1,0:T(8,128)(2,1)S(1)} %get-tuple-element.38), channel_id=1, source_target_pairs={{0,128},{32,160},{64,192},{96,224},{128,0},{160,32},{192,64},{224,... | collective-permute-start | bytes 786440 | tf_op jit(solution)/shard_map/ppermute | solution.py:556
  33.7 24.8 %copy-start.3 = (s32[1,128]{1,0:T(1,128)S(1)}, s32[1,128]{1,0:T(1,128)}, u32[]{:S(2)}) copy-start(s32[1,128]{1,0:T(1,128)} %slot_ref.1) | copy-start | bytes 1540
  35.5 10.8 %collective-permute-start.3 = (bf16[2,256,256]{2,1,0:T(8,128)(2,1)S(1)}, bf16[2,256,256]{2,1,0:T(8,128)(2,1)S(1)}, u32[]{:S(2)}, u32[]{:S(2)}) collective-permute-start(bf16[2,256,256]{2,1,0:T(8,128)(2,1)S(1)} %get-tuple-element.30), channel_id=1, source_target_pairs={{0,128},{32,160},{64,192},{96,224},{128,0},{160,32},{192,64},{224,... | collective-permute-start | bytes 786440 | tf_op jit(solution)/shard_map/ppermute | solution.py:564
  37.5 8.9 %collective-permute-start.2 = (bf16[2,256,128]{2,1,0:T(8,128)(2,1)S(1)}, bf16[2,256,128]{2,1,0:T(8,128)(2,1)S(1)}, u32[]{:S(2)}, u32[]{:S(2)}) collective-permute-start(bf16[2,256,128]{2,1,0:T(8,128)(2,1)S(1)} %get-tuple-element.28), channel_id=1, source_target_pairs={{0,64},{32,96},{64,0},{96,32},{128,192},{160,224},{192,128},{224,1... | collective-permute-start | bytes 393224 | tf_op jit(solution)/shard_map/ppermute | solution.py:563

commit v4 on v3

--- a/solution.py
+++ b/solution.py
@@ -14,12 +14,16 @@
 ROWS_DEV = 64
 TABLES = 32
 CAP = 4
-SUM_ROWS = CAP * WIDTH // 128
-SEND_ROWS = SUM_ROWS + 8
-GIVE_SUMS = TABLES * SUM_ROWS
-GIVE_ROWS = GIVE_SUMS + 16
+CORES = 2
+FARS = TABLES // CORES
+QUARTER = 128
+HALF_SLOTS = FARS * CAP
+NEAR_ROWS = HALF_SLOTS + 8
+FAR_SUMS = 4 * CORES * CAP
+FAR_ROWS = FAR_SUMS + 8
 X_COUNT = 4
 Y_COUNT = 4
+CTX_COUNT = X_COUNT * Y_COUNT
 TILE = 2 * TOKENS
 VMEM_LIMIT = 48 * 1024 * 1024
 BF16 = jnp.bfloat16
@@ -31,8 +35,16 @@
     for pair in range(2)
     for upper in range(2)
 ]
-X_GROUPS = [[x * Y_COUNT + y for x in range(X_COUNT)] for y in range(Y_COUNT)]
-Y_GROUPS = [[x * Y_COUNT + y for y in range(Y_COUNT)] for x in range(X_COUNT)]
+X_CORE_GROUPS = [
+    [
+        (x * Y_COUNT + y) * TABLES + far * CORES + core
+        for x in range(X_COUNT)
+        for core in range(CORES)
+    ]
+    for y in range(Y_COUNT)
+    for far in range(FARS)
+]
+FAR_GROUPS = [[far * CORES + core for far in range(FARS)] for core in range(CORES)]
 SWAP_QUERY = [(c, c ^ 2) for c in range(X_COUNT * Y_COUNT)]
 SWAP_KEY = [(c, c ^ Y_COUNT) for c in range(X_COUNT * Y_COUNT)]
 
@@ -178,15 +190,22 @@
     items = item_ref[...]
     owner_of = (items // (ROWS_DEV * TABLES)).astype(F32)
     place_of = (items % ROWS_DEV).astype(F32)
-    slot = lax.broadcasted_iota(jnp.int32, (TABLES, TABLES * CAP), 1)
-    owner = lax.broadcasted_iota(jnp.int32, (TABLES, TABLES * CAP), 0)
-    coded = jnp.zeros((TABLES, 128), F32)
-    for level in range(CAP):
-        match = slot == owner * CAP + level
-        for value, lane in ((owner_of, level), (place_of, CAP + level)):
-            column = jnp.sum(jnp.where(match, value, 0.0), axis=1, keepdims=True)
-            coded = jnp.where(slot == lane, column, coded)
-    code_ref[...] = coded
+    slot = lax.broadcasted_iota(jnp.int32, (TABLES * CAP, 128), 0)
+    lane = lax.broadcasted_iota(jnp.int32, (TABLES * CAP, 128), 1)
+    wanted = lane % HALF_SLOTS
+    wanted = (wanted % FARS) * (CORES * CAP) + wanted // FARS
+    for core in range(CORES):
+        match = slot == wanted + core * CAP
+        row = sum(
+            dot(
+                jnp.broadcast_to(values, (8, 128)).astype(BF16),
+                (match & (lane // HALF_SLOTS == part)).astype(F32).astype(BF16),
+                MATMUL,
+            )
+            for part, values in enumerate((owner_of, place_of))
+        )
+        first = lax.broadcasted_iota(jnp.int32, (8, 128), 0) == 0
+        code_ref[core] = jnp.where(first, row, 0.0)
 
 
 def local_terms(pre, gain_grad, grad, in_proj, items):
@@ -196,7 +215,7 @@
             jax.ShapeDtypeStruct((TOKENS, 3 * WIDTH), F32),
             jax.ShapeDtypeStruct((TOKENS, WIDTH), BF16),
             jax.ShapeDtypeStruct((TOKENS, WIDTH), F32),
-            jax.ShapeDtypeStruct((TABLES, 128), F32),
+            jax.ShapeDtypeStruct((CORES, 8, 128), F32),
         ),
         in_specs=in_vmem(5),
         out_specs=tuple(in_vmem(4)),
@@ -431,17 +450,17 @@
     high = input_grad.astype(BF16)
     low = (input_grad - high.astype(F32)).astype(BF16)
     order = lax.broadcasted_iota(jnp.int32, (TABLES * CAP, 1), 0)
-    slot_of = (order % TABLES) * CAP + order // TABLES
+    within = order % HALF_SLOTS
+    slot_of = ((within % FARS) * CORES + order // HALF_SLOTS) * CAP + within // FARS
     picks = (slot_ref[...] == slot_of).astype(F32).astype(BF16)
     summed = dot(picks, high, MATMUL) + dot(picks, low, MATMUL)
-    for level in range(CAP):
-        for chunk in range(WIDTH // 128):
-            wide_ref[pl.ds(level * 4 + chunk, TABLES, stride=SEND_ROWS), :] = summed[
-                level * TABLES : (level + 1) * TABLES, chunk * 128 : (chunk + 1) * 128
+    for x in range(X_COUNT):
+        for core in range(CORES):
+            target = x * CORES + core
+            wide_ref[target, :HALF_SLOTS] = summed[
+                core * HALF_SLOTS : (core + 1) * HALF_SLOTS, x * QUARTER : (x + 1) * QUARTER
             ]
-    wide_ref[pl.ds(SUM_ROWS, TABLES, stride=SEND_ROWS), :] = code_ref[...]
-    for row in range(SUM_ROWS + 1, SEND_ROWS):
-        wide_ref[pl.ds(row, TABLES, stride=SEND_ROWS), :] = jnp.zeros((TABLES, 128), F32)
+            wide_ref[target, HALF_SLOTS:] = code_ref[core]
     rows_ref[...] = wide_ref[...].astype(BF16)
 
 
@@ -450,71 +469,76 @@
         finish_kernel,
         out_shape=(
             pltpu.VMEM((TOKENS, 4 * WIDTH), BF16),
-            jax.ShapeDtypeStruct((TABLES * SEND_ROWS, 128), BF16),
+            jax.ShapeDtypeStruct((X_COUNT * CORES, NEAR_ROWS, QUARTER), BF16),
         ),
         in_specs=in_vmem(7),
         out_specs=tuple(in_vmem(2)),
-        scratch_shapes=[pltpu.VMEM((TABLES * SEND_ROWS, 128), F32)],
+        scratch_shapes=[pltpu.VMEM((X_COUNT * CORES, NEAR_ROWS, QUARTER), F32)],
         compiler_params=params(),
         name="finish",
     )(grads, slope, gate, base, in_proj, slots, codes)
 
 
-def compact_kernel(rows_ref, out_ref, wide_ref, packed_ref):
-    x = lax.div(lax.axis_index("ctx"), Y_COUNT)
+def arrange_kernel(rows_ref, out_ref, wide_ref, packed_ref):
+    givers = X_COUNT * CORES
     wide_ref[...] = rows_ref[...].astype(F32)
-    for owner in range(TABLES):
-        packed_ref[owner * SUM_ROWS : (owner + 1) * SUM_ROWS, :] = wide_ref[
-            owner * SEND_ROWS : owner * SEND_ROWS + SUM_ROWS, :
-        ]
-    coded = wide_ref[pl.ds(SUM_ROWS, TABLES, stride=SEND_ROWS), :].T[: 2 * CAP]
-    lane = lax.broadcasted_iota(jnp.int32, (2 * CAP, 128), 1)
-    spaced = jnp.where(lane // TABLES == x, jnp.concatenate([coded] * X_COUNT, axis=1), 0.0)
-    packed_ref[GIVE_SUMS : GIVE_SUMS + 2 * CAP, :] = spaced
-    packed_ref[GIVE_SUMS + 2 * CAP :, :] = jnp.zeros((GIVE_ROWS - GIVE_SUMS - 2 * CAP, 128), F32)
-    packed = packed_ref[...].astype(BF16)
-    for x_to in range(X_COUNT):
-        out_ref[x_to] = packed
-
-
-def compact_rows(rows):
-    return pl.pallas_call(
-        compact_kernel,
-        out_shape=jax.ShapeDtypeStruct((X_COUNT, GIVE_ROWS, 128), BF16),
+    for giver in range(givers):
+        for level in range(CAP):
+            packed_ref[pl.ds(giver * CAP + level, FARS, stride=FAR_ROWS), :] = wide_ref[
+                giver, level * FARS : (level + 1) * FARS
+            ]
+    own = lax.rem(lax.div(lax.axis_index("table"), CORES), 4)
+    coded = jnp.concatenate(
+        [wide_ref[giver, HALF_SLOTS : HALF_SLOTS + 1] for giver in range(givers)], axis=0
+    ).T
+    giver = lax.broadcasted_iota(jnp.int32, (givers, 128), 0)
+    lane = lax.broadcasted_iota(jnp.int32, (givers, 128), 1)
+    for part in range(2):
+        row = sum(
+            dot(
+                coded[
+                    part * HALF_SLOTS + level * FARS : part * HALF_SLOTS + (level + 1) * FARS
+                ].astype(BF16),
+                (lane == own * FAR_SUMS + giver * CAP + level).astype(F32).astype(BF16),
+                MATMUL,
+            )
+            for level in range(CAP)
+        )
+        packed_ref[pl.ds(FAR_SUMS + part, FARS, stride=FAR_ROWS), :] = row
+    for row in range(FAR_SUMS + 2, FAR_ROWS):
+        packed_ref[pl.ds(row, FARS, stride=FAR_ROWS), :] = jnp.zeros((FARS, 128), F32)
+    out_ref[...] = packed_ref[...].astype(BF16)
+
+
+def arrange_rows(rows):
+    return pl.pallas_call(
+        arrange_kernel,
+        out_shape=jax.ShapeDtypeStruct((FARS * FAR_ROWS, QUARTER), BF16),
         in_specs=in_vmem(1),
         out_specs=in_vmem(1)[0],
         scratch_shapes=[
-            pltpu.VMEM((TABLES * SEND_ROWS, 128), F32),
-            pltpu.VMEM((GIVE_ROWS, 128), F32),
+            pltpu.VMEM((X_COUNT * CORES, NEAR_ROWS, QUARTER), F32),
+            pltpu.VMEM((FARS * FAR_ROWS, QUARTER), F32),
         ],
         compiler_params=params(),
-        name="compact_rows",
+        name="arrange_rows",
     )(rows)
 
 
 def scatter_kernel(rows_ref, proj_ref, out_ref, proj_out, wide_ref, sem):
     copy = pltpu.make_async_copy(proj_ref, proj_out, sem)
     copy.start()
-    targets = Y_COUNT * ROWS_DEV
-    first = lax.div(lax.axis_index("ctx"), Y_COUNT) * targets
+    targets = CTX_COUNT * ROWS_DEV
     wide_ref[...] = rows_ref[...].astype(F32)
-    coded = sum(wide_ref[x, GIVE_SUMS : GIVE_SUMS + 2 * CAP, :] for x in range(X_COUNT))
-    ids = (coded[:CAP] * ROWS_DEV + coded[CAP:]).astype(jnp.int32)
-    target = first + lax.broadcasted_iota(jnp.int32, (targets, 1), 0)
-    hots = [(ids[level : level + 1, :] == target).astype(F32).astype(BF16) for level in range(CAP)]
-    for chunk in range(WIDTH // 128):
-        total = None
-        for level in range(CAP):
-            rows = jnp.concatenate(
-                [
-                    wide_ref[x, pl.ds(level * 4 + chunk, TABLES, stride=SUM_ROWS), :]
-                    for x in range(X_COUNT)
-                ],
-                axis=0,
-            ).astype(BF16)
-            part = dot(hots[level], rows, MATMUL)
-            total = part if total is None else total + part
-        out_ref[:, chunk * 128 : (chunk + 1) * 128] = total.astype(BF16)
+    rows = wide_ref[:, :FAR_SUMS].reshape(FARS * FAR_SUMS, QUARTER).astype(BF16)
+    ids = []
+    for first in range(0, FARS, 4):
+        coded = sum(wide_ref[far, FAR_SUMS : FAR_SUMS + 8] for far in range(first, first + 4))
+        ids.append(coded[:1] * ROWS_DEV + coded[1:2])
+    ids = jnp.concatenate(ids, axis=1).astype(jnp.int32)
+    target = lax.broadcasted_iota(jnp.int32, (targets, 1), 0)
+    hots = (ids == target).astype(F32).astype(BF16)
+    out_ref[...] = dot(hots, rows, MATMUL).astype(BF16)
     copy.wait()
 
 
@@ -522,18 +546,36 @@
     return pl.pallas_call(
         scatter_kernel,
         out_shape=(
-            jax.ShapeDtypeStruct((Y_COUNT * ROWS_DEV, WIDTH), BF16),
+            jax.ShapeDtypeStruct((CTX_COUNT * ROWS_DEV, QUARTER), BF16),
             jax.ShapeDtypeStruct((TOKENS, 4 * WIDTH), BF16),
         ),
         in_specs=in_vmem(2),
         out_specs=tuple(in_vmem(1) + in_hbm(1)),
         scratch_shapes=[
-            pltpu.VMEM((X_COUNT, GIVE_ROWS, 128), F32),
+            pltpu.VMEM((FARS, FAR_ROWS, QUARTER), F32),
             pltpu.SemaphoreType.DMA(()),
         ],
         compiler_params=params(),
         name="scatter_rows",
     )(rows, proj)
+
+
+def total_kernel(pieces_ref, out_ref):
+    for x in range(X_COUNT):
+        out_ref[:, x * QUARTER : (x + 1) * QUARTER] = sum(
+            pieces_ref[x * Y_COUNT + y].astype(F32) for y in range(Y_COUNT)
+        )
+
+
+def total_rows(pieces):
+    return pl.pallas_call(
+        total_kernel,
+        out_shape=jax.ShapeDtypeStruct((ROWS_DEV, WIDTH), F32),
+        in_specs=in_vmem(1),
+        out_specs=in_vmem(1)[0],
+        compiler_params=params(),
+        name="total_rows",
+    )(pieces)
 
 
 def per_device(
@@ -567,14 +609,12 @@
         joined.reshape(HEADS, TOKENS, 3 * HEAD_DIM), "ctx", 0, 0, axis_index_groups=HEAD_GROUPS
     )
     proj_grad, rows = finish(grads, slope, gate, base, in_proj, token_slot, codes)
-    rows = lax.all_to_all(rows.reshape(TABLES, SEND_ROWS, 128), "table", 0, 0)
-    rows = compact_rows(rows.reshape(TABLES * SEND_ROWS, 128))
-    rows = lax.all_to_all(rows, "ctx", 0, 0, axis_index_groups=X_GROUPS)
+    rows = lax.all_to_all(rows, ("ctx", "table"), 0, 0, axis_index_groups=X_CORE_GROUPS)
+    rows = arrange_rows(rows).reshape(FARS, FAR_ROWS, QUARTER)
+    rows = lax.all_to_all(rows, "table", 0, 0, axis_index_groups=FAR_GROUPS)
     dense, proj_grad = scatter_rows(rows, proj_grad)
-    pieces = lax.all_to_all(
-        dense.reshape(Y_COUNT, ROWS_DEV, WIDTH), "ctx", 0, 0, axis_index_groups=Y_GROUPS
-    )
-    table_grad = jnp.sum(pieces.astype(F32), axis=0)
+    pieces = lax.all_to_all(dense.reshape(CTX_COUNT, ROWS_DEV, QUARTER), "ctx", 0, 0)
+    table_grad = total_rows(pieces)
     return (proj_grad[None], table_grad)
 
 

time: 114 us -> 110 us (0.965)
  blocking collectives: 79.7 us -> 76.4 us
    all_to_all x3, blocking collectives: 52.1 us -> 48.8 us  [the longest x1 27.9 us: per_device(): rows = lax.all_to_all(rows, 'table', 0, 0, axis_index_groups=FAR_GROUPS)]
where the time goes in v4:
time: 110 us
  blocking collectives  76.4 us (69%)
  starting transfers between devices  12.1 us (11%)
  Pallas kernels  10.2 us (9%)
  waiting for transfers between devices  9.84 us (9%)
  between operations  1.42 us (1%)
    all_to_all x1, blocking collectives, per_device(): rows = lax.all_to_all(rows, 'table', 0, 0, axis_index_groups=FAR_GROUPS)  27.9 us
    all_to_all x1, blocking collectives, per_device(): own = lax.all_to_all(parts, 'ctx', 0, 0, axis_index_groups=HEAD_GROUPS)  15.5 us
    all_to_all x1, blocking collectives, per_device(): lax.all_to_all(joined.reshape(HEADS, TOKENS, 3 * HEAD_DIM), 'ctx', 0, 0,...  12.2 us
    all_to_all x1, blocking collectives, per_device(): lax.all_to_all(dense.reshape(CTX_COUNT, ROWS_DEV, QUARTER), 'ctx', 0, 0)  12.1 us
    all_to_all x1, blocking collectives, per_device(): lax.all_to_all(rows, ('ctx', 'table'), 0, 0, axis_index_groups=X_CORE_GRO...  8.7 us
    ppermute x1, waiting for transfers between devices, per_device(): query_far = lax.ppermute(own[:, :, :2 * HEAD_DIM], 'ctx', SWAP_QUERY)  6.27 us
    ppermute x1, starting transfers between devices, per_device(): query_got = lax.ppermute(query_send, 'ctx', SWAP_QUERY)  5.29 us
    ppermute x1, waiting for transfers between devices, per_device(): query_got = lax.ppermute(query_send, 'ctx', SWAP_QUERY)  3.56 us
  transfers between devices with their start and end apart: 4, of which 2 were waited for; matrix products, arithmetic and copies ran while one was open for 0% of the time, Pallas kernels for 3%

profile of v4, /device:TPU:8, one launch (start us, length us, event | category | flops | bytes accessed | tf_op | source)
XLA Modules:
  0.0 110.0 jit_solution(8476924325334298608)
XLA Ops:
  1.3 0.0 copy-start
  1.3 0.0 copy-start.1
  1.3 0.0 copy-start.2
  1.3 2.8 %project.1 = (bf16[4,128,512]{2,1,0:T(8,128)(2,1)S(1)}, f32[128,2048]{1,0:T(8,128)S(1)}, f32[128,512]{1,0:T(8,128)S(1)}) custom-call(s32[1]{0:T(128)S(6)} %copy.11.length_ref, bf16[128,512]{1,0:T(8,128)(2,1)} %bitcast.18, bf16[128,512]{1,0:T(8,128)(2,1)} %bitcast.19, bf16[128,512]{1,0:T(8,128)(2,1)} %bitcast.15, bf16[512,2048]{1,0:T(8,128)(2,1)} %in_proj_ref.3, ...), custom_call_target="tpu_custom_call" | custom-call | tf_op jit(solution)/shard_map/project/pallas_call | solution.py:157
  4.2 15.5 %all_to_all.25 = bf16[4,128,512]{2,1,0:T(8,128)(2,1)S(1)} all-to-all(bf16[4,128,512]{2,1,0:T(8,128)(2,1)S(1)} %get-tuple-element.20), channel_id=1, replica_groups={{0,32,384,416},{64,96,448,480},{128,160,256,288},{192,224,320,352},{1,3..., dimensions={0} | all-to-all | bytes 1048576 | tf_op jit(solution)/shard_map/all_to_all | solution.py:595
  19.7 3.0 %collective-permute-start = (bf16[2,256,256]{2,1,0:T(8,128)(2,1)S(1)}, bf16[2,256,256]{2,1,0:T(8,128)(2,1)S(1)}, u32[]{:S(2)}, u32[]{:S(2)}) collective-permute-start(bf16[2,256,256]{2,1,0:T(8,128)(2,1)S(1)} %get-tuple-element.39), channel_id=1, source_target_pairs={{0,64},{32,96},{64,0},{96,32},{128,192},{160,224},{192,128},{224,1... | collective-permute-start | bytes 786440 | tf_op jit(solution)/shard_map/ppermute | solution.py:597
  22.6 1.9 %collective-permute-start.1 = (bf16[2,256,256]{2,1,0:T(8,128)(2,1)S(1)}, bf16[2,256,256]{2,1,0:T(8,128)(2,1)S(1)}, u32[]{:S(2)}, u32[]{:S(2)}) collective-permute-start(bf16[2,256,256]{2,1,0:T(8,128)(2,1)S(1)} %get-tuple-element.38), channel_id=1, source_target_pairs={{0,128},{32,160},{64,192},{96,224},{128,0},{160,32},{192,64},{224,... | collective-permute-start | bytes 786440 | tf_op jit(solution)/shard_map/ppermute | solution.py:598
  24.5 0.0 copy-done
  24.6 0.0 copy-done.1
  24.6 0.0 copy-done.2
  24.6 0.6 local_terms.1
  25.2 1.1 %attend_own.1 = (f32[2,256,128]{2,1,0:T(8,128)S(1)}, f32[2,256,256]{2,1,0:T(8,128)S(1)}) custom-call(s32[1]{0:T(128)S(6)} %copy.11.length_ref, bf16[2,256,512]{2,1,0:T(8,128)(2,1)S(1)} %bitcast.10), custom_call_target="tpu_custom_call" | custom-call | flops 251658240 | bytes 2097152 | tf_op jit(solution)/shard_map/attend_own/pallas_call | solution.py:358
  26.3 6.3 %collective-permute-done.query_far_ref = bf16[2,256,256]{2,1,0:T(8,128)(2,1)S(1)} collective-permute-done((bf16[2,256,256]{2,1,0:T(8,128)(2,1)S(1)}, bf16[2,256,256]{2,1,0:T(8,128)(2,1)S(1)}, u32[]{:S(2)}, u32[]{:S(2)}) %collective-permute-start) | collective-permute-done | bytes 262176 | tf_op jit(solution)/shard_map/ppermute | solution.py:597
  32.6 1.1 %attend_queries.1 = (f32[2,256,128]{2,1,0:T(8,128)S(1)}, f32[2,256,256]{2,1,0:T(8,128)S(1)}) custom-call(s32[1]{0:T(128)S(6)} %copy.11.length_ref, bf16[2,256,512]{2,1,0:T(8,128)(2,1)S(1)} %bitcast.11, bf16[2,256,256]{2,1,0:T(8,128)(2,1)S(1)} %collective-permute-done.query_far_ref, f32[2,256,256]{2,1,0:T(8,128)S(1)} %get-tuple-element.22.sums_ref, ...), custom_call_target="tpu_custom_call" | custom-call | flops 251658240 | bytes 2097152 | tf_op jit(solution)/shard_map/attend_queries/pallas_call | solution.py:370
  33.7 0.0 copy-start.3
  33.7 0.0 collective-permute-done.1.key_far_ref
  33.7 1.8 %attend_keys.1 = (f32[2,256,128]{2,1,0:T(8,128)S(1)}, bf16[2,256,128]{2,1,0:T(8,128)(2,1)S(1)}, bf16[2,256,256]{2,1,0:T(8,128)(2,1)S(1)}) custom-call(s32[1]{0:T(128)S(6)} %copy.11.length_ref, bf16[2,256,512]{2,1,0:T(8,128)(2,1)S(1)} %bitcast.12, bf16[2,256,256]{2,1,0:T(8,128)(2,1)S(1)} %collective-permute-done.query_far_ref, ...), custom_call_target="tpu_custom_call" | custom-call | flops 335544320 | bytes 2097152 | tf_op jit(solution)/shard_map/attend_keys/pallas_call | solution.py:382
  35.5 1.9 %collective-permute-start.3 = (bf16[2,256,256]{2,1,0:T(8,128)(2,1)S(1)}, bf16[2,256,256]{2,1,0:T(8,128)(2,1)S(1)}, u32[]{:S(2)}, u32[]{:S(2)}) collective-permute-start(bf16[2,256,256]{2,1,0:T(8,128)(2,1)S(1)} %get-tuple-element.30), channel_id=1, source_target_pairs={{0,128},{32,160},{64,192},{96,224},{128,0},{160,32},{192,64},{224,... | collective-permute-start | bytes 786440 | tf_op jit(solution)/shard_map/ppermute | solution.py:606
  37.5 5.3 %collective-permute-start.2 = (bf16[2,256,128]{2,1,0:T(8,128)(2,1)S(1)}, bf16[2,256,128]{2,1,0:T(8,128)(2,1)S(1)}, u32[]{:S(2)}, u32[]{:S(2)}) collective-permute-start(bf16[2,256,128]{2,1,0:T(8,128)(2,1)S(1)} %get-tuple-element.28), channel_id=1, source_target_pairs={{0,64},{32,96},{64,0},{96,32},{128,192},{160,224},{192,128},{224,1... | collective-permute-start | bytes 393224 | tf_op jit(solution)/shard_map/ppermute | solution.py:605
  42.8 3.6 %collective-permute-done.2.query_got_ref = bf16[2,256,128]{2,1,0:T(8,128)(2,1)S(1)} collective-permute-done((bf16[2,256,128]{2,1,0:T(8,128)(2,1)S(1)}, bf16[2,256,128]{2,1,0:T(8,128)(2,1)S(1)}, u32[]{:S(2)}, u32[]{:S(2)}) %collective-permute-start.2) | collective-permute-done | bytes 131104 | tf_op jit(solution)/shard_map/ppermute | solution.py:605
  46.3 0.0 collective-permute-done.3.key_got_ref
  46.3 0.1 join_parts.1
  46.4 12.2 %all_to_all.26.grads_ref = bf16[4,128,384]{2,1,0:T(8,128)(2,1)S(1)} all-to-all(bf16[4,128,384]{2,1,0:T(8,128)(2,1)S(1)} %bitcast.13), channel_id=1, replica_groups={{0,32,384,416},{64,96,448,480},{128,160,256,288},{192,224,320,352},{1,3..., dimensions={0} | all-to-all | bytes 786432 | tf_op jit(solution)/shard_map/all_to_all | solution.py:608
  58.6 0.0 copy-done.3
  58.6 0.9 finish.1
  59.4 8.7 %all_to_all.27.rows_ref = bf16[8,72,128]{2,1,0:T(8,128)(2,1)S(1)} all-to-all(bf16[8,72,128]{2,1,0:T(8,128)(2,1)S(1)} %get-tuple-element.34), channel_id=1, replica_groups={{0,1,128,129,256,257,384,385},{2,3,130,131,258,259,386,387},{4,5,132,13..., dimensions={0} | all-to-all | bytes 294912 | tf_op jit(solution)/shard_map/all_to_all | solution.py:612
  68.1 0.3 arrange_rows.1
  68.4 27.9 %all_to_all.28.rows_ref = bf16[16,40,128]{2,1,0:T(8,128)(2,1)S(1)} all-to-all(bf16[16,40,128]{2,1,0:T(8,128)(2,1)S(1)} %bitcast.14), channel_id=1, replica_groups={{0,2,4,6,8,10,12,14,16,18,20,22,24,26,28,30},{1,3,5,7,9,11,13,15,17,19,..., dimensions={0} | all-to-all | bytes 327680 | tf_op jit(solution)/shard_map/all_to_all | solution.py:614
  96.3 0.8 scatter_rows.1
  97.1 12.1 %all_to_all.29.pieces_ref = bf16[16,64,128]{2,1,0:T(8,128)(2,1)S(1)} all-to-all(bf16[16,64,128]{2,1,0:T(8,128)(2,1)S(1)} %bitcast.17), channel_id=1, replica_groups=mesh['ctx'=16,'table'=32] {'ctx'}, dimensions={0} | all-to-all | bytes 524288 | tf_op jit(solution)/shard_map/all_to_all | solution.py:616
  109.3 0.7 total_rows.1
  (1 shorter events, 0.0 us)
Async XLA Ops:
  1.3 23.3 %copy-start = (bf16[512,2048]{1,0:T(8,128)(2,1)S(1)}, bf16[512,2048]{1,0:T(8,128)(2,1)}, u32[]{:S(2)}) copy-start(bf16[512,2048]{1,0:T(8,128)(2,1)} %in_proj_ref.3) | copy-start | bytes 6291460
  1.3 23.3 %copy-start.1 = (bf16[1,128,512]{2,1,0:T(8,128)(2,1)S(1)}, bf16[1,128,512]{2,1,0:T(8,128)(2,1)}, u32[]{:S(2)}) copy-start(bf16[1,128,512]{2,1,0:T(8,128)(2,1)} %param.11) | copy-start | bytes 393220
  1.3 23.3 %copy-start.2 = (s32[1,128]{1,0:T(1,128)S(1)}, s32[1,128]{1,0:T(1,128)}, u32[]{:S(2)}) copy-start(s32[1,128]{1,0:T(1,128)} %item_ref.1) | copy-start | bytes 1540
  19.7 12.9 %collective-permute-start = (bf16[2,256,256]{2,1,0:T(8,128)(2,1)S(1)}, bf16[2,256,256]{2,1,0:T(8,128)(2,1)S(1)}, u32[]{:S(2)}, u32[]{:S(2)}) collective-permute-start(bf16[2,256,256]{2,1,0:T(8,128)(2,1)S(1)} %get-tuple-element.39), channel_id=1, source_target_pairs={{0,64},{32,96},{64,0},{96,32},{128,192},{160,224},{192,128},{224,1... | collective-permute-start | bytes 786440 | tf_op jit(solution)/shard_map/ppermute | solution.py:597
  22.6 11.1 %collective-permute-start.1 = (bf16[2,256,256]{2,1,0:T(8,128)(2,1)S(1)}, bf16[2,256,256]{2,1,0:T(8,128)(2,1)S(1)}, u32[]{:S(2)}, u32[]{:S(2)}) collective-permute-start(bf16[2,256,256]{2,1,0:T(8,128)(2,1)S(1)} %get-tuple-element.38), channel_id=1, source_target_pairs={{0,128},{32,160},{64,192},{96,224},{128,0},{160,32},{192,64},{224,... | collective-permute-start | bytes 786440 | tf_op jit(solution)/shard_map/ppermute | solution.py:598
  33.7 24.8 %copy-start.3 = (s32[1,128]{1,0:T(1,128)S(1)}, s32[1,128]{1,0:T(1,128)}, u32[]{:S(2)}) copy-start(s32[1,128]{1,0:T(1,128)} %slot_ref.1) | copy-start | bytes 1540
  35.5 10.8 %collective-permute-start.3 = (bf16[2,256,256]{2,1,0:T(8,128)(2,1)S(1)}, bf16[2,256,256]{2,1,0:T(8,128)(2,1)S(1)}, u32[]{:S(2)}, u32[]{:S(2)}) collective-permute-start(bf16[2,256,256]{2,1,0:T(8,128)(2,1)S(1)} %get-tuple-element.30), channel_id=1, source_target_pairs={{0,128},{32,160},{64,192},{96,224},{128,0},{160,32},{192,64},{224,... | collective-permute-start | bytes 786440 | tf_op jit(solution)/shard_map/ppermute | solution.py:606
  37.5 8.9 %collective-permute-start.2 = (bf16[2,256,128]{2,1,0:T(8,128)(2,1)S(1)}, bf16[2,256,128]{2,1,0:T(8,128)(2,1)S(1)}, u32[]{:S(2)}, u32[]{:S(2)}) collective-permute-start(bf16[2,256,128]{2,1,0:T(8,128)(2,1)S(1)} %get-tuple-element.28), channel_id=1, source_target_pairs={{0,64},{32,96},{64,0},{96,32},{128,192},{160,224},{192,128},{224,1... | collective-permute-start | bytes 393224 | tf_op jit(solution)/shard_map/ppermute | solution.py:605

commit v5 on v4

--- a/solution.py
+++ b/solution.py
@@ -29,11 +29,24 @@
 BF16 = jnp.bfloat16
 F32 = jnp.float32
 
+def device(x, y, table):
+    return (x * Y_COUNT + y) * TABLES + table
+
+
+def y_of(core, part, bit):
+    return part * 2 + bit if core == 0 else bit * 2 + part
+
+
 X_PAIRS = ((0, 3), (1, 2))
 HEAD_GROUPS = [
-    [X_PAIRS[pair][place] * Y_COUNT + upper * 2 + parity for place in range(2) for parity in range(2)]
+    [
+        device(X_PAIRS[pair][place], y_of(table % CORES, part, bit), table)
+        for place in range(2)
+        for bit in range(2)
+    ]
     for pair in range(2)
-    for upper in range(2)
+    for part in range(2)
+    for table in range(TABLES)
 ]
 X_CORE_GROUPS = [
     [
@@ -45,8 +58,15 @@
     for far in range(FARS)
 ]
 FAR_GROUPS = [[far * CORES + core for far in range(FARS)] for core in range(CORES)]
-SWAP_QUERY = [(c, c ^ 2) for c in range(X_COUNT * Y_COUNT)]
-SWAP_KEY = [(c, c ^ Y_COUNT) for c in range(X_COUNT * Y_COUNT)]
+SWAP_QUERY = [
+    (c * TABLES + t, (c ^ (2 if t % CORES == 0 else 1)) * TABLES + t)
+    for c in range(CTX_COUNT)
+    for t in range(TABLES)
+]
+SWAP_KEY = [
+    (c * TABLES + t, (c ^ Y_COUNT) * TABLES + t) for c in range(CTX_COUNT) for t in range(TABLES)
+]
+AXES = ("ctx", "table")
 
 MATMUL = (((1,), (0,)), ((), ()))
 MATMUL_NT = (((1,), (1,)), ((), ()))
@@ -260,7 +280,16 @@
 def place_of_device():
     ctx = lax.axis_index("ctx")
     x = lax.div(ctx, Y_COUNT)
-    return (x ^ lax.div(x, 2)) & 1, lax.div(lax.rem(ctx, Y_COUNT), 2)
+    y = lax.rem(ctx, Y_COUNT)
+    core = lax.rem(lax.axis_index("table"), CORES)
+    part = jnp.where(core == 0, lax.div(y, 2), lax.rem(y, 2))
+    return (x ^ lax.div(x, 2)) & 1, part, core
+
+
+def position(index, part, core):
+    halves = part * TILE + index
+    parities = (index // TOKENS) * TILE + part * TOKENS + index % TOKENS
+    return jnp.where(core == 0, halves, parities)
 
 
 def weight_of(length_ref):
@@ -268,11 +297,11 @@
 
 
 def attend_near(length_ref, query_ref, own_ref, flip):
-    _, upper = place_of_device()
+    _, part, core = place_of_device()
     weight = weight_of(length_ref)
     rows = lax.broadcasted_iota(jnp.int32, (2 * TILE, 1), 0)
-    rows = jnp.where(rows < TILE, -1, rows - TILE + upper * TILE)
-    columns = lax.broadcasted_iota(jnp.int32, (1, TILE), 1) + (upper ^ flip) * TILE
+    rows = jnp.where(rows < TILE, -1, position(rows - TILE, part, core))
+    columns = position(lax.broadcasted_iota(jnp.int32, (1, TILE), 1), part ^ flip, core)
     live = rows <= columns
     column = 2 * HEAD_DIM
     low = tile_grads(query_ref, 0, own_ref, 0, column, weight, live[TILE:])
@@ -315,7 +344,7 @@
     query_acc,
     key_acc,
 ):
-    pair, _ = place_of_device()
+    pair, _, _ = place_of_device()
     weight = weight_of(length_ref)
     last = 1 - pair
     for place, (query_ref, near_ref) in enumerate(
@@ -592,24 +621,24 @@
     parts, pre, gain_grad = project(
         seq_lengths, item_inputs[0], attn_saved[0], out_grad[0], in_proj, out_proj, norm_gain[None]
     )
-    own = lax.all_to_all(parts, "ctx", 0, 0, axis_index_groups=HEAD_GROUPS)
+    own = lax.all_to_all(parts, AXES, 0, 0, axis_index_groups=HEAD_GROUPS)
     own = own.reshape(2, TILE, 4 * HEAD_DIM)
-    query_far = lax.ppermute(own[:, :, : 2 * HEAD_DIM], "ctx", SWAP_QUERY)
-    key_far = lax.ppermute(own[:, :, 2 * HEAD_DIM :], "ctx", SWAP_KEY)
+    query_far = lax.ppermute(own[:, :, : 2 * HEAD_DIM], AXES, SWAP_QUERY)
+    key_far = lax.ppermute(own[:, :, 2 * HEAD_DIM :], AXES, SWAP_KEY)
     near_own, sums = attend_own(seq_lengths, own)
     slope, gate, base, codes = local_terms(pre, gain_grad, out_grad[0], in_proj, slot_rows)
     near_far, key_own = attend_queries(seq_lengths, own, query_far, sums, codes)
     query_own, query_send, key_send = attend_keys(
         seq_lengths, own, query_far, key_far, near_own, near_far
     )
-    query_got = lax.ppermute(query_send, "ctx", SWAP_QUERY)
-    key_got = lax.ppermute(key_send, "ctx", SWAP_KEY)
+    query_got = lax.ppermute(query_send, AXES, SWAP_QUERY)
+    key_got = lax.ppermute(key_send, AXES, SWAP_KEY)
     joined = join_parts(query_own, query_got, key_own, key_got)
     grads = lax.all_to_all(
-        joined.reshape(HEADS, TOKENS, 3 * HEAD_DIM), "ctx", 0, 0, axis_index_groups=HEAD_GROUPS
+        joined.reshape(HEADS, TOKENS, 3 * HEAD_DIM), AXES, 0, 0, axis_index_groups=HEAD_GROUPS
     )
     proj_grad, rows = finish(grads, slope, gate, base, in_proj, token_slot, codes)
-    rows = lax.all_to_all(rows, ("ctx", "table"), 0, 0, axis_index_groups=X_CORE_GROUPS)
+    rows = lax.all_to_all(rows, AXES, 0, 0, axis_index_groups=X_CORE_GROUPS)
     rows = arrange_rows(rows).reshape(FARS, FAR_ROWS, QUARTER)
     rows = lax.all_to_all(rows, "table", 0, 0, axis_index_groups=FAR_GROUPS)
     dense, proj_grad = scatter_rows(rows, proj_grad)

time: 110 us -> 107 us (0.973)
  blocking collectives: 76.4 us -> 71.9 us
    all_to_all x1, blocking collectives: 27.9 us -> 24.7 us  [per_device(): rows = lax.all_to_all(rows, 'table', 0, 0, axis_index_groups=FAR_GROUPS)]
    all_to_all x3, blocking collectives: 36.3 us -> 34.6 us  [the longest x1 16.3 us: per_device(): own = lax.all_to_all(parts, AXES, 0, 0, axis_index_groups=HEAD_GROUPS)]
  transfers between devices with their start and end apart: 4 -> 4, of which waited for: 2 -> 3; matrix products, arithmetic and copies ran while one was open for 0% -> 0% of each run, Pallas kernels for 3% -> 3%
where the time goes in v5:
time: 107 us; the launch traced here: 106 us
  blocking collectives  71.9 us (67%)
  starting transfers between devices  12.2 us (11%)
  waiting for transfers between devices  10.4 us (10%)
  Pallas kernels  10.2 us (10%)
  between operations  1.42 us (1%)
    all_to_all x1, blocking collectives, per_device(): rows = lax.all_to_all(rows, 'table', 0, 0, axis_index_groups=FAR_GROUPS)  24.7 us
    all_to_all x1, blocking collectives, per_device(): own = lax.all_to_all(parts, AXES, 0, 0, axis_index_groups=HEAD_GROUPS)  16.3 us
    all_to_all x1, blocking collectives, per_device(): lax.all_to_all(dense.reshape(CTX_COUNT, ROWS_DEV, QUARTER), 'ctx', 0, 0)  12.7 us
    all_to_all x1, blocking collectives, per_device(): lax.all_to_all(joined.reshape(HEADS, TOKENS, 3 * HEAD_DIM), AXES, 0, 0, a...  9.62 us
    all_to_all x1, blocking collectives, per_device(): rows = lax.all_to_all(rows, AXES, 0, 0, axis_index_groups=X_CORE_GROUPS)  8.7 us
    ppermute x1, waiting for transfers between devices, per_device(): query_got = lax.ppermute(query_send, AXES, SWAP_QUERY)  6.98 us
    ppermute x1, starting transfers between devices, per_device(): query_got = lax.ppermute(query_send, AXES, SWAP_QUERY)  4.86 us
    ppermute x1, starting transfers between devices, per_device(): query_far = lax.ppermute(own[:, :, :2 * HEAD_DIM], AXES, SWAP_QUERY)  3.5 us
  transfers between devices with their start and end apart: 4, of which 3 were waited for; matrix products, arithmetic and copies ran while one was open for 0% of the time, Pallas kernels for 3%

profile of v5, /device:TPU:8, one launch (start us, length us, event | category | flops | bytes accessed | tf_op | source)
XLA Modules:
  0.0 106.2 jit_solution(13888058492452004692)
XLA Ops:
  1.3 0.0 copy-start
  1.3 0.0 copy-start.1
  1.3 0.0 copy-start.2
  1.3 2.8 %project.1 = (bf16[4,128,512]{2,1,0:T(8,128)(2,1)S(1)}, f32[128,2048]{1,0:T(8,128)S(1)}, f32[128,512]{1,0:T(8,128)S(1)}) custom-call(s32[1]{0:T(128)S(6)} %copy.11.length_ref, bf16[128,512]{1,0:T(8,128)(2,1)} %bitcast.18, bf16[128,512]{1,0:T(8,128)(2,1)} %bitcast.19, bf16[128,512]{1,0:T(8,128)(2,1)} %bitcast.15, bf16[512,2048]{1,0:T(8,128)(2,1)} %in_proj_ref.3, ...), custom_call_target="tpu_custom_call" | custom-call | tf_op jit(solution)/shard_map/project/pallas_call | solution.py:177
  4.2 16.3 %all_to_all.25 = bf16[4,128,512]{2,1,0:T(8,128)(2,1)S(1)} all-to-all(bf16[4,128,512]{2,1,0:T(8,128)(2,1)S(1)} %get-tuple-element.20), channel_id=1, replica_groups={{0,32,384,416},{1,65,385,449},{2,34,386,418},{3,67,387,451},{4,36,388,4..., dimensions={0} | all-to-all | bytes 1048576 | tf_op jit(solution)/shard_map/all_to_all | solution.py:624
  20.5 3.5 %collective-permute-start = (bf16[2,256,256]{2,1,0:T(8,128)(2,1)S(1)}, bf16[2,256,256]{2,1,0:T(8,128)(2,1)S(1)}, u32[]{:S(2)}, u32[]{:S(2)}) collective-permute-start(bf16[2,256,256]{2,1,0:T(8,128)(2,1)S(1)} %get-tuple-element.39), channel_id=1, source_target_pairs={{0,64},{1,33},{2,66},{3,35},{4,68},{5,37},{6,70},{7,39},{8,72},{9,... | collective-permute-start | bytes 786440 | tf_op jit(solution)/shard_map/ppermute | solution.py:626
  24.0 1.9 %collective-permute-start.1 = (bf16[2,256,256]{2,1,0:T(8,128)(2,1)S(1)}, bf16[2,256,256]{2,1,0:T(8,128)(2,1)S(1)}, u32[]{:S(2)}, u32[]{:S(2)}) collective-permute-start(bf16[2,256,256]{2,1,0:T(8,128)(2,1)S(1)} %get-tuple-element.38), channel_id=1, source_target_pairs={{0,128},{1,129},{2,130},{3,131},{4,132},{5,133},{6,134},{7,135},{8... | collective-permute-start | bytes 786440 | tf_op jit(solution)/shard_map/ppermute | solution.py:627
  25.9 0.0 copy-done
  25.9 0.0 copy-done.1
  25.9 0.0 copy-done.2
  25.9 0.6 local_terms.1
  26.5 1.1 %attend_own.1 = (f32[2,256,128]{2,1,0:T(8,128)S(1)}, f32[2,256,256]{2,1,0:T(8,128)S(1)}) custom-call(s32[1]{0:T(128)S(6)} %copy.11.length_ref, bf16[2,256,512]{2,1,0:T(8,128)(2,1)S(1)} %bitcast.10), custom_call_target="tpu_custom_call" | custom-call | flops 251658240 | bytes 2097152 | tf_op jit(solution)/shard_map/attend_own/pallas_call | solution.py:387
  27.7 3.0 %collective-permute-done.query_far_ref = bf16[2,256,256]{2,1,0:T(8,128)(2,1)S(1)} collective-permute-done((bf16[2,256,256]{2,1,0:T(8,128)(2,1)S(1)}, bf16[2,256,256]{2,1,0:T(8,128)(2,1)S(1)}, u32[]{:S(2)}, u32[]{:S(2)}) %collective-permute-start) | collective-permute-done | bytes 262176 | tf_op jit(solution)/shard_map/ppermute | solution.py:626
  30.7 1.1 %attend_queries.1 = (f32[2,256,128]{2,1,0:T(8,128)S(1)}, f32[2,256,256]{2,1,0:T(8,128)S(1)}) custom-call(s32[1]{0:T(128)S(6)} %copy.11.length_ref, bf16[2,256,512]{2,1,0:T(8,128)(2,1)S(1)} %bitcast.11, bf16[2,256,256]{2,1,0:T(8,128)(2,1)S(1)} %collective-permute-done.query_far_ref, f32[2,256,256]{2,1,0:T(8,128)S(1)} %get-tuple-element.22.sums_ref, ...), custom_call_target="tpu_custom_call" | custom-call | flops 251658240 | bytes 2097152 | tf_op jit(solution)/shard_map/attend_queries/pallas_call | solution.py:399
  31.8 0.0 copy-start.3
  31.8 0.4 collective-permute-done.1.key_far_ref
  32.2 1.8 %attend_keys.1 = (f32[2,256,128]{2,1,0:T(8,128)S(1)}, bf16[2,256,128]{2,1,0:T(8,128)(2,1)S(1)}, bf16[2,256,256]{2,1,0:T(8,128)(2,1)S(1)}) custom-call(s32[1]{0:T(128)S(6)} %copy.11.length_ref, bf16[2,256,512]{2,1,0:T(8,128)(2,1)S(1)} %bitcast.12, bf16[2,256,256]{2,1,0:T(8,128)(2,1)S(1)} %collective-permute-done.query_far_ref, ...), custom_call_target="tpu_custom_call" | custom-call | flops 335544320 | bytes 2097152 | tf_op jit(solution)/shard_map/attend_keys/pallas_call | solution.py:411
  34.0 1.9 %collective-permute-start.3 = (bf16[2,256,256]{2,1,0:T(8,128)(2,1)S(1)}, bf16[2,256,256]{2,1,0:T(8,128)(2,1)S(1)}, u32[]{:S(2)}, u32[]{:S(2)}) collective-permute-start(bf16[2,256,256]{2,1,0:T(8,128)(2,1)S(1)} %get-tuple-element.30), channel_id=1, source_target_pairs={{0,128},{1,129},{2,130},{3,131},{4,132},{5,133},{6,134},{7,135},{8... | collective-permute-start | bytes 786440 | tf_op jit(solution)/shard_map/ppermute | solution.py:635
  36.0 4.9 %collective-permute-start.2 = (bf16[2,256,128]{2,1,0:T(8,128)(2,1)S(1)}, bf16[2,256,128]{2,1,0:T(8,128)(2,1)S(1)}, u32[]{:S(2)}, u32[]{:S(2)}) collective-permute-start(bf16[2,256,128]{2,1,0:T(8,128)(2,1)S(1)} %get-tuple-element.28), channel_id=1, source_target_pairs={{0,64},{1,33},{2,66},{3,35},{4,68},{5,37},{6,70},{7,39},{8,72},{9,... | collective-permute-start | bytes 393224 | tf_op jit(solution)/shard_map/ppermute | solution.py:634
  40.8 7.0 %collective-permute-done.2.query_got_ref = bf16[2,256,128]{2,1,0:T(8,128)(2,1)S(1)} collective-permute-done((bf16[2,256,128]{2,1,0:T(8,128)(2,1)S(1)}, bf16[2,256,128]{2,1,0:T(8,128)(2,1)S(1)}, u32[]{:S(2)}, u32[]{:S(2)}) %collective-permute-start.2) | collective-permute-done | bytes 131104 | tf_op jit(solution)/shard_map/ppermute | solution.py:634
  47.8 0.0 collective-permute-done.3.key_got_ref
  47.8 0.1 join_parts.1
  47.9 9.6 %all_to_all.26.grads_ref = bf16[4,128,384]{2,1,0:T(8,128)(2,1)S(1)} all-to-all(bf16[4,128,384]{2,1,0:T(8,128)(2,1)S(1)} %bitcast.13), channel_id=1, replica_groups={{0,32,384,416},{1,65,385,449},{2,34,386,418},{3,67,387,451},{4,36,388,4..., dimensions={0} | all-to-all | bytes 786432 | tf_op jit(solution)/shard_map/all_to_all | solution.py:637
  57.5 0.0 copy-done.3
  57.5 0.9 finish.1
  58.4 8.7 %all_to_all.27.rows_ref = bf16[8,72,128]{2,1,0:T(8,128)(2,1)S(1)} all-to-all(bf16[8,72,128]{2,1,0:T(8,128)(2,1)S(1)} %get-tuple-element.34), channel_id=1, replica_groups={{0,1,128,129,256,257,384,385},{2,3,130,131,258,259,386,387},{4,5,132,13..., dimensions={0} | all-to-all | bytes 294912 | tf_op jit(solution)/shard_map/all_to_all | solution.py:641
  67.1 0.3 arrange_rows.1
  67.4 24.7 %all_to_all.28.rows_ref = bf16[16,40,128]{2,1,0:T(8,128)(2,1)S(1)} all-to-all(bf16[16,40,128]{2,1,0:T(8,128)(2,1)S(1)} %bitcast.14), channel_id=1, replica_groups={{0,2,4,6,8,10,12,14,16,18,20,22,24,26,28,30},{1,3,5,7,9,11,13,15,17,19,..., dimensions={0} | all-to-all | bytes 327680 | tf_op jit(solution)/shard_map/all_to_all | solution.py:643
  92.0 0.8 scatter_rows.1
  92.8 12.7 %all_to_all.29.pieces_ref = bf16[16,64,128]{2,1,0:T(8,128)(2,1)S(1)} all-to-all(bf16[16,64,128]{2,1,0:T(8,128)(2,1)S(1)} %bitcast.17), channel_id=1, replica_groups=mesh['ctx'=16,'table'=32] {'ctx'}, dimensions={0} | all-to-all | bytes 524288 | tf_op jit(solution)/shard_map/all_to_all | solution.py:645
  105.5 0.7 total_rows.1
  (1 shorter events, 0.0 us)
Async XLA Ops:
  1.3 24.6 %copy-start = (bf16[512,2048]{1,0:T(8,128)(2,1)S(1)}, bf16[512,2048]{1,0:T(8,128)(2,1)}, u32[]{:S(2)}) copy-start(bf16[512,2048]{1,0:T(8,128)(2,1)} %in_proj_ref.3) | copy-start | bytes 6291460
  1.3 24.6 %copy-start.1 = (bf16[1,128,512]{2,1,0:T(8,128)(2,1)S(1)}, bf16[1,128,512]{2,1,0:T(8,128)(2,1)}, u32[]{:S(2)}) copy-start(bf16[1,128,512]{2,1,0:T(8,128)(2,1)} %param.11) | copy-start | bytes 393220
  1.3 24.6 %copy-start.2 = (s32[1,128]{1,0:T(1,128)S(1)}, s32[1,128]{1,0:T(1,128)}, u32[]{:S(2)}) copy-start(s32[1,128]{1,0:T(1,128)} %item_ref.1) | copy-start | bytes 1540
  20.5 10.2 %collective-permute-start = (bf16[2,256,256]{2,1,0:T(8,128)(2,1)S(1)}, bf16[2,256,256]{2,1,0:T(8,128)(2,1)S(1)}, u32[]{:S(2)}, u32[]{:S(2)}) collective-permute-start(bf16[2,256,256]{2,1,0:T(8,128)(2,1)S(1)} %get-tuple-element.39), channel_id=1, source_target_pairs={{0,64},{1,33},{2,66},{3,35},{4,68},{5,37},{6,70},{7,39},{8,72},{9,... | collective-permute-start | bytes 786440 | tf_op jit(solution)/shard_map/ppermute | solution.py:626
  24.0 8.3 %collective-permute-start.1 = (bf16[2,256,256]{2,1,0:T(8,128)(2,1)S(1)}, bf16[2,256,256]{2,1,0:T(8,128)(2,1)S(1)}, u32[]{:S(2)}, u32[]{:S(2)}) collective-permute-start(bf16[2,256,256]{2,1,0:T(8,128)(2,1)S(1)} %get-tuple-element.38), channel_id=1, source_target_pairs={{0,128},{1,129},{2,130},{3,131},{4,132},{5,133},{6,134},{7,135},{8... | collective-permute-start | bytes 786440 | tf_op jit(solution)/shard_map/ppermute | solution.py:627
  31.8 25.7 %copy-start.3 = (s32[1,128]{1,0:T(1,128)S(1)}, s32[1,128]{1,0:T(1,128)}, u32[]{:S(2)}) copy-start(s32[1,128]{1,0:T(1,128)} %slot_ref.1) | copy-start | bytes 1540
  34.0 13.8 %collective-permute-start.3 = (bf16[2,256,256]{2,1,0:T(8,128)(2,1)S(1)}, bf16[2,256,256]{2,1,0:T(8,128)(2,1)S(1)}, u32[]{:S(2)}, u32[]{:S(2)}) collective-permute-start(bf16[2,256,256]{2,1,0:T(8,128)(2,1)S(1)} %get-tuple-element.30), channel_id=1, source_target_pairs={{0,128},{1,129},{2,130},{3,131},{4,132},{5,133},{6,134},{7,135},{8... | collective-permute-start | bytes 786440 | tf_op jit(solution)/shard_map/ppermute | solution.py:635
  36.0 11.8 %collective-permute-start.2 = (bf16[2,256,128]{2,1,0:T(8,128)(2,1)S(1)}, bf16[2,256,128]{2,1,0:T(8,128)(2,1)S(1)}, u32[]{:S(2)}, u32[]{:S(2)}) collective-permute-start(bf16[2,256,128]{2,1,0:T(8,128)(2,1)S(1)} %get-tuple-element.28), channel_id=1, source_target_pairs={{0,64},{1,33},{2,66},{3,35},{4,68},{5,37},{6,70},{7,39},{8,72},{9,... | collective-permute-start | bytes 393224 | tf_op jit(solution)/shard_map/ppermute | solution.py:634

commit v6 on v5

--- a/solution.py
+++ b/solution.py
@@ -249,18 +249,8 @@
     )(pre, gain_grad, grad, in_proj, items)
 
 
-def tile_grads(query_ref, query_place, key_ref, key_place, key_column, weight, live):
+def tile_grads(queries, outs, keys, values, weight, live):
     scale = HEAD_DIM ** (-0.5)
-    queries = query_ref[query_place, :, :HEAD_DIM]
-    outs = query_ref[query_place, :, HEAD_DIM : 2 * HEAD_DIM]
-    if key_place is None:
-        keys, values = (
-            key_ref[:, :, column : column + HEAD_DIM].reshape(2 * TILE, HEAD_DIM)
-            for column in (key_column, key_column + HEAD_DIM)
-        )
-    else:
-        keys = key_ref[key_place, :, key_column : key_column + HEAD_DIM]
-        values = key_ref[key_place, :, key_column + HEAD_DIM : key_column + 2 * HEAD_DIM]
     scores = dot(keys, queries, MATMUL_NT) * scale
     attn_grad = dot(values, outs, MATMUL_NT)
     squash = 0.5 + 0.5 * jnp.tanh(scores * 0.5)
@@ -277,6 +267,13 @@
     )
 
 
+def two_of(ref, place, column):
+    blocks = (slice(column, column + HEAD_DIM), slice(column + HEAD_DIM, column + 2 * HEAD_DIM))
+    if place is None:
+        return [ref[:, :, block].reshape(2 * TILE, HEAD_DIM) for block in blocks]
+    return [ref[place, :, block] for block in blocks]
+
+
 def place_of_device():
     ctx = lax.axis_index("ctx")
     x = lax.div(ctx, Y_COUNT)
@@ -304,8 +301,8 @@
     columns = position(lax.broadcasted_iota(jnp.int32, (1, TILE), 1), part ^ flip, core)
     live = rows <= columns
     column = 2 * HEAD_DIM
-    low = tile_grads(query_ref, 0, own_ref, 0, column, weight, live[TILE:])
-    high = tile_grads(query_ref, 1, own_ref, None, column, weight, live)
+    low = tile_grads(*two_of(query_ref, 0, 0), *two_of(own_ref, 0, column), weight, live[TILE:])
+    high = tile_grads(*two_of(query_ref, 1, 0), *two_of(own_ref, None, column), weight, live)
     return low, high
 
 
@@ -347,27 +344,26 @@
     pair, _, _ = place_of_device()
     weight = weight_of(length_ref)
     last = 1 - pair
-    for place, (query_ref, near_ref) in enumerate(
-        ((own_ref, near_own_ref), (query_far_ref, near_far_ref))
-    ):
-        query_acc[...] = near_ref[...]
-        first = tile_grads(query_ref, 1, key_far_ref, 0, 0, weight, None)
-        query_acc[1] += first[0]
-        if place == 0:
-            key_acc[0, :, :HEAD_DIM] = first[1]
-            key_acc[0, :, HEAD_DIM:] = first[2]
-            key_acc[1] = jnp.zeros_like(key_acc[1])
+    query_own_ref[...] = near_own_ref[...]
+    query_acc[...] = near_far_ref[...]
+    key_acc[1] = jnp.zeros_like(key_acc[1])
+    for query_tile, key_tile in ((1, 0), (last, last)):
+        queries, outs = (
+            jnp.concatenate(both, axis=0)
+            for both in zip(two_of(own_ref, query_tile, 0), two_of(query_far_ref, query_tile, 0))
+        )
+        query_part, key_part, value_part = tile_grads(
+            queries, outs, *two_of(key_far_ref, key_tile, 0), weight, None
+        )
+        query_own_ref[query_tile] += query_part[:TILE]
+        query_acc[query_tile] += query_part[TILE:]
+        if key_tile is not last:
+            key_acc[0, :, :HEAD_DIM] = key_part
+            key_acc[0, :, HEAD_DIM:] = value_part
         else:
-            key_acc[0, :, :HEAD_DIM] += first[1]
-            key_acc[0, :, HEAD_DIM:] += first[2]
-        second = tile_grads(query_ref, last, key_far_ref, last, 0, weight, None)
-        query_acc[last] += second[0]
-        key_acc[last, :, :HEAD_DIM] += second[1]
-        key_acc[last, :, HEAD_DIM:] += second[2]
-        if place == 0:
-            query_own_ref[...] = query_acc[...]
-        else:
-            query_send_ref[...] = query_acc[...].astype(BF16)
+            key_acc[last, :, :HEAD_DIM] += key_part
+            key_acc[last, :, HEAD_DIM:] += value_part
+    query_send_ref[...] = query_acc[...].astype(BF16)
     key_send_ref[...] = key_acc[...].astype(BF16)
 
 
@@ -536,7 +532,7 @@
         packed_ref[pl.ds(FAR_SUMS + part, FARS, stride=FAR_ROWS), :] = row
     for row in range(FAR_SUMS + 2, FAR_ROWS):
         packed_ref[pl.ds(row, FARS, stride=FAR_ROWS), :] = jnp.zeros((FARS, 128), F32)
-    out_ref[...] = packed_ref[...].astype(BF16)
+    out_ref[...] = packed_ref[: FARS * FAR_ROWS].astype(BF16)
 
 
 def arrange_rows(rows):
@@ -547,7 +543,7 @@
         out_specs=in_vmem(1)[0],
         scratch_shapes=[
             pltpu.VMEM((X_COUNT * CORES, NEAR_ROWS, QUARTER), F32),
-            pltpu.VMEM((FARS * FAR_ROWS, QUARTER), F32),
+            pltpu.VMEM(((FARS + 1) * FAR_ROWS, QUARTER), F32),
         ],
         compiler_params=params(),
         name="arrange_rows",

time: 107 us -> 106 us (level)
  no operation moved by 1% of the time
where the time goes in v6:
time: 106 us
  blocking collectives  71.9 us (68%)
  starting transfers between devices  12.2 us (12%)
  waiting for transfers between devices  10.4 us (10%)
  Pallas kernels  9.84 us (9%)
  between operations  1.42 us (1%)
    all_to_all x1, blocking collectives, per_device(): rows = lax.all_to_all(rows, 'table', 0, 0, axis_index_groups=FAR_GROUPS)  24.7 us
    all_to_all x1, blocking collectives, per_device(): own = lax.all_to_all(parts, AXES, 0, 0, axis_index_groups=HEAD_GROUPS)  16.3 us
    all_to_all x1, blocking collectives, per_device(): lax.all_to_all(dense.reshape(CTX_COUNT, ROWS_DEV, QUARTER), 'ctx', 0, 0)  12.7 us
    all_to_all x1, blocking collectives, per_device(): lax.all_to_all(joined.reshape(HEADS, TOKENS, 3 * HEAD_DIM), AXES, 0, 0, a...  9.62 us
    all_to_all x1, blocking collectives, per_device(): rows = lax.all_to_all(rows, AXES, 0, 0, axis_index_groups=X_CORE_GROUPS)  8.7 us
    ppermute x1, waiting for transfers between devices, per_device(): query_got = lax.ppermute(query_send, AXES, SWAP_QUERY)  6.97 us
    ppermute x1, starting transfers between devices, per_device(): query_got = lax.ppermute(query_send, AXES, SWAP_QUERY)  4.86 us
    ppermute x1, starting transfers between devices, per_device(): query_far = lax.ppermute(own[:, :, :2 * HEAD_DIM], AXES, SWAP_QUERY)  3.5 us
  transfers between devices with their start and end apart: 4, of which 3 were waited for; matrix products, arithmetic and copies ran while one was open for 0% of the time, Pallas kernels for 3%

profile of v6, /device:TPU:8, one launch (start us, length us, event | category | flops | bytes accessed | tf_op | source)
XLA Modules:
  0.0 105.8 jit_solution(17610623872985349705)
XLA Ops:
  1.3 0.0 copy-start
  1.3 0.0 copy-start.1
  1.3 0.0 copy-start.2
  1.3 2.8 %project.1 = (bf16[4,128,512]{2,1,0:T(8,128)(2,1)S(1)}, f32[128,2048]{1,0:T(8,128)S(1)}, f32[128,512]{1,0:T(8,128)S(1)}) custom-call(s32[1]{0:T(128)S(6)} %copy.11.length_ref, bf16[128,512]{1,0:T(8,128)(2,1)} %bitcast.18, bf16[128,512]{1,0:T(8,128)(2,1)} %bitcast.19, bf16[128,512]{1,0:T(8,128)(2,1)} %bitcast.15, bf16[512,2048]{1,0:T(8,128)(2,1)} %in_proj_ref.3, ...), custom_call_target="tpu_custom_call" | custom-call | tf_op jit(solution)/shard_map/project/pallas_call | solution.py:177
  4.2 16.3 %all_to_all.25 = bf16[4,128,512]{2,1,0:T(8,128)(2,1)S(1)} all-to-all(bf16[4,128,512]{2,1,0:T(8,128)(2,1)S(1)} %get-tuple-element.20), channel_id=1, replica_groups={{0,32,384,416},{1,65,385,449},{2,34,386,418},{3,67,387,451},{4,36,388,4..., dimensions={0} | all-to-all | bytes 1048576 | tf_op jit(solution)/shard_map/all_to_all | solution.py:620
  20.5 3.5 %collective-permute-start = (bf16[2,256,256]{2,1,0:T(8,128)(2,1)S(1)}, bf16[2,256,256]{2,1,0:T(8,128)(2,1)S(1)}, u32[]{:S(2)}, u32[]{:S(2)}) collective-permute-start(bf16[2,256,256]{2,1,0:T(8,128)(2,1)S(1)} %get-tuple-element.39), channel_id=1, source_target_pairs={{0,64},{1,33},{2,66},{3,35},{4,68},{5,37},{6,70},{7,39},{8,72},{9,... | collective-permute-start | bytes 786440 | tf_op jit(solution)/shard_map/ppermute | solution.py:622
  24.0 1.9 %collective-permute-start.1 = (bf16[2,256,256]{2,1,0:T(8,128)(2,1)S(1)}, bf16[2,256,256]{2,1,0:T(8,128)(2,1)S(1)}, u32[]{:S(2)}, u32[]{:S(2)}) collective-permute-start(bf16[2,256,256]{2,1,0:T(8,128)(2,1)S(1)} %get-tuple-element.38), channel_id=1, source_target_pairs={{0,128},{1,129},{2,130},{3,131},{4,132},{5,133},{6,134},{7,135},{8... | collective-permute-start | bytes 786440 | tf_op jit(solution)/shard_map/ppermute | solution.py:623
  25.9 0.0 copy-done
  25.9 0.0 copy-done.1
  25.9 0.0 copy-done.2
  25.9 0.6 local_terms.1
  26.5 1.1 %attend_own.1 = (f32[2,256,128]{2,1,0:T(8,128)S(1)}, f32[2,256,256]{2,1,0:T(8,128)S(1)}) custom-call(s32[1]{0:T(128)S(6)} %copy.11.length_ref, bf16[2,256,512]{2,1,0:T(8,128)(2,1)S(1)} %bitcast.10), custom_call_target="tpu_custom_call" | custom-call | flops 251658240 | bytes 2097152 | tf_op jit(solution)/shard_map/attend_own/pallas_call | solution.py:383
  27.7 3.0 %collective-permute-done.query_far_ref = bf16[2,256,256]{2,1,0:T(8,128)(2,1)S(1)} collective-permute-done((bf16[2,256,256]{2,1,0:T(8,128)(2,1)S(1)}, bf16[2,256,256]{2,1,0:T(8,128)(2,1)S(1)}, u32[]{:S(2)}, u32[]{:S(2)}) %collective-permute-start) | collective-permute-done | bytes 262176 | tf_op jit(solution)/shard_map/ppermute | solution.py:622
  30.7 1.1 %attend_queries.1 = (f32[2,256,128]{2,1,0:T(8,128)S(1)}, f32[2,256,256]{2,1,0:T(8,128)S(1)}) custom-call(s32[1]{0:T(128)S(6)} %copy.11.length_ref, bf16[2,256,512]{2,1,0:T(8,128)(2,1)S(1)} %bitcast.11, bf16[2,256,256]{2,1,0:T(8,128)(2,1)S(1)} %collective-permute-done.query_far_ref, f32[2,256,256]{2,1,0:T(8,128)S(1)} %get-tuple-element.22.sums_ref, ...), custom_call_target="tpu_custom_call" | custom-call | flops 251658240 | bytes 2097152 | tf_op jit(solution)/shard_map/attend_queries/pallas_call | solution.py:395
  31.8 0.0 copy-start.3
  31.8 0.4 collective-permute-done.1.key_far_ref
  32.2 1.4 %attend_keys.1 = (f32[2,256,128]{2,1,0:T(8,128)S(1)}, bf16[2,256,128]{2,1,0:T(8,128)(2,1)S(1)}, bf16[2,256,256]{2,1,0:T(8,128)(2,1)S(1)}) custom-call(s32[1]{0:T(128)S(6)} %copy.11.length_ref, bf16[2,256,512]{2,1,0:T(8,128)(2,1)S(1)} %bitcast.12, bf16[2,256,256]{2,1,0:T(8,128)(2,1)S(1)} %collective-permute-done.query_far_ref, ...), custom_call_target="tpu_custom_call" | custom-call | flops 335544320 | bytes 2097152 | tf_op jit(solution)/shard_map/attend_keys/pallas_call | solution.py:407
  33.7 1.9 %collective-permute-start.3 = (bf16[2,256,256]{2,1,0:T(8,128)(2,1)S(1)}, bf16[2,256,256]{2,1,0:T(8,128)(2,1)S(1)}, u32[]{:S(2)}, u32[]{:S(2)}) collective-permute-start(bf16[2,256,256]{2,1,0:T(8,128)(2,1)S(1)} %get-tuple-element.30), channel_id=1, source_target_pairs={{0,128},{1,129},{2,130},{3,131},{4,132},{5,133},{6,134},{7,135},{8... | collective-permute-start | bytes 786440 | tf_op jit(solution)/shard_map/ppermute | solution.py:631
  35.6 4.9 %collective-permute-start.2 = (bf16[2,256,128]{2,1,0:T(8,128)(2,1)S(1)}, bf16[2,256,128]{2,1,0:T(8,128)(2,1)S(1)}, u32[]{:S(2)}, u32[]{:S(2)}) collective-permute-start(bf16[2,256,128]{2,1,0:T(8,128)(2,1)S(1)} %get-tuple-element.28), channel_id=1, source_target_pairs={{0,64},{1,33},{2,66},{3,35},{4,68},{5,37},{6,70},{7,39},{8,72},{9,... | collective-permute-start | bytes 393224 | tf_op jit(solution)/shard_map/ppermute | solution.py:630
  40.5 7.0 %collective-permute-done.2.query_got_ref = bf16[2,256,128]{2,1,0:T(8,128)(2,1)S(1)} collective-permute-done((bf16[2,256,128]{2,1,0:T(8,128)(2,1)S(1)}, bf16[2,256,128]{2,1,0:T(8,128)(2,1)S(1)}, u32[]{:S(2)}, u32[]{:S(2)}) %collective-permute-start.2) | collective-permute-done | bytes 131104 | tf_op jit(solution)/shard_map/ppermute | solution.py:630
  47.4 0.0 collective-permute-done.3.key_got_ref
  47.5 0.1 join_parts.1
  47.5 9.6 %all_to_all.26.grads_ref = bf16[4,128,384]{2,1,0:T(8,128)(2,1)S(1)} all-to-all(bf16[4,128,384]{2,1,0:T(8,128)(2,1)S(1)} %bitcast.13), channel_id=1, replica_groups={{0,32,384,416},{1,65,385,449},{2,34,386,418},{3,67,387,451},{4,36,388,4..., dimensions={0} | all-to-all | bytes 786432 | tf_op jit(solution)/shard_map/all_to_all | solution.py:633
  57.2 0.0 copy-done.3
  57.2 0.9 finish.1
  58.0 8.7 %all_to_all.27.rows_ref = bf16[8,72,128]{2,1,0:T(8,128)(2,1)S(1)} all-to-all(bf16[8,72,128]{2,1,0:T(8,128)(2,1)S(1)} %get-tuple-element.34), channel_id=1, replica_groups={{0,1,128,129,256,257,384,385},{2,3,130,131,258,259,386,387},{4,5,132,13..., dimensions={0} | all-to-all | bytes 294912 | tf_op jit(solution)/shard_map/all_to_all | solution.py:637
  66.7 0.3 arrange_rows.1
  67.0 24.7 %all_to_all.28.rows_ref = bf16[16,40,128]{2,1,0:T(8,128)(2,1)S(1)} all-to-all(bf16[16,40,128]{2,1,0:T(8,128)(2,1)S(1)} %bitcast.14), channel_id=1, replica_groups={{0,2,4,6,8,10,12,14,16,18,20,22,24,26,28,30},{1,3,5,7,9,11,13,15,17,19,..., dimensions={0} | all-to-all | bytes 327680 | tf_op jit(solution)/shard_map/all_to_all | solution.py:639
  91.7 0.8 scatter_rows.1
  92.5 12.7 %all_to_all.29.pieces_ref = bf16[16,64,128]{2,1,0:T(8,128)(2,1)S(1)} all-to-all(bf16[16,64,128]{2,1,0:T(8,128)(2,1)S(1)} %bitcast.17), channel_id=1, replica_groups=mesh['ctx'=16,'table'=32] {'ctx'}, dimensions={0} | all-to-all | bytes 524288 | tf_op jit(solution)/shard_map/all_to_all | solution.py:641
  105.1 0.7 total_rows.1
  (1 shorter events, 0.0 us)
Async XLA Ops:
  1.3 24.6 %copy-start = (bf16[512,2048]{1,0:T(8,128)(2,1)S(1)}, bf16[512,2048]{1,0:T(8,128)(2,1)}, u32[]{:S(2)}) copy-start(bf16[512,2048]{1,0:T(8,128)(2,1)} %in_proj_ref.3) | copy-start | bytes 6291460
  1.3 24.6 %copy-start.1 = (bf16[1,128,512]{2,1,0:T(8,128)(2,1)S(1)}, bf16[1,128,512]{2,1,0:T(8,128)(2,1)}, u32[]{:S(2)}) copy-start(bf16[1,128,512]{2,1,0:T(8,128)(2,1)} %param.11) | copy-start | bytes 393220
  1.3 24.6 %copy-start.2 = (s32[1,128]{1,0:T(1,128)S(1)}, s32[1,128]{1,0:T(1,128)}, u32[]{:S(2)}) copy-start(s32[1,128]{1,0:T(1,128)} %item_ref.1) | copy-start | bytes 1540
  20.5 10.2 %collective-permute-start = (bf16[2,256,256]{2,1,0:T(8,128)(2,1)S(1)}, bf16[2,256,256]{2,1,0:T(8,128)(2,1)S(1)}, u32[]{:S(2)}, u32[]{:S(2)}) collective-permute-start(bf16[2,256,256]{2,1,0:T(8,128)(2,1)S(1)} %get-tuple-element.39), channel_id=1, source_target_pairs={{0,64},{1,33},{2,66},{3,35},{4,68},{5,37},{6,70},{7,39},{8,72},{9,... | collective-permute-start | bytes 786440 | tf_op jit(solution)/shard_map/ppermute | solution.py:622
  24.0 8.3 %collective-permute-start.1 = (bf16[2,256,256]{2,1,0:T(8,128)(2,1)S(1)}, bf16[2,256,256]{2,1,0:T(8,128)(2,1)S(1)}, u32[]{:S(2)}, u32[]{:S(2)}) collective-permute-start(bf16[2,256,256]{2,1,0:T(8,128)(2,1)S(1)} %get-tuple-element.38), channel_id=1, source_target_pairs={{0,128},{1,129},{2,130},{3,131},{4,132},{5,133},{6,134},{7,135},{8... | collective-permute-start | bytes 786440 | tf_op jit(solution)/shard_map/ppermute | solution.py:623
  31.8 25.4 %copy-start.3 = (s32[1,128]{1,0:T(1,128)S(1)}, s32[1,128]{1,0:T(1,128)}, u32[]{:S(2)}) copy-start(s32[1,128]{1,0:T(1,128)} %slot_ref.1) | copy-start | bytes 1540
  33.7 13.8 %collective-permute-start.3 = (bf16[2,256,256]{2,1,0:T(8,128)(2,1)S(1)}, bf16[2,256,256]{2,1,0:T(8,128)(2,1)S(1)}, u32[]{:S(2)}, u32[]{:S(2)}) collective-permute-start(bf16[2,256,256]{2,1,0:T(8,128)(2,1)S(1)} %get-tuple-element.30), channel_id=1, source_target_pairs={{0,128},{1,129},{2,130},{3,131},{4,132},{5,133},{6,134},{7,135},{8... | collective-permute-start | bytes 786440 | tf_op jit(solution)/shard_map/ppermute | solution.py:631
  35.6 11.8 %collective-permute-start.2 = (bf16[2,256,128]{2,1,0:T(8,128)(2,1)S(1)}, bf16[2,256,128]{2,1,0:T(8,128)(2,1)S(1)}, u32[]{:S(2)}, u32[]{:S(2)}) collective-permute-start(bf16[2,256,128]{2,1,0:T(8,128)(2,1)S(1)} %get-tuple-element.28), channel_id=1, source_target_pairs={{0,64},{1,33},{2,66},{3,35},{4,68},{5,37},{6,70},{7,39},{8,72},{9,... | collective-permute-start | bytes 393224 | tf_op jit(solution)/shard_map/ppermute | solution.py:630

commit v7 on v6

--- a/solution.py
+++ b/solution.py
@@ -23,6 +23,7 @@
 FAR_ROWS = FAR_SUMS + 8
 X_COUNT = 4
 Y_COUNT = 4
+HALF = TOKENS // 2
 CTX_COUNT = X_COUNT * Y_COUNT
 TILE = 2 * TOKENS
 VMEM_LIMIT = 48 * 1024 * 1024
@@ -551,7 +552,7 @@
 
 
 def scatter_kernel(rows_ref, proj_ref, out_ref, proj_out, wide_ref, sem):
-    copy = pltpu.make_async_copy(proj_ref, proj_out, sem)
+    copy = pltpu.make_async_copy(proj_ref.at[:HALF], proj_out.at[:HALF], sem)
     copy.start()
     targets = CTX_COUNT * ROWS_DEV
     wide_ref[...] = rows_ref[...].astype(F32)
@@ -585,22 +586,33 @@
     )(rows, proj)
 
 
-def total_kernel(pieces_ref, out_ref):
+def total_kernel(pieces_ref, proj_ref, _, total_out, proj_out, total_ref, sems):
+    copy = pltpu.make_async_copy(proj_ref.at[HALF:], proj_out.at[HALF:], sems.at[0])
+    copy.start()
     for x in range(X_COUNT):
-        out_ref[:, x * QUARTER : (x + 1) * QUARTER] = sum(
+        total_ref[:, x * QUARTER : (x + 1) * QUARTER] = sum(
             pieces_ref[x * Y_COUNT + y].astype(F32) for y in range(Y_COUNT)
         )
-
-
-def total_rows(pieces):
+    total_copy = pltpu.make_async_copy(total_ref, total_out, sems.at[1])
+    total_copy.start()
+    copy.wait()
+    total_copy.wait()
+
+
+def total_rows(pieces, proj, proj_out):
     return pl.pallas_call(
         total_kernel,
-        out_shape=jax.ShapeDtypeStruct((ROWS_DEV, WIDTH), F32),
-        in_specs=in_vmem(1),
-        out_specs=in_vmem(1)[0],
+        out_shape=(
+            jax.ShapeDtypeStruct((ROWS_DEV, WIDTH), F32),
+            jax.ShapeDtypeStruct((TOKENS, 4 * WIDTH), BF16),
+        ),
+        in_specs=in_vmem(2) + in_hbm(1),
+        out_specs=tuple(in_hbm(2)),
+        input_output_aliases={2: 1},
+        scratch_shapes=[pltpu.VMEM((ROWS_DEV, WIDTH), F32), pltpu.SemaphoreType.DMA((2,))],
         compiler_params=params(),
         name="total_rows",
-    )(pieces)
+    )(pieces, proj, proj_out)
 
 
 def per_device(
@@ -633,13 +645,13 @@
     grads = lax.all_to_all(
         joined.reshape(HEADS, TOKENS, 3 * HEAD_DIM), AXES, 0, 0, axis_index_groups=HEAD_GROUPS
     )
-    proj_grad, rows = finish(grads, slope, gate, base, in_proj, token_slot, codes)
+    proj, rows = finish(grads, slope, gate, base, in_proj, token_slot, codes)
     rows = lax.all_to_all(rows, AXES, 0, 0, axis_index_groups=X_CORE_GROUPS)
     rows = arrange_rows(rows).reshape(FARS, FAR_ROWS, QUARTER)
     rows = lax.all_to_all(rows, "table", 0, 0, axis_index_groups=FAR_GROUPS)
-    dense, proj_grad = scatter_rows(rows, proj_grad)
+    dense, proj_out = scatter_rows(rows, proj)
     pieces = lax.all_to_all(dense.reshape(CTX_COUNT, ROWS_DEV, QUARTER), "ctx", 0, 0)
-    table_grad = total_rows(pieces)
+    table_grad, proj_grad = total_rows(pieces, proj, proj_out)
     return (proj_grad[None], table_grad)
 
 

time: 106 us -> 106 us (level)
  no operation moved by 1% of the time
where the time goes in v7:
time: 106 us
  blocking collectives  71.9 us (68%)
  starting transfers between devices  12.2 us (12%)
  waiting for transfers between devices  10.4 us (10%)
  Pallas kernels  9.81 us (9%)
  between operations  1.42 us (1%)
    all_to_all x1, blocking collectives, per_device(): rows = lax.all_to_all(rows, 'table', 0, 0, axis_index_groups=FAR_GROUPS)  24.7 us
    all_to_all x1, blocking collectives, per_device(): own = lax.all_to_all(parts, AXES, 0, 0, axis_index_groups=HEAD_GROUPS)  16.3 us
    all_to_all x1, blocking collectives, per_device(): lax.all_to_all(dense.reshape(CTX_COUNT, ROWS_DEV, QUARTER), 'ctx', 0, 0)  12.7 us
    all_to_all x1, blocking collectives, per_device(): lax.all_to_all(joined.reshape(HEADS, TOKENS, 3 * HEAD_DIM), AXES, 0, 0, a...  9.62 us
    all_to_all x1, blocking collectives, per_device(): rows = lax.all_to_all(rows, AXES, 0, 0, axis_index_groups=X_CORE_GROUPS)  8.7 us
    ppermute x1, waiting for transfers between devices, per_device(): query_got = lax.ppermute(query_send, AXES, SWAP_QUERY)  6.98 us
    ppermute x1, starting transfers between devices, per_device(): query_got = lax.ppermute(query_send, AXES, SWAP_QUERY)  4.86 us
    ppermute x1, starting transfers between devices, per_device(): query_far = lax.ppermute(own[:, :, :2 * HEAD_DIM], AXES, SWAP_QUERY)  3.49 us
  transfers between devices with their start and end apart: 4, of which 3 were waited for; matrix products, arithmetic and copies ran while one was open for 0% of the time, Pallas kernels for 3%

profile of v7, /device:TPU:8, one launch (start us, length us, event | category | flops | bytes accessed | tf_op | source)
XLA Modules:
  0.0 105.8 jit_solution(1739394444662621842)
XLA Ops:
  1.3 0.0 copy-start
  1.3 0.0 copy-start.1
  1.3 0.0 copy-start.2
  1.3 2.8 %project.1 = (bf16[4,128,512]{2,1,0:T(8,128)(2,1)S(1)}, f32[128,2048]{1,0:T(8,128)S(1)}, f32[128,512]{1,0:T(8,128)S(1)}) custom-call(s32[1]{0:T(128)S(6)} %copy.13.length_ref, bf16[128,512]{1,0:T(8,128)(2,1)} %bitcast.19, bf16[128,512]{1,0:T(8,128)(2,1)} %bitcast.20, bf16[128,512]{1,0:T(8,128)(2,1)} %bitcast.15, bf16[512,2048]{1,0:T(8,128)(2,1)} %in_proj_ref.3, ...), custom_call_target="tpu_custom_call" | custom-call | tf_op jit(solution)/shard_map/project/pallas_call | solution.py:178
  4.2 16.3 %all_to_all.25 = bf16[4,128,512]{2,1,0:T(8,128)(2,1)S(1)} all-to-all(bf16[4,128,512]{2,1,0:T(8,128)(2,1)S(1)} %get-tuple-element.22), channel_id=1, replica_groups={{0,32,384,416},{1,65,385,449},{2,34,386,418},{3,67,387,451},{4,36,388,4..., dimensions={0} | all-to-all | bytes 1048576 | tf_op jit(solution)/shard_map/all_to_all | solution.py:632
  20.5 3.5 %collective-permute-start = (bf16[2,256,256]{2,1,0:T(8,128)(2,1)S(1)}, bf16[2,256,256]{2,1,0:T(8,128)(2,1)S(1)}, u32[]{:S(2)}, u32[]{:S(2)}) collective-permute-start(bf16[2,256,256]{2,1,0:T(8,128)(2,1)S(1)} %get-tuple-element.43), channel_id=1, source_target_pairs={{0,64},{1,33},{2,66},{3,35},{4,68},{5,37},{6,70},{7,39},{8,72},{9,... | collective-permute-start | bytes 786440 | tf_op jit(solution)/shard_map/ppermute | solution.py:634
  24.0 1.9 %collective-permute-start.1 = (bf16[2,256,256]{2,1,0:T(8,128)(2,1)S(1)}, bf16[2,256,256]{2,1,0:T(8,128)(2,1)S(1)}, u32[]{:S(2)}, u32[]{:S(2)}) collective-permute-start(bf16[2,256,256]{2,1,0:T(8,128)(2,1)S(1)} %get-tuple-element.42), channel_id=1, source_target_pairs={{0,128},{1,129},{2,130},{3,131},{4,132},{5,133},{6,134},{7,135},{8... | collective-permute-start | bytes 786440 | tf_op jit(solution)/shard_map/ppermute | solution.py:635
  25.9 0.0 copy-done
  25.9 0.0 copy-done.1
  25.9 0.0 copy-done.2
  25.9 0.6 local_terms.1
  26.5 1.1 %attend_own.1 = (f32[2,256,128]{2,1,0:T(8,128)S(1)}, f32[2,256,256]{2,1,0:T(8,128)S(1)}) custom-call(s32[1]{0:T(128)S(6)} %copy.13.length_ref, bf16[2,256,512]{2,1,0:T(8,128)(2,1)S(1)} %bitcast.10), custom_call_target="tpu_custom_call" | custom-call | flops 251658240 | bytes 2097152 | tf_op jit(solution)/shard_map/attend_own/pallas_call | solution.py:384
  27.7 3.0 %collective-permute-done.query_far_ref = bf16[2,256,256]{2,1,0:T(8,128)(2,1)S(1)} collective-permute-done((bf16[2,256,256]{2,1,0:T(8,128)(2,1)S(1)}, bf16[2,256,256]{2,1,0:T(8,128)(2,1)S(1)}, u32[]{:S(2)}, u32[]{:S(2)}) %collective-permute-start) | collective-permute-done | bytes 262176 | tf_op jit(solution)/shard_map/ppermute | solution.py:634
  30.7 1.1 %attend_queries.1 = (f32[2,256,128]{2,1,0:T(8,128)S(1)}, f32[2,256,256]{2,1,0:T(8,128)S(1)}) custom-call(s32[1]{0:T(128)S(6)} %copy.13.length_ref, bf16[2,256,512]{2,1,0:T(8,128)(2,1)S(1)} %bitcast.11, bf16[2,256,256]{2,1,0:T(8,128)(2,1)S(1)} %collective-permute-done.query_far_ref, f32[2,256,256]{2,1,0:T(8,128)S(1)} %get-tuple-element.24.sums_ref, ...), custom_call_target="tpu_custom_call" | custom-call | flops 251658240 | bytes 2097152 | tf_op jit(solution)/shard_map/attend_queries/pallas_call | solution.py:396
  31.8 0.0 copy-start.3
  31.8 0.4 collective-permute-done.1.key_far_ref
  32.2 1.4 %attend_keys.1 = (f32[2,256,128]{2,1,0:T(8,128)S(1)}, bf16[2,256,128]{2,1,0:T(8,128)(2,1)S(1)}, bf16[2,256,256]{2,1,0:T(8,128)(2,1)S(1)}) custom-call(s32[1]{0:T(128)S(6)} %copy.13.length_ref, bf16[2,256,512]{2,1,0:T(8,128)(2,1)S(1)} %bitcast.12, bf16[2,256,256]{2,1,0:T(8,128)(2,1)S(1)} %collective-permute-done.query_far_ref, ...), custom_call_target="tpu_custom_call" | custom-call | flops 335544320 | bytes 2097152 | tf_op jit(solution)/shard_map/attend_keys/pallas_call | solution.py:408
  33.7 1.9 %collective-permute-start.3 = (bf16[2,256,256]{2,1,0:T(8,128)(2,1)S(1)}, bf16[2,256,256]{2,1,0:T(8,128)(2,1)S(1)}, u32[]{:S(2)}, u32[]{:S(2)}) collective-permute-start(bf16[2,256,256]{2,1,0:T(8,128)(2,1)S(1)} %get-tuple-element.32), channel_id=1, source_target_pairs={{0,128},{1,129},{2,130},{3,131},{4,132},{5,133},{6,134},{7,135},{8... | collective-permute-start | bytes 786440 | tf_op jit(solution)/shard_map/ppermute | solution.py:643
  35.6 4.9 %collective-permute-start.2 = (bf16[2,256,128]{2,1,0:T(8,128)(2,1)S(1)}, bf16[2,256,128]{2,1,0:T(8,128)(2,1)S(1)}, u32[]{:S(2)}, u32[]{:S(2)}) collective-permute-start(bf16[2,256,128]{2,1,0:T(8,128)(2,1)S(1)} %get-tuple-element.30), channel_id=1, source_target_pairs={{0,64},{1,33},{2,66},{3,35},{4,68},{5,37},{6,70},{7,39},{8,72},{9,... | collective-permute-start | bytes 393224 | tf_op jit(solution)/shard_map/ppermute | solution.py:642
  40.5 7.0 %collective-permute-done.2.query_got_ref = bf16[2,256,128]{2,1,0:T(8,128)(2,1)S(1)} collective-permute-done((bf16[2,256,128]{2,1,0:T(8,128)(2,1)S(1)}, bf16[2,256,128]{2,1,0:T(8,128)(2,1)S(1)}, u32[]{:S(2)}, u32[]{:S(2)}) %collective-permute-start.2) | collective-permute-done | bytes 131104 | tf_op jit(solution)/shard_map/ppermute | solution.py:642
  47.4 0.0 collective-permute-done.3.key_got_ref
  47.5 0.1 join_parts.1
  47.5 9.6 %all_to_all.26.grads_ref = bf16[4,128,384]{2,1,0:T(8,128)(2,1)S(1)} all-to-all(bf16[4,128,384]{2,1,0:T(8,128)(2,1)S(1)} %bitcast.13), channel_id=1, replica_groups={{0,32,384,416},{1,65,385,449},{2,34,386,418},{3,67,387,451},{4,36,388,4..., dimensions={0} | all-to-all | bytes 786432 | tf_op jit(solution)/shard_map/all_to_all | solution.py:645
  57.2 0.0 copy-done.3
  57.2 0.9 finish.1
  58.0 8.7 %all_to_all.27.rows_ref = bf16[8,72,128]{2,1,0:T(8,128)(2,1)S(1)} all-to-all(bf16[8,72,128]{2,1,0:T(8,128)(2,1)S(1)} %get-tuple-element.36), channel_id=1, replica_groups={{0,1,128,129,256,257,384,385},{2,3,130,131,258,259,386,387},{4,5,132,13..., dimensions={0} | all-to-all | bytes 294912 | tf_op jit(solution)/shard_map/all_to_all | solution.py:649
  66.7 0.3 arrange_rows.1
  67.0 24.7 %all_to_all.28.rows_ref = bf16[16,40,128]{2,1,0:T(8,128)(2,1)S(1)} all-to-all(bf16[16,40,128]{2,1,0:T(8,128)(2,1)S(1)} %bitcast.14), channel_id=1, replica_groups={{0,2,4,6,8,10,12,14,16,18,20,22,24,26,28,30},{1,3,5,7,9,11,13,15,17,19,..., dimensions={0} | all-to-all | bytes 327680 | tf_op jit(solution)/shard_map/all_to_all | solution.py:651
  91.7 0.7 scatter_rows.1
  92.4 12.7 %all_to_all.29.pieces_ref = bf16[16,64,128]{2,1,0:T(8,128)(2,1)S(1)} all-to-all(bf16[16,64,128]{2,1,0:T(8,128)(2,1)S(1)} %bitcast.17), channel_id=1, replica_groups=mesh['ctx'=16,'table'=32] {'ctx'}, dimensions={0} | all-to-all | bytes 524288 | tf_op jit(solution)/shard_map/all_to_all | solution.py:653
  105.1 0.8 total_rows.1
  (1 shorter events, 0.0 us)
Async XLA Ops:
  1.3 24.6 %copy-start = (bf16[512,2048]{1,0:T(8,128)(2,1)S(1)}, bf16[512,2048]{1,0:T(8,128)(2,1)}, u32[]{:S(2)}) copy-start(bf16[512,2048]{1,0:T(8,128)(2,1)} %in_proj_ref.3) | copy-start | bytes 6291460
  1.3 24.6 %copy-start.1 = (bf16[1,128,512]{2,1,0:T(8,128)(2,1)S(1)}, bf16[1,128,512]{2,1,0:T(8,128)(2,1)}, u32[]{:S(2)}) copy-start(bf16[1,128,512]{2,1,0:T(8,128)(2,1)} %param.11) | copy-start | bytes 393220
  1.3 24.6 %copy-start.2 = (s32[1,128]{1,0:T(1,128)S(1)}, s32[1,128]{1,0:T(1,128)}, u32[]{:S(2)}) copy-start(s32[1,128]{1,0:T(1,128)} %item_ref.1) | copy-start | bytes 1540
  20.5 10.2 %collective-permute-start = (bf16[2,256,256]{2,1,0:T(8,128)(2,1)S(1)}, bf16[2,256,256]{2,1,0:T(8,128)(2,1)S(1)}, u32[]{:S(2)}, u32[]{:S(2)}) collective-permute-start(bf16[2,256,256]{2,1,0:T(8,128)(2,1)S(1)} %get-tuple-element.43), channel_id=1, source_target_pairs={{0,64},{1,33},{2,66},{3,35},{4,68},{5,37},{6,70},{7,39},{8,72},{9,... | collective-permute-start | bytes 786440 | tf_op jit(solution)/shard_map/ppermute | solution.py:634
  24.0 8.3 %collective-permute-start.1 = (bf16[2,256,256]{2,1,0:T(8,128)(2,1)S(1)}, bf16[2,256,256]{2,1,0:T(8,128)(2,1)S(1)}, u32[]{:S(2)}, u32[]{:S(2)}) collective-permute-start(bf16[2,256,256]{2,1,0:T(8,128)(2,1)S(1)} %get-tuple-element.42), channel_id=1, source_target_pairs={{0,128},{1,129},{2,130},{3,131},{4,132},{5,133},{6,134},{7,135},{8... | collective-permute-start | bytes 786440 | tf_op jit(solution)/shard_map/ppermute | solution.py:635
  31.8 25.4 %copy-start.3 = (s32[1,128]{1,0:T(1,128)S(1)}, s32[1,128]{1,0:T(1,128)}, u32[]{:S(2)}) copy-start(s32[1,128]{1,0:T(1,128)} %slot_ref.1) | copy-start | bytes 1540
  33.7 13.8 %collective-permute-start.3 = (bf16[2,256,256]{2,1,0:T(8,128)(2,1)S(1)}, bf16[2,256,256]{2,1,0:T(8,128)(2,1)S(1)}, u32[]{:S(2)}, u32[]{:S(2)}) collective-permute-start(bf16[2,256,256]{2,1,0:T(8,128)(2,1)S(1)} %get-tuple-element.32), channel_id=1, source_target_pairs={{0,128},{1,129},{2,130},{3,131},{4,132},{5,133},{6,134},{7,135},{8... | collective-permute-start | bytes 786440 | tf_op jit(solution)/shard_map/ppermute | solution.py:643
  35.6 11.8 %collective-permute-start.2 = (bf16[2,256,128]{2,1,0:T(8,128)(2,1)S(1)}, bf16[2,256,128]{2,1,0:T(8,128)(2,1)S(1)}, u32[]{:S(2)}, u32[]{:S(2)}) collective-permute-start(bf16[2,256,128]{2,1,0:T(8,128)(2,1)S(1)} %get-tuple-element.30), channel_id=1, source_target_pairs={{0,64},{1,33},{2,66},{3,35},{4,68},{5,37},{6,70},{7,39},{8,72},{9,... | collective-permute-start | bytes 393224 | tf_op jit(solution)/shard_map/ppermute | solution.py:642

commit v8 on v7

--- a/solution.py
+++ b/solution.py
@@ -94,6 +94,11 @@
     return pltpu.CompilerParams(vmem_limit_bytes=limit)
 
 
+def silu(value):
+    half = 0.5 * value
+    return half + half * jnp.tanh(half)
+
+
 def project_kernel(
     length_ref,
     inputs_hbm,
@@ -151,7 +156,7 @@
     inputs = inputs_ref[...]
     pre = dot(inputs, in_proj_ref[0], MATMUL)
     pre_ref[:, :WIDTH] = pre
-    gating = (pre * jax.nn.sigmoid(pre)).astype(BF16).astype(F32)
+    gating = silu(pre).astype(BF16).astype(F32)
     gain_grad_ref[...] = back * (normed * gain)
     carried = back * gating * gain
     out_attn = inv_std * (
@@ -168,7 +173,7 @@
         in_copies[block].wait()
         pre = dot(inputs, in_proj_ref[block], MATMUL)
         pre_ref[:, block * WIDTH : (block + 1) * WIDTH] = pre
-        hidden = (pre * jax.nn.sigmoid(pre)).astype(BF16)
+        hidden = silu(pre).astype(BF16)
         for head in range(HEADS):
             cols = slice(head * HEAD_DIM, (head + 1) * HEAD_DIM)
             parts_ref[head, :, place * HEAD_DIM : (place + 1) * HEAD_DIM] = hidden[:, cols]

time: 106 us -> 106 us (level)
  no operation moved by 1% of the time
where the time goes in v8:
time: 106 us
  blocking collectives  71.9 us (68%)
  starting transfers between devices  12.2 us (12%)
  waiting for transfers between devices  10.4 us (10%)
  Pallas kernels  9.88 us (9%)
  between operations  1.42 us (1%)
    all_to_all x1, blocking collectives, per_device(): rows = lax.all_to_all(rows, 'table', 0, 0, axis_index_groups=FAR_GROUPS)  24.7 us
    all_to_all x1, blocking collectives, per_device(): own = lax.all_to_all(parts, AXES, 0, 0, axis_index_groups=HEAD_GROUPS)  16.3 us
    all_to_all x1, blocking collectives, per_device(): lax.all_to_all(dense.reshape(CTX_COUNT, ROWS_DEV, QUARTER), 'ctx', 0, 0)  12.6 us
    all_to_all x1, blocking collectives, per_device(): lax.all_to_all(joined.reshape(HEADS, TOKENS, 3 * HEAD_DIM), AXES, 0, 0, a...  9.62 us
    all_to_all x1, blocking collectives, per_device(): rows = lax.all_to_all(rows, AXES, 0, 0, axis_index_groups=X_CORE_GROUPS)  8.7 us
    ppermute x1, waiting for transfers between devices, per_device(): query_got = lax.ppermute(query_send, AXES, SWAP_QUERY)  6.98 us
    ppermute x1, starting transfers between devices, per_device(): query_got = lax.ppermute(query_send, AXES, SWAP_QUERY)  4.86 us
    ppermute x1, starting transfers between devices, per_device(): query_far = lax.ppermute(own[:, :, :2 * HEAD_DIM], AXES, SWAP_QUERY)  3.5 us
  transfers between devices with their start and end apart: 4, of which 3 were waited for; matrix products, arithmetic and copies ran while one was open for 0% of the time, Pallas kernels for 3%

profile of v8, /device:TPU:8, one launch (start us, length us, event | category | flops | bytes accessed | tf_op | source)
XLA Modules:
  0.0 105.9 jit_solution(1570771947729387152)
XLA Ops:
  1.3 0.0 copy-start
  1.3 0.0 copy-start.1
  1.3 0.0 copy-start.2
  1.3 2.9 %project.1 = (bf16[4,128,512]{2,1,0:T(8,128)(2,1)S(1)}, f32[128,2048]{1,0:T(8,128)S(1)}, f32[128,512]{1,0:T(8,128)S(1)}) custom-call(s32[1]{0:T(128)S(6)} %copy.13.length_ref, bf16[128,512]{1,0:T(8,128)(2,1)} %bitcast.19, bf16[128,512]{1,0:T(8,128)(2,1)} %bitcast.20, bf16[128,512]{1,0:T(8,128)(2,1)} %bitcast.15, bf16[512,2048]{1,0:T(8,128)(2,1)} %in_proj_ref.3, ...), custom_call_target="tpu_custom_call" | custom-call | tf_op jit(solution)/shard_map/project/pallas_call | solution.py:183
  4.2 16.3 %all_to_all.25 = bf16[4,128,512]{2,1,0:T(8,128)(2,1)S(1)} all-to-all(bf16[4,128,512]{2,1,0:T(8,128)(2,1)S(1)} %get-tuple-element.22), channel_id=1, replica_groups={{0,32,384,416},{1,65,385,449},{2,34,386,418},{3,67,387,451},{4,36,388,4..., dimensions={0} | all-to-all | bytes 1048576 | tf_op jit(solution)/shard_map/all_to_all | solution.py:637
  20.5 3.5 %collective-permute-start = (bf16[2,256,256]{2,1,0:T(8,128)(2,1)S(1)}, bf16[2,256,256]{2,1,0:T(8,128)(2,1)S(1)}, u32[]{:S(2)}, u32[]{:S(2)}) collective-permute-start(bf16[2,256,256]{2,1,0:T(8,128)(2,1)S(1)} %get-tuple-element.43), channel_id=1, source_target_pairs={{0,64},{1,33},{2,66},{3,35},{4,68},{5,37},{6,70},{7,39},{8,72},{9,... | collective-permute-start | bytes 786440 | tf_op jit(solution)/shard_map/ppermute | solution.py:639
  24.0 1.9 %collective-permute-start.1 = (bf16[2,256,256]{2,1,0:T(8,128)(2,1)S(1)}, bf16[2,256,256]{2,1,0:T(8,128)(2,1)S(1)}, u32[]{:S(2)}, u32[]{:S(2)}) collective-permute-start(bf16[2,256,256]{2,1,0:T(8,128)(2,1)S(1)} %get-tuple-element.42), channel_id=1, source_target_pairs={{0,128},{1,129},{2,130},{3,131},{4,132},{5,133},{6,134},{7,135},{8... | collective-permute-start | bytes 786440 | tf_op jit(solution)/shard_map/ppermute | solution.py:640
  26.0 0.0 copy-done
  26.0 0.0 copy-done.1
  26.0 0.0 copy-done.2
  26.0 0.6 local_terms.1
  26.6 1.1 %attend_own.1 = (f32[2,256,128]{2,1,0:T(8,128)S(1)}, f32[2,256,256]{2,1,0:T(8,128)S(1)}) custom-call(s32[1]{0:T(128)S(6)} %copy.13.length_ref, bf16[2,256,512]{2,1,0:T(8,128)(2,1)S(1)} %bitcast.10), custom_call_target="tpu_custom_call" | custom-call | flops 251658240 | bytes 2097152 | tf_op jit(solution)/shard_map/attend_own/pallas_call | solution.py:389
  27.7 3.0 %collective-permute-done.query_far_ref = bf16[2,256,256]{2,1,0:T(8,128)(2,1)S(1)} collective-permute-done((bf16[2,256,256]{2,1,0:T(8,128)(2,1)S(1)}, bf16[2,256,256]{2,1,0:T(8,128)(2,1)S(1)}, u32[]{:S(2)}, u32[]{:S(2)}) %collective-permute-start) | collective-permute-done | bytes 262176 | tf_op jit(solution)/shard_map/ppermute | solution.py:639
  30.7 1.1 %attend_queries.1 = (f32[2,256,128]{2,1,0:T(8,128)S(1)}, f32[2,256,256]{2,1,0:T(8,128)S(1)}) custom-call(s32[1]{0:T(128)S(6)} %copy.13.length_ref, bf16[2,256,512]{2,1,0:T(8,128)(2,1)S(1)} %bitcast.11, bf16[2,256,256]{2,1,0:T(8,128)(2,1)S(1)} %collective-permute-done.query_far_ref, f32[2,256,256]{2,1,0:T(8,128)S(1)} %get-tuple-element.24.sums_ref, ...), custom_call_target="tpu_custom_call" | custom-call | flops 251658240 | bytes 2097152 | tf_op jit(solution)/shard_map/attend_queries/pallas_call | solution.py:401
  31.9 0.0 copy-start.3
  31.9 0.4 collective-permute-done.1.key_far_ref
  32.3 1.4 %attend_keys.1 = (f32[2,256,128]{2,1,0:T(8,128)S(1)}, bf16[2,256,128]{2,1,0:T(8,128)(2,1)S(1)}, bf16[2,256,256]{2,1,0:T(8,128)(2,1)S(1)}) custom-call(s32[1]{0:T(128)S(6)} %copy.13.length_ref, bf16[2,256,512]{2,1,0:T(8,128)(2,1)S(1)} %bitcast.12, bf16[2,256,256]{2,1,0:T(8,128)(2,1)S(1)} %collective-permute-done.query_far_ref, ...), custom_call_target="tpu_custom_call" | custom-call | flops 335544320 | bytes 2097152 | tf_op jit(solution)/shard_map/attend_keys/pallas_call | solution.py:413
  33.7 1.9 %collective-permute-start.3 = (bf16[2,256,256]{2,1,0:T(8,128)(2,1)S(1)}, bf16[2,256,256]{2,1,0:T(8,128)(2,1)S(1)}, u32[]{:S(2)}, u32[]{:S(2)}) collective-permute-start(bf16[2,256,256]{2,1,0:T(8,128)(2,1)S(1)} %get-tuple-element.32), channel_id=1, source_target_pairs={{0,128},{1,129},{2,130},{3,131},{4,132},{5,133},{6,134},{7,135},{8... | collective-permute-start | bytes 786440 | tf_op jit(solution)/shard_map/ppermute | solution.py:648
  35.7 4.9 %collective-permute-start.2 = (bf16[2,256,128]{2,1,0:T(8,128)(2,1)S(1)}, bf16[2,256,128]{2,1,0:T(8,128)(2,1)S(1)}, u32[]{:S(2)}, u32[]{:S(2)}) collective-permute-start(bf16[2,256,128]{2,1,0:T(8,128)(2,1)S(1)} %get-tuple-element.30), channel_id=1, source_target_pairs={{0,64},{1,33},{2,66},{3,35},{4,68},{5,37},{6,70},{7,39},{8,72},{9,... | collective-permute-start | bytes 393224 | tf_op jit(solution)/shard_map/ppermute | solution.py:647
  40.5 7.0 %collective-permute-done.2.query_got_ref = bf16[2,256,128]{2,1,0:T(8,128)(2,1)S(1)} collective-permute-done((bf16[2,256,128]{2,1,0:T(8,128)(2,1)S(1)}, bf16[2,256,128]{2,1,0:T(8,128)(2,1)S(1)}, u32[]{:S(2)}, u32[]{:S(2)}) %collective-permute-start.2) | collective-permute-done | bytes 131104 | tf_op jit(solution)/shard_map/ppermute | solution.py:647
  47.5 0.0 collective-permute-done.3.key_got_ref
  47.5 0.1 join_parts.1
  47.6 9.6 %all_to_all.26.grads_ref = bf16[4,128,384]{2,1,0:T(8,128)(2,1)S(1)} all-to-all(bf16[4,128,384]{2,1,0:T(8,128)(2,1)S(1)} %bitcast.13), channel_id=1, replica_groups={{0,32,384,416},{1,65,385,449},{2,34,386,418},{3,67,387,451},{4,36,388,4..., dimensions={0} | all-to-all | bytes 786432 | tf_op jit(solution)/shard_map/all_to_all | solution.py:650
  57.2 0.0 copy-done.3
  57.2 0.9 finish.1
  58.1 8.7 %all_to_all.27.rows_ref = bf16[8,72,128]{2,1,0:T(8,128)(2,1)S(1)} all-to-all(bf16[8,72,128]{2,1,0:T(8,128)(2,1)S(1)} %get-tuple-element.36), channel_id=1, replica_groups={{0,1,128,129,256,257,384,385},{2,3,130,131,258,259,386,387},{4,5,132,13..., dimensions={0} | all-to-all | bytes 294912 | tf_op jit(solution)/shard_map/all_to_all | solution.py:654
  66.8 0.3 arrange_rows.1
  67.0 24.7 %all_to_all.28.rows_ref = bf16[16,40,128]{2,1,0:T(8,128)(2,1)S(1)} all-to-all(bf16[16,40,128]{2,1,0:T(8,128)(2,1)S(1)} %bitcast.14), channel_id=1, replica_groups={{0,2,4,6,8,10,12,14,16,18,20,22,24,26,28,30},{1,3,5,7,9,11,13,15,17,19,..., dimensions={0} | all-to-all | bytes 327680 | tf_op jit(solution)/shard_map/all_to_all | solution.py:656
  91.7 0.7 scatter_rows.1
  92.4 12.6 %all_to_all.29.pieces_ref = bf16[16,64,128]{2,1,0:T(8,128)(2,1)S(1)} all-to-all(bf16[16,64,128]{2,1,0:T(8,128)(2,1)S(1)} %bitcast.17), channel_id=1, replica_groups=mesh['ctx'=16,'table'=32] {'ctx'}, dimensions={0} | all-to-all | bytes 524288 | tf_op jit(solution)/shard_map/all_to_all | solution.py:658
  105.1 0.8 total_rows.1
  (1 shorter events, 0.0 us)
Async XLA Ops:
  1.3 24.7 %copy-start = (bf16[512,2048]{1,0:T(8,128)(2,1)S(1)}, bf16[512,2048]{1,0:T(8,128)(2,1)}, u32[]{:S(2)}) copy-start(bf16[512,2048]{1,0:T(8,128)(2,1)} %in_proj_ref.3) | copy-start | bytes 6291460
  1.3 24.7 %copy-start.1 = (bf16[1,128,512]{2,1,0:T(8,128)(2,1)S(1)}, bf16[1,128,512]{2,1,0:T(8,128)(2,1)}, u32[]{:S(2)}) copy-start(bf16[1,128,512]{2,1,0:T(8,128)(2,1)} %param.11) | copy-start | bytes 393220
  1.3 24.7 %copy-start.2 = (s32[1,128]{1,0:T(1,128)S(1)}, s32[1,128]{1,0:T(1,128)}, u32[]{:S(2)}) copy-start(s32[1,128]{1,0:T(1,128)} %item_ref.1) | copy-start | bytes 1540
  20.5 10.2 %collective-permute-start = (bf16[2,256,256]{2,1,0:T(8,128)(2,1)S(1)}, bf16[2,256,256]{2,1,0:T(8,128)(2,1)S(1)}, u32[]{:S(2)}, u32[]{:S(2)}) collective-permute-start(bf16[2,256,256]{2,1,0:T(8,128)(2,1)S(1)} %get-tuple-element.43), channel_id=1, source_target_pairs={{0,64},{1,33},{2,66},{3,35},{4,68},{5,37},{6,70},{7,39},{8,72},{9,... | collective-permute-start | bytes 786440 | tf_op jit(solution)/shard_map/ppermute | solution.py:639
  24.0 8.3 %collective-permute-start.1 = (bf16[2,256,256]{2,1,0:T(8,128)(2,1)S(1)}, bf16[2,256,256]{2,1,0:T(8,128)(2,1)S(1)}, u32[]{:S(2)}, u32[]{:S(2)}) collective-permute-start(bf16[2,256,256]{2,1,0:T(8,128)(2,1)S(1)} %get-tuple-element.42), channel_id=1, source_target_pairs={{0,128},{1,129},{2,130},{3,131},{4,132},{5,133},{6,134},{7,135},{8... | collective-permute-start | bytes 786440 | tf_op jit(solution)/shard_map/ppermute | solution.py:640
  31.9 25.4 %copy-start.3 = (s32[1,128]{1,0:T(1,128)S(1)}, s32[1,128]{1,0:T(1,128)}, u32[]{:S(2)}) copy-start(s32[1,128]{1,0:T(1,128)} %slot_ref.1) | copy-start | bytes 1540
  33.7 13.8 %collective-permute-start.3 = (bf16[2,256,256]{2,1,0:T(8,128)(2,1)S(1)}, bf16[2,256,256]{2,1,0:T(8,128)(2,1)S(1)}, u32[]{:S(2)}, u32[]{:S(2)}) collective-permute-start(bf16[2,256,256]{2,1,0:T(8,128)(2,1)S(1)} %get-tuple-element.32), channel_id=1, source_target_pairs={{0,128},{1,129},{2,130},{3,131},{4,132},{5,133},{6,134},{7,135},{8... | collective-permute-start | bytes 786440 | tf_op jit(solution)/shard_map/ppermute | solution.py:648
  35.7 11.8 %collective-permute-start.2 = (bf16[2,256,128]{2,1,0:T(8,128)(2,1)S(1)}, bf16[2,256,128]{2,1,0:T(8,128)(2,1)S(1)}, u32[]{:S(2)}, u32[]{:S(2)}) collective-permute-start(bf16[2,256,128]{2,1,0:T(8,128)(2,1)S(1)} %get-tuple-element.30), channel_id=1, source_target_pairs={{0,64},{1,33},{2,66},{3,35},{4,68},{5,37},{6,70},{7,39},{8,72},{9,... | collective-permute-start | bytes 393224 | tf_op jit(solution)/shard_map/ppermute | solution.py:647
